TPU v7x, 32 devices: a whole 2x2x4 slice. The times are simulated.
32 devices in a mesh: segment: 4 (over y, x), dp: 8 (over z, core).
Axes of the slice: x: 2, y: 2, z: 4, core: 2. Of those that a mesh axis runs over, the one named last changes fastest.
Arguments:
- block_input: bfloat16 [16, 1024, 768], P('dp')
- cotangent: bfloat16 [16, 1024, 768], P('dp'), may hold values from -6 to 6
- lengths: int32 [16], P('dp'), may hold values from 128 to 1024, as said below
- steps: int32 [16], P('dp'), may hold values from 0 to 1023
- mod_weight: bfloat16 [4, 768, 2304], P('segment'), may hold values from -0.21875 to 0.21875
- mod_bias: bfloat16 [4, 2304], P('segment'), may hold values from -3 to 3
- first_weight: bfloat16 [4, 768, 3072], P('segment')
- down_rows: bfloat16 [4, 1536, 768], P('segment'), may hold values from -0.109375 to 0.109375
Outputs:
- block_output: bfloat16 [16, 1024, 768], P('dp', 'segment')
- input_grad: float32 [16, 1024, 768], P('dp', 'segment')
- mod_weight_grad: float32 [4, 768, 2304], P('segment', 'dp')
- mod_bias_grad: float32 [4, 2304], P('segment', 'dp')
- first_weight_grad: float32 [4, 768, 3072], P('segment', 'dp')
- down_rows_grad: float32 [4, 1536, 768], P('segment', 'dp')
Inputs may be any that keep to these rules, and one draw needn't show every extreme that they name: In each aligned group of 2 sequences (those of one index of dp) one, drawn from the seed, has exactly 1024 tokens; the others lean to short lengths.
All inputs are finite; a program needn't handle non-finite values.
Results may differ from a plain program's by a relative error of at most 0.028.
Values may be sent and summed in bfloat16 or wider, within the bound.
A program may use at most 320 MiB of HBM per device.

v0:
```python
import math

import jax
import jax.numpy as jnp
from jax import lax
from jax.sharding import PartitionSpec as P

D = 768
HEADS = 12
HEAD_DIM = 64
FF = 3072
SEQ_LEN = 1024


def shifted(value, axis, by):
    size = lax.axis_size(axis)
    pairs = [(i, i + by) for i in range(size) if 0 <= i + by < size]
    return lax.ppermute(value, axis, pairs)


def time_cond(steps):
    half_width = D // 2
    frequency = jnp.exp(
        jnp.arange(half_width, dtype=jnp.float32) * (-math.log(10000.0) / half_width)
    )
    angles = steps.astype(jnp.float32)[:, None] * frequency[None, :]
    return jax.nn.silu(jnp.concatenate([jnp.cos(angles), jnp.sin(angles)], axis=1))


def rope_tables():
    pair_count = HEAD_DIM // 2
    inverse = jnp.exp(jnp.arange(pair_count, dtype=jnp.float32) * (-math.log(10000.0) / pair_count))
    angles = jnp.arange(SEQ_LEN, dtype=jnp.float32)[:, None] * inverse[None, :]
    return (jnp.cos(angles)[:, None, :], jnp.sin(angles)[:, None, :])


def rotate(values, cosine, sine_table):
    first_half = values[..., : HEAD_DIM // 2]
    second_half = values[..., HEAD_DIM // 2 :]
    return jnp.concatenate(
        [
            first_half * cosine - second_half * sine_table,
            second_half * cosine + first_half * sine_table,
        ],
        axis=-1,
    )


def layer_norm(stream):
    center = stream - jnp.mean(stream, axis=-1, keepdims=True)
    return center * lax.rsqrt(jnp.mean(center * center, axis=-1, keepdims=True) + 1e-06)


def modulate(stream, offset, scaling):
    return layer_norm(stream) * (1.0 + scaling) + offset


def gelu_tanh(inputs):
    return jax.nn.gelu(inputs, approximate=True)


def rounded(values):
    return lax.optimization_barrier(values.astype(jnp.bfloat16)).astype(jnp.float32)


def split_heads(values):
    return values.reshape(SEQ_LEN, HEADS, HEAD_DIM)


def norm_parts(stream, modrow):
    offset, scaling, gating = (modrow[:D], modrow[D : 2 * D], modrow[2 * D :])
    normed_wide, modulate_back = jax.vjp(modulate, stream.astype(jnp.float32), offset, scaling)
    return (normed_wide.astype(jnp.bfloat16), modulate_back, gating)


def attention_inputs(normed, weights):
    project = jnp.dot(normed, weights[:, : 3 * D], preferred_element_type=jnp.float32)
    cosine, sine_table = rope_tables()
    queries = (rotate(split_heads(project[:, :D]), cosine, sine_table) * 0.125).astype(jnp.bfloat16)
    keys_rot = rotate(split_heads(project[:, D : 2 * D]), cosine, sine_table).astype(jnp.bfloat16)
    values = split_heads(project[:, 2 * D :]).astype(jnp.bfloat16)
    return (queries, keys_rot, values)


def attend_forward(queries, keys_rot, values, length):
    block_rows = min(512, SEQ_LEN)
    usable = jnp.arange(SEQ_LEN) < length

    def attend_block(query_block):
        scores = jnp.einsum(
            "qhd,khd->hqk", query_block, keys_rot, preferred_element_type=jnp.float32
        )
        scores = jnp.where(usable[None, None, :], scores, -jnp.inf)
        largest = jnp.max(scores, axis=-1, keepdims=True)
        exp_scores = jnp.exp(scores - largest)
        totals = jnp.sum(exp_scores, axis=-1, keepdims=True)
        weights_soft = (exp_scores / totals).astype(jnp.bfloat16)
        mixture = jnp.einsum(
            "hqk,khd->qhd", weights_soft, values, preferred_element_type=jnp.float32
        )
        return (mixture, largest[..., 0] + jnp.log(totals[..., 0]))

    mixture, logsum = lax.map(
        attend_block, queries.reshape(SEQ_LEN // block_rows, block_rows, HEADS, HEAD_DIM)
    )
    return (mixture.reshape(SEQ_LEN, D), logsum)


def attend_backward(queries, keys_rot, values, length, logsum, grad_mixture):
    block_rows = min(512, SEQ_LEN)
    block_count = SEQ_LEN // block_rows
    usable = jnp.arange(SEQ_LEN) < length

    def attend_block(carried_grads, pieces):
        key_grad, value_grad = carried_grads
        query_block, grad_block, sums_block = pieces
        scores = jnp.einsum(
            "qhd,khd->hqk", query_block, keys_rot, preferred_element_type=jnp.float32
        )
        scores = jnp.where(usable[None, None, :], scores, -jnp.inf)
        weights_soft = jnp.exp(scores - sums_block[..., None])
        prob_grad = jnp.einsum(
            "qhd,khd->hqk", grad_block, values, preferred_element_type=jnp.float32
        )
        row_terms = jnp.sum(weights_soft * prob_grad, axis=-1, keepdims=True)
        score_grad = (weights_soft * (prob_grad - row_terms)).astype(jnp.bfloat16)
        query_grad = jnp.einsum(
            "hqk,khd->qhd", score_grad, keys_rot, preferred_element_type=jnp.float32
        )
        key_grad = key_grad + jnp.einsum(
            "hqk,qhd->khd", score_grad, query_block, preferred_element_type=jnp.float32
        )
        value_grad = value_grad + jnp.einsum(
            "hqk,qhd->khd",
            weights_soft.astype(jnp.bfloat16),
            grad_block,
            preferred_element_type=jnp.float32,
        )
        return ((key_grad, value_grad), query_grad)

    zero_grads = jnp.zeros((SEQ_LEN, HEADS, HEAD_DIM), jnp.float32)
    pieces = (
        queries.reshape(block_count, block_rows, HEADS, HEAD_DIM),
        grad_mixture.reshape(block_count, block_rows, HEADS, HEAD_DIM),
        logsum,
    )
    (key_grad, value_grad), query_grad = lax.scan(attend_block, (zero_grads, zero_grads), pieces)
    return (query_grad.reshape(SEQ_LEN, HEADS, HEAD_DIM), key_grad, value_grad)


def spare_forward(stream, live_rows, length, modrow, weights, down_full):
    return jnp.zeros((SEQ_LEN, D), jnp.float32)


def attention_forward(stream, live_rows, length, modrow, weights, down_full):
    normed, modulate_back, gating = norm_parts(stream, modrow)
    queries, keys_rot, values = attention_inputs(normed, weights)
    mixture, logsum = attend_forward(queries, keys_rot, values, length)
    branch = jnp.dot(
        mixture.astype(jnp.bfloat16), weights[:, 3 * D :], preferred_element_type=jnp.float32
    )
    return stream.astype(jnp.float32) + live_rows[:, None] * gating * branch


def feedforward_forward(stream, live_rows, length, modrow, weights, down_full):
    normed, modulate_back, gating = norm_parts(stream, modrow)
    hidden = jnp.dot(normed, weights, preferred_element_type=jnp.float32)
    activation = gelu_tanh(hidden).astype(jnp.bfloat16)
    branch = jnp.dot(activation, down_full, preferred_element_type=jnp.float32)
    return stream.astype(jnp.float32) + live_rows[:, None] * gating * branch


def spare_backward(stream, grad_out, live_rows, length, modrow, weights, down_full):
    return (
        jnp.zeros((SEQ_LEN, D), jnp.float32),
        jnp.zeros((3 * D,), jnp.float32),
        jnp.zeros((D, FF), jnp.float32),
        jnp.zeros((FF, D), jnp.float32),
    )


def attention_backward(stream, grad_out, live_rows, length, modrow, weights, down_full):
    normed, modulate_back, gating = norm_parts(stream, modrow)
    queries, keys_rot, values = attention_inputs(normed, weights)
    mixture, logsum = attend_forward(queries, keys_rot, values, length)
    mixture_low = mixture.astype(jnp.bfloat16)
    out_weight = weights[:, 3 * D :]
    branch = jnp.dot(mixture_low, out_weight, preferred_element_type=jnp.float32)
    masked = grad_out * live_rows[:, None]
    gate_grad = jnp.sum(masked * branch, axis=0)
    branch_grad = (masked * gating).astype(jnp.bfloat16)
    out_weight_grad = jnp.dot(mixture_low.T, branch_grad, preferred_element_type=jnp.float32)
    mixture_grad = jnp.dot(branch_grad, out_weight.T, preferred_element_type=jnp.float32).astype(
        jnp.bfloat16
    )
    query_grad, key_grad, value_grad = attend_backward(
        queries, keys_rot, values, length, logsum, split_heads(mixture_grad)
    )
    cosine, sine_table = rope_tables()
    query_pre = rotate(rounded(query_grad) * 0.125, cosine, -sine_table)
    key_pre = rotate(rounded(key_grad), cosine, -sine_table)
    value_pre = rounded(value_grad)
    project_grad = jnp.concatenate(
        [query_pre.reshape(SEQ_LEN, D), key_pre.reshape(SEQ_LEN, D), value_pre.reshape(SEQ_LEN, D)],
        axis=1,
    ).astype(jnp.bfloat16)
    in_weight = weights[:, : 3 * D]
    in_weight_grad = jnp.dot(normed.T, project_grad, preferred_element_type=jnp.float32)
    normed_grad = jnp.dot(project_grad, in_weight.T, preferred_element_type=jnp.float32)
    stream_grad, offset_grad, scaling_grad = modulate_back(normed_grad)
    return (
        grad_out + stream_grad,
        jnp.concatenate([offset_grad, scaling_grad, gate_grad]),
        jnp.concatenate([in_weight_grad, out_weight_grad], axis=1),
        jnp.zeros((FF, D), jnp.float32),
    )


def feedforward_backward(stream, grad_out, live_rows, length, modrow, weights, down_full):
    normed, modulate_back, gating = norm_parts(stream, modrow)
    hidden = jnp.dot(normed, weights, preferred_element_type=jnp.float32)
    activation_wide, gelu_back = jax.vjp(gelu_tanh, hidden)
    activation = activation_wide.astype(jnp.bfloat16)
    branch = jnp.dot(activation, down_full, preferred_element_type=jnp.float32)
    masked = grad_out * live_rows[:, None]
    gate_grad = jnp.sum(masked * branch, axis=0)
    branch_grad = (masked * gating).astype(jnp.bfloat16)
    down_grad = jnp.dot(activation.T, branch_grad, preferred_element_type=jnp.float32)
    activation_grad = jnp.dot(branch_grad, down_full.T, preferred_element_type=jnp.float32)
    hidden_grad = gelu_back(activation_grad)[0].astype(jnp.bfloat16)
    up_grad = jnp.dot(normed.T, hidden_grad, preferred_element_type=jnp.float32)
    normed_grad = jnp.dot(hidden_grad, weights.T, preferred_element_type=jnp.float32)
    stream_grad, offset_grad, scaling_grad = modulate_back(normed_grad)
    return (
        grad_out + stream_grad,
        jnp.concatenate([offset_grad, scaling_grad, gate_grad]),
        up_grad,
        down_grad,
    )


def local(block_input, cotangent, lengths, steps, mod_weight, mod_bias, first_weight, down_rows):
    segments = lax.axis_size("segment")
    segment_index = lax.axis_index("segment")
    micro_count = block_input.shape[0]
    odd_segment = segment_index % 2 == 1
    weights = first_weight[0]
    own_rows = down_rows[0]
    partner = shifted(own_rows, "segment", 1)
    down_full = jnp.concatenate([partner, own_rows], axis=0)
    conditions = time_cond(steps).astype(jnp.bfloat16)
    modulation = jnp.dot(conditions, mod_weight[0], preferred_element_type=jnp.float32) + mod_bias[
        0
    ].astype(jnp.float32)
    positions = jnp.arange(SEQ_LEN)
    tick_count = micro_count + segments - 1
    forward_kinds = [spare_forward, attention_forward, feedforward_forward]
    backward_kinds = [spare_backward, attention_backward, feedforward_backward]

    def forward_tick(moment, state):
        carried, kept_inputs, final_rows = state
        micro_index = moment - segment_index
        active = (micro_index >= 0) & (micro_index < micro_count)
        slot_index = jnp.clip(micro_index, 0, micro_count - 1)
        entering = jnp.where(segment_index == 0, block_input[slot_index], carried)
        kept_inputs = kept_inputs.at[slot_index].set(
            jnp.where(active, entering, kept_inputs[slot_index])
        )
        length = lengths[slot_index]
        live_rows = (positions < length).astype(jnp.float32)
        selector = jnp.where(active, 1 + segment_index % 2, 0)
        leaving = lax.switch(
            selector,
            forward_kinds,
            entering,
            live_rows,
            length,
            modulation[slot_index],
            weights,
            down_full,
        )
        keep_final = active & (segment_index == segments - 1)
        final_rows = final_rows.at[slot_index].set(
            jnp.where(keep_final, leaving, final_rows[slot_index])
        )
        carried = shifted(leaving.astype(jnp.bfloat16), "segment", 1)
        return (carried, kept_inputs, final_rows)

    forward_start = (
        jnp.zeros((SEQ_LEN, D), jnp.bfloat16),
        jnp.zeros((micro_count, SEQ_LEN, D), jnp.bfloat16),
        jnp.zeros((micro_count, SEQ_LEN, D), jnp.float32),
    )
    carried, kept_inputs, final_rows = lax.fori_loop(0, tick_count, forward_tick, forward_start)

    def backward_tick(moment, state):
        back_carried, input_grads, mod_grads, first_grad, down_grad = state
        micro_index = moment - (segments - 1 - segment_index)
        active = (micro_index >= 0) & (micro_index < micro_count)
        slot_index = jnp.clip(micro_index, 0, micro_count - 1)
        grad_out = jnp.where(
            segment_index == segments - 1, cotangent[slot_index], back_carried
        ).astype(jnp.float32)
        length = lengths[slot_index]
        live_rows = (positions < length).astype(jnp.float32)
        selector = jnp.where(active, 1 + segment_index % 2, 0)
        stream_grad, mod_grad, weight_grad, rows_grad = lax.switch(
            selector,
            backward_kinds,
            kept_inputs[slot_index],
            grad_out,
            live_rows,
            length,
            modulation[slot_index],
            weights,
            down_full,
        )
        mod_grads = mod_grads.at[slot_index].set(jnp.where(active, mod_grad, mod_grads[slot_index]))
        first_grad = first_grad + weight_grad
        down_grad = down_grad + rows_grad
        keep_grad = active & (segment_index == 0)
        input_grads = input_grads.at[slot_index].set(
            jnp.where(keep_grad, stream_grad, input_grads[slot_index])
        )
        back_carried = shifted(stream_grad.astype(jnp.bfloat16), "segment", -1)
        return (back_carried, input_grads, mod_grads, first_grad, down_grad)

    backward_start = (
        jnp.zeros((SEQ_LEN, D), jnp.bfloat16),
        jnp.zeros((micro_count, SEQ_LEN, D), jnp.float32),
        jnp.zeros((micro_count, 3 * D), jnp.float32),
        jnp.zeros((D, FF), jnp.float32),
        jnp.zeros((FF, D), jnp.float32),
    )
    back_carried, input_grads, mod_grads, first_grad, down_grad = lax.fori_loop(
        0, tick_count, backward_tick, backward_start
    )
    cond_wide = conditions.astype(jnp.float32)
    mod_w_grad = jnp.dot(
        cond_wide.T, mod_grads, precision=lax.Precision.HIGHEST, preferred_element_type=jnp.float32
    )
    mod_b_grad = jnp.sum(mod_grads, axis=0)
    half_rows = FF // 2
    outgoing = jnp.where(odd_segment, down_grad[:half_rows], 0.0)
    incoming = shifted(outgoing.astype(jnp.bfloat16), "segment", -1).astype(outgoing.dtype)
    own_rows_grad = jnp.where(odd_segment, down_grad[half_rows:], incoming)
    mod_w_sum, mod_b_sum, first_sum, rows_sum = (
        lax.psum_scatter(mod_w_grad, "dp", scatter_dimension=0, tiled=True),
        lax.psum_scatter(mod_b_grad, "dp", scatter_dimension=0, tiled=True),
        lax.psum_scatter(first_grad, "dp", scatter_dimension=0, tiled=True),
        lax.psum_scatter(own_rows_grad, "dp", scatter_dimension=0, tiled=True),
    )
    top_term = jnp.where(segment_index == segments - 1, final_rows, 0.0)
    bottom = jnp.where(segment_index == 0, input_grads, 0.0)
    out_rows, grad_rows = (
        lax.psum_scatter(
            top_term.astype(jnp.bfloat16), "segment", scatter_dimension=1, tiled=True
        ).astype(jnp.float32),
        lax.psum_scatter(
            bottom.astype(jnp.bfloat16), "segment", scatter_dimension=1, tiled=True
        ).astype(jnp.float32),
    )
    return (
        out_rows.astype(jnp.bfloat16),
        grad_rows,
        mod_w_sum[None],
        mod_b_sum[None],
        first_sum[None],
        rows_sum[None],
    )


def solution(mesh):
    in_specs = (
        P("dp", None, None),
        P("dp", None, None),
        P("dp"),
        P("dp"),
        P("segment", None, None),
        P("segment", None),
        P("segment", None, None),
        P("segment", None, None),
    )
    out_specs = (
        P("dp", "segment", None),
        P("dp", "segment", None),
        P("segment", "dp", None),
        P("segment", "dp"),
        P("segment", "dp", None),
        P("segment", "dp", None),
    )
    return jax.shard_map(local, mesh=mesh, in_specs=in_specs, out_specs=out_specs, check_vma=False)
```

profile of v0, /device:TPU:0, one launch (start us, length us, event | category | flops | bytes accessed | tf_op | source)
XLA Modules:
  0.0 2484.9 jit_solution(12798698584482451048)
XLA Ops:
  16.7 46.4 %collective-permute-done.2 = bf16[1536,768]{1,0:T(8,128)(2,1)} collective-permute-done((bf16[1536,768]{1,0:T(8,128)(2,1)}, bf16[1536,768]{1,0:T(8,128)(2,1)}, u32[]{:S(2)}, u32[]{:S(2)}) %collective-permute-start.2) | collective-permute-done | bytes 2359328 | tf_op jit(solution)/shard_map/ppermute | solution.py:18
  72.2 665.5 %while.87 = (s32[]{:T(128)}, bf16[1024,768]{1,0:T(8,128)(2,1)}, bf16[2,1024,768]{2,1,0:T(8,128)(2,1)}, bf16[2,1024,768]{2,1,0:T(8,128)(2,1)}, s32[]{:T(128)}, /*...) while((s32[]{:T(128)}, bf16[1024,768]{1,0:T(8,128)(2,1)}, ...), condition=%wide.region_13.14_spmd.clone, body=%wide.region_0.13_spmd.clone.sunk | while | flops 9709293568 | bytes 338100544 | solution.py:294
  80.9 140.1 %conditional.6 = (bf16[1024,768]{1,0:T(8,128)(2,1)}) conditional(s32[]{:T(128)} %clamp.22, () %tuple.233, (bf16[1024,768]{1,0:T(8,128)(2,1)S(1)}, f32[1024]{0:T(1024)S(1)}, f32[2304]{0:T(1024)S(1)}, bf16[768,3072]{1,0:T(8,128)(2,1)}, s32[]{:T(128)}) %tuple.234, (bf16[1024,768]{1,0:T(8,128)(2,1)S(1)}, f32[1024]{0:T(1024)S(1)}, ...), branch_computations={%region_1.1_spmd, %region_2.0_spmd, %region_9.11_spmd} | conditional | flops 9705359360 | bytes 256288384 | solution.py:272
  110.2 103.3 %while.84 = (s32[]{:T(128)}, bf16[2,512,12,64]{1,3,2,0:T(8,128)(2,1)}, bf16[2,512,12,64]{1,3,2,0:T(8,128)(2,1)S(1)}, bf16[1024,12,64]{0,2,1:T(8,128)(2,1)S(1)}, ...) while((s32[]{:T(128)}, bf16[2,512,12,64]{1,3,2,0:T(8,128)(2,1)}, ...), condition=%wide.region_8.7_spmd.clone, body=%wide.region_5.6_spmd.clone.sunk | while | flops 1648363520 | bytes 118810776 | solution.py:103
  120.8 29.1 %fusion.249 = (f32[12,512]{1,0:T(8,128)S(1)}, f32[12,512,1024]{2,1,0:T(8,128)}) fusion(f32[12,512,1024]{2,1,0:T(8,128)} %fusion.248, pred[1024]{0:T(1024)(128)(4,1)S(1)} %iota_compare_fusion.10), kind=kOutput, calls=%fused_computation.273.clone.1 | output fusion | flops 25166848 | bytes 50357248 | tf_op jit(solution)/shard_map/while/body/eval_jaxpr/cond/branch_1_fun/while/body/eval_jaxpr/sub | solution.py:95
  172.5 29.1 %fusion.249 = (f32[12,512]{1,0:T(8,128)S(1)}, f32[12,512,1024]{2,1,0:T(8,128)}) fusion(f32[12,512,1024]{2,1,0:T(8,128)} %fusion.248, pred[1024]{0:T(1024)(128)(4,1)S(1)} %iota_compare_fusion.10), kind=kOutput, calls=%fused_computation.273.clone.1 | output fusion | flops 25166848 | bytes 50357248 | tf_op jit(solution)/shard_map/while/body/eval_jaxpr/cond/branch_1_fun/while/body/eval_jaxpr/sub | solution.py:95
  225.9 29.8 %collective-permute-done.1 = bf16[1024,768]{1,0:T(8,128)(2,1)S(1)} collective-permute-done((bf16[1024,768]{1,0:T(8,128)(2,1)}, bf16[1024,768]{1,0:T(8,128)(2,1)S(1)}, u32[]{:S(2)}, u32[]{:S(2)}) %collective-permute-start.1) | collective-permute-done | bytes 1572896 | tf_op jit(solution)/shard_map/while/body/eval_jaxpr/ppermute | solution.py:18
  265.5 140.1 %conditional.6 = (bf16[1024,768]{1,0:T(8,128)(2,1)}) conditional(s32[]{:T(128)} %clamp.22, () %tuple.233, (bf16[1024,768]{1,0:T(8,128)(2,1)S(1)}, f32[1024]{0:T(1024)S(1)}, f32[2304]{0:T(1024)S(1)}, bf16[768,3072]{1,0:T(8,128)(2,1)}, s32[]{:T(128)}) %tuple.234, (bf16[1024,768]{1,0:T(8,128)(2,1)S(1)}, f32[1024]{0:T(1024)S(1)}, ...), branch_computations={%region_1.1_spmd, %region_2.0_spmd, %region_9.11_spmd} | conditional | flops 9705359360 | bytes 256288384 | solution.py:272
  294.8 103.3 %while.84 = (s32[]{:T(128)}, bf16[2,512,12,64]{1,3,2,0:T(8,128)(2,1)}, bf16[2,512,12,64]{1,3,2,0:T(8,128)(2,1)S(1)}, bf16[1024,12,64]{0,2,1:T(8,128)(2,1)S(1)}, ...) while((s32[]{:T(128)}, bf16[2,512,12,64]{1,3,2,0:T(8,128)(2,1)}, ...), condition=%wide.region_8.7_spmd.clone, body=%wide.region_5.6_spmd.clone.sunk | while | flops 1648363520 | bytes 118810776 | solution.py:103
  305.4 29.1 %fusion.249 = (f32[12,512]{1,0:T(8,128)S(1)}, f32[12,512,1024]{2,1,0:T(8,128)}) fusion(f32[12,512,1024]{2,1,0:T(8,128)} %fusion.248, pred[1024]{0:T(1024)(128)(4,1)S(1)} %iota_compare_fusion.10), kind=kOutput, calls=%fused_computation.273.clone.1 | output fusion | flops 25166848 | bytes 50357248 | tf_op jit(solution)/shard_map/while/body/eval_jaxpr/cond/branch_1_fun/while/body/eval_jaxpr/sub | solution.py:95
  357.1 29.1 %fusion.249 = (f32[12,512]{1,0:T(8,128)S(1)}, f32[12,512,1024]{2,1,0:T(8,128)}) fusion(f32[12,512,1024]{2,1,0:T(8,128)} %fusion.248, pred[1024]{0:T(1024)(128)(4,1)S(1)} %iota_compare_fusion.10), kind=kOutput, calls=%fused_computation.273.clone.1 | output fusion | flops 25166848 | bytes 50357248 | tf_op jit(solution)/shard_map/while/body/eval_jaxpr/cond/branch_1_fun/while/body/eval_jaxpr/sub | solution.py:95
  410.5 29.1 %collective-permute-done.1 = bf16[1024,768]{1,0:T(8,128)(2,1)S(1)} collective-permute-done((bf16[1024,768]{1,0:T(8,128)(2,1)}, bf16[1024,768]{1,0:T(8,128)(2,1)S(1)}, u32[]{:S(2)}, u32[]{:S(2)}) %collective-permute-start.1) | collective-permute-done | bytes 1572896 | tf_op jit(solution)/shard_map/while/body/eval_jaxpr/ppermute | solution.py:18
  474.1 28.2 %collective-permute-done.1 = bf16[1024,768]{1,0:T(8,128)(2,1)S(1)} collective-permute-done((bf16[1024,768]{1,0:T(8,128)(2,1)}, bf16[1024,768]{1,0:T(8,128)(2,1)S(1)}, u32[]{:S(2)}, u32[]{:S(2)}) %collective-permute-start.1) | collective-permute-done | bytes 1572896 | tf_op jit(solution)/shard_map/while/body/eval_jaxpr/ppermute | solution.py:18
  523.7 27.3 %collective-permute-done.1 = bf16[1024,768]{1,0:T(8,128)(2,1)S(1)} collective-permute-done((bf16[1024,768]{1,0:T(8,128)(2,1)}, bf16[1024,768]{1,0:T(8,128)(2,1)S(1)}, u32[]{:S(2)}, u32[]{:S(2)}) %collective-permute-start.1) | collective-permute-done | bytes 1572896 | tf_op jit(solution)/shard_map/while/body/eval_jaxpr/ppermute | solution.py:18
  562.1 144.6 %collective-permute-start.1 = (bf16[1024,768]{1,0:T(8,128)(2,1)}, bf16[1024,768]{1,0:T(8,128)(2,1)S(1)}, u32[]{:S(2)}, u32[]{:S(2)}) collective-permute-start(bf16[1024,768]{1,0:T(8,128)(2,1)} %get-tuple-element.1847), channel_id=1, source_target_pairs={{0,8},{8,16},{16,24},{1,9},{9,17},{17,25},{2,10},{10,18},{18,26},{... | collective-permute-start | bytes 4718600 | tf_op jit(solution)/shard_map/while/body/eval_jaxpr/ppermute | solution.py:18
  710.2 26.3 %collective-permute-done.1 = bf16[1024,768]{1,0:T(8,128)(2,1)S(1)} collective-permute-done((bf16[1024,768]{1,0:T(8,128)(2,1)}, bf16[1024,768]{1,0:T(8,128)(2,1)S(1)}, u32[]{:S(2)}, u32[]{:S(2)}) %collective-permute-start.1) | collective-permute-done | bytes 1572896 | tf_op jit(solution)/shard_map/while/body/eval_jaxpr/ppermute | solution.py:18
  740.9 1379.6 %while.88 = (s32[]{:T(128)}, bf16[1024,768]{1,0:T(8,128)(2,1)}, bf16[2,1024,768]{2,1,0:T(8,128)(2,1)}, f32[2,2304]{1,0:T(2,128)S(1)}, f32[768,3072]{1,0:T(8,128)...) while((s32[]{:T(128)}, bf16[1024,768]{1,0:T(8,128)(2,1)}, ...), condition=%wide.region_42.43_spmd.clone, body=%wide.region_15.42_spmd.clone.sunk | while | flops 29165631488 | bytes 740556608 | solution.py:335
  920.9 451.8 %collective-permute-done = bf16[1024,768]{1,0:T(8,128)(2,1)} collective-permute-done((bf16[1024,768]{1,0:T(8,128)(2,1)}, bf16[1024,768]{1,0:T(8,128)(2,1)}, u32[]{:S(2)}, u32[]{:S(2)}) %collective-permute-start) | collective-permute-done | bytes 1572896 | tf_op jit(solution)/shard_map/while/body/eval_jaxpr/ppermute | solution.py:18
  1380.3 329.4 %conditional.7 = (bf16[1024,768]{1,0:T(8,128)(2,1)}, f32[2304]{0:T(1024)}, f32[768,3072]{1,0:T(8,128)}, f32[3072,768]{1,0:T(8,128)}) conditional(s32[]{:T(128)} %clamp.23, () %tuple.238, (bf16[1024,768]{1,0:T(8,128)(2,1)S(1)}, f32[2304]{0:T(1024)S(1)}, bf16[768,3072]{1,0:T(8,128)(2,1)}, f32[1024]{0:T(1024)S(1)}, ...), branch_computations={%region_16.16_spmd, %region_17.31_spmd, %region_32.39_spmd} | conditional | flops 29153042432 | bytes 641128704 | solution.py:307
  1411.7 67.6 %while.85 = (s32[]{:T(128)}, bf16[2,512,12,64]{1,3,2,0:T(8,128)(2,1)}, f32[2,12,512]{2,1,0:T(8,128)S(1)}, bf16[2,512,12,64]{1,3,2,0:T(8,128)(2,1)S(1)}, bf16[102...) while((s32[]{:T(128)}, ...), condition=%wide.region_23.22_spmd.clone, body=%wide.region_20.21_spmd.clone.sunk | while | flops 1667230720 | bytes 100118728 | solution.py:103
  1494.9 161.6 %while.86 = (s32[]{:T(128)}, f32[1024,12,64]{0,2,1:T(8,128)}, f32[1024,12,64]{0,2,1:T(8,128)}, bf16[2,512,12,64]{1,3,2,0:T(8,128)(2,1)}, bf16[2,512,12,64]{1,3,2...) while((s32[]{:T(128)}, f32[1024,12,64]{0,2,1:T(8,128)}, ...), condition=%wide.region_26.25_spmd.clone, body=%wide.region_24.24_spmd.clone.sunk | while | flops 4105169920 | bytes 217239728 | solution.py:147
  1522.9 21.5 multiply_convert_fusion.11
  1602.5 21.5 multiply_convert_fusion.11
  1752.8 329.6 %conditional.7 = (bf16[1024,768]{1,0:T(8,128)(2,1)}, f32[2304]{0:T(1024)}, f32[768,3072]{1,0:T(8,128)}, f32[3072,768]{1,0:T(8,128)}) conditional(s32[]{:T(128)} %clamp.23, () %tuple.238, (bf16[1024,768]{1,0:T(8,128)(2,1)S(1)}, f32[2304]{0:T(1024)S(1)}, bf16[768,3072]{1,0:T(8,128)(2,1)}, f32[1024]{0:T(1024)S(1)}, ...), branch_computations={%region_16.16_spmd, %region_17.31_spmd, %region_32.39_spmd} | conditional | flops 29153042432 | bytes 641128704 | solution.py:307
  1784.6 67.6 %while.85 = (s32[]{:T(128)}, bf16[2,512,12,64]{1,3,2,0:T(8,128)(2,1)}, f32[2,12,512]{2,1,0:T(8,128)S(1)}, bf16[2,512,12,64]{1,3,2,0:T(8,128)(2,1)S(1)}, bf16[102...) while((s32[]{:T(128)}, ...), condition=%wide.region_23.22_spmd.clone, body=%wide.region_20.21_spmd.clone.sunk | while | flops 1667230720 | bytes 100118728 | solution.py:103
  1867.8 161.4 %while.86 = (s32[]{:T(128)}, f32[1024,12,64]{0,2,1:T(8,128)}, f32[1024,12,64]{0,2,1:T(8,128)}, bf16[2,512,12,64]{1,3,2,0:T(8,128)(2,1)}, bf16[2,512,12,64]{1,3,2...) while((s32[]{:T(128)}, f32[1024,12,64]{0,2,1:T(8,128)}, ...), condition=%wide.region_26.25_spmd.clone, body=%wide.region_24.24_spmd.clone.sunk | while | flops 4105169920 | bytes 217239728 | solution.py:147
  1895.5 21.5 multiply_convert_fusion.11
  2133.9 73.6 %collective-permute-done.3 = bf16[1536,768]{1,0:T(8,128)(2,1)S(1)} collective-permute-done((bf16[1536,768]{1,0:T(8,128)(2,1)S(1)}, bf16[1536,768]{1,0:T(8,128)(2,1)S(1)}, u32[]{:S(2)}, u32[]{:S(2)}) %collective-permute-start.3) | collective-permute-done | bytes 2359328 | tf_op jit(solution)/shard_map/ppermute | solution.py:18
  2221.7 25.9 %all-reduce = f32[2304]{0:T(1024)} all-reduce(f32[2304]{0:T(1024)S(1)} %reduce_sum.209), channel_id=5, replica_groups=mesh['segment'=4,'dp'=8] {'dp'}, use_global_device_ids=true, to_apply=%region_46.47.clone | all-reduce | flops 2304 | bytes 18432
  2251.5 47.2 %reduce-scatter.14.cloned.1.call-done = f32[192,768]{1,0:T(8,128)} async-done(((f32[1536,768]{1,0:T(8,128)}), f32[192,768]{1,0:T(8,128)}) %reduce-scatter.14.cloned.1.call-update) | async-done | bytes 589840 | tf_op jit(solution)/shard_map/reduce_scatter | solution.py:351
  2298.7 78.4 %reduce-scatter.10.cloned.1.call-done = f32[96,2304]{1,0:T(8,128)} async-done(((f32[768,2304]{1,0:T(8,128)}), f32[96,2304]{1,0:T(8,128)}) %reduce-scatter.10.cloned.1.call-update) | async-done | bytes 884752 | tf_op jit(solution)/shard_map/reduce_scatter | solution.py:348
  2377.1 100.6 %reduce-scatter.12.cloned.1.call-done = f32[96,3072]{1,0:T(8,128)} async-done(((f32[768,3072]{1,0:T(8,128)}), f32[96,3072]{1,0:T(8,128)}) %reduce-scatter.12.cloned.1.call-update) | async-done | bytes 1179664 | tf_op jit(solution)/shard_map/reduce_scatter | solution.py:350
  (757 shorter events, 1184.4 us)
Async XLA Ops:
  7.2 2241.7 %reduce-scatter.8.cloned.1.call-start = ((), (), s32[]{:S(2)}) async-start(), calls=%async_computation.6 | async-start | bytes 3932160 | tf_op jit(solution)/shard_map/reduce_scatter | solution.py:359
  7.2 55.9 %collective-permute-start.2 = (bf16[1536,768]{1,0:T(8,128)(2,1)}, bf16[1536,768]{1,0:T(8,128)(2,1)}, u32[]{:S(2)}, u32[]{:S(2)}) collective-permute-start(bf16[1536,768]{1,0:T(8,128)(2,1)} %bitcast.239), channel_id=1, source_target_pairs={{0,8},{8,16},{16,24},{1,9},{9,17},{17,25},{2,10},{10,18},{18,26},{... | collective-permute-start | bytes 7077896 | tf_op jit(solution)/shard_map/ppermute | solution.py:18
  13.8 49.4 %copy-start.30 = (bf16[1,1536,768]{2,1,0:T(8,128)(2,1)S(1)}, bf16[1,1536,768]{2,1,0:T(8,128)(2,1)}, u32[]{:S(2)}) copy-start(bf16[1,1536,768]{2,1,0:T(8,128)(2,1)} %param.39) | copy-start | bytes 7077892
  221.0 34.6 %collective-permute-start.1 = (bf16[1024,768]{1,0:T(8,128)(2,1)}, bf16[1024,768]{1,0:T(8,128)(2,1)S(1)}, u32[]{:S(2)}, u32[]{:S(2)}) collective-permute-start(bf16[1024,768]{1,0:T(8,128)(2,1)} %get-tuple-element.1847), channel_id=1, source_target_pairs={{0,8},{8,16},{16,24},{1,9},{9,17},{17,25},{2,10},{10,18},{18,26},{... | collective-permute-start | bytes 4718600 | tf_op jit(solution)/shard_map/while/body/eval_jaxpr/ppermute | solution.py:18
  224.8 32.0 %copy-start.56 = (s32[3]{0:T(128)S(1)}, s32[3]{0:T(128)}, u32[]{:S(2)}) copy-start(s32[3]{0:T(128)} %get-tuple-element.1892) | copy-start | bytes 40 | tf_op jit(solution)/shard_map/while
  224.8 32.0 %copy-start.64 = (s32[2]{0:T(128)S(1)}, s32[2]{0:T(128)}, u32[]{:S(2)}) copy-start(s32[2]{0:T(128)} %get-tuple-element.1916) | copy-start | bytes 28 | tf_op jit(solution)/shard_map/while
  225.9 29.8 %copy-start.21 = (bf16[2,1024,768]{2,1,0:T(8,128)(2,1)}, bf16[2,1024,768]{2,1,0:T(8,128)(2,1)S(1)}, u32[]{:S(2)}) copy-start(bf16[2,1024,768]{2,1,0:T(8,128)(2,1)S(1)} %fusion.228) | copy-start | bytes 9437188 | tf_op jit(solution)/shard_map/while
  405.6 34.0 %collective-permute-start.1 = (bf16[1024,768]{1,0:T(8,128)(2,1)}, bf16[1024,768]{1,0:T(8,128)(2,1)S(1)}, u32[]{:S(2)}, u32[]{:S(2)}) collective-permute-start(bf16[1024,768]{1,0:T(8,128)(2,1)} %get-tuple-element.1847), channel_id=1, source_target_pairs={{0,8},{8,16},{16,24},{1,9},{9,17},{17,25},{2,10},{10,18},{18,26},{... | collective-permute-start | bytes 4718600 | tf_op jit(solution)/shard_map/while/body/eval_jaxpr/ppermute | solution.py:18
  409.4 31.4 %copy-start.56 = (s32[3]{0:T(128)S(1)}, s32[3]{0:T(128)}, u32[]{:S(2)}) copy-start(s32[3]{0:T(128)} %get-tuple-element.1892) | copy-start | bytes 40 | tf_op jit(solution)/shard_map/while
  409.4 31.4 %copy-start.64 = (s32[2]{0:T(128)S(1)}, s32[2]{0:T(128)}, u32[]{:S(2)}) copy-start(s32[2]{0:T(128)} %get-tuple-element.1916) | copy-start | bytes 28 | tf_op jit(solution)/shard_map/while
  450.7 51.6 %collective-permute-start.1 = (bf16[1024,768]{1,0:T(8,128)(2,1)}, bf16[1024,768]{1,0:T(8,128)(2,1)S(1)}, u32[]{:S(2)}, u32[]{:S(2)}) collective-permute-start(bf16[1024,768]{1,0:T(8,128)(2,1)} %get-tuple-element.1847), channel_id=1, source_target_pairs={{0,8},{8,16},{16,24},{1,9},{9,17},{17,25},{2,10},{10,18},{18,26},{... | collective-permute-start | bytes 4718600 | tf_op jit(solution)/shard_map/while/body/eval_jaxpr/ppermute | solution.py:18
  473.0 30.5 %copy-start.56 = (s32[3]{0:T(128)S(1)}, s32[3]{0:T(128)}, u32[]{:S(2)}) copy-start(s32[3]{0:T(128)} %get-tuple-element.1892) | copy-start | bytes 40 | tf_op jit(solution)/shard_map/while
  473.0 30.5 %copy-start.64 = (s32[2]{0:T(128)S(1)}, s32[2]{0:T(128)}, u32[]{:S(2)}) copy-start(s32[2]{0:T(128)} %get-tuple-element.1916) | copy-start | bytes 28 | tf_op jit(solution)/shard_map/while
  513.4 37.6 %collective-permute-start.1 = (bf16[1024,768]{1,0:T(8,128)(2,1)}, bf16[1024,768]{1,0:T(8,128)(2,1)S(1)}, u32[]{:S(2)}, u32[]{:S(2)}) collective-permute-start(bf16[1024,768]{1,0:T(8,128)(2,1)} %get-tuple-element.1847), channel_id=1, source_target_pairs={{0,8},{8,16},{16,24},{1,9},{9,17},{17,25},{2,10},{10,18},{18,26},{... | collective-permute-start | bytes 4718600 | tf_op jit(solution)/shard_map/while/body/eval_jaxpr/ppermute | solution.py:18
  562.1 174.5 %collective-permute-start.1 = (bf16[1024,768]{1,0:T(8,128)(2,1)}, bf16[1024,768]{1,0:T(8,128)(2,1)S(1)}, u32[]{:S(2)}, u32[]{:S(2)}) collective-permute-start(bf16[1024,768]{1,0:T(8,128)(2,1)} %get-tuple-element.1847), channel_id=1, source_target_pairs={{0,8},{8,16},{16,24},{1,9},{9,17},{17,25},{2,10},{10,18},{18,26},{... | collective-permute-start | bytes 4718600 | tf_op jit(solution)/shard_map/while/body/eval_jaxpr/ppermute | solution.py:18
  768.3 35.1 %collective-permute-start = (bf16[1024,768]{1,0:T(8,128)(2,1)}, bf16[1024,768]{1,0:T(8,128)(2,1)}, u32[]{:S(2)}, u32[]{:S(2)}) collective-permute-start(bf16[1024,768]{1,0:T(8,128)(2,1)} %get-tuple-element.1600), channel_id=1, source_target_pairs={{8,0},{16,8},{24,16},{9,1},{17,9},{25,17},{10,2},{18,10},{26,18},{... | collective-permute-start | bytes 4718600 | tf_op jit(solution)/shard_map/while/body/eval_jaxpr/ppermute | solution.py:18
  821.9 46.5 %collective-permute-start = (bf16[1024,768]{1,0:T(8,128)(2,1)}, bf16[1024,768]{1,0:T(8,128)(2,1)}, u32[]{:S(2)}, u32[]{:S(2)}) collective-permute-start(bf16[1024,768]{1,0:T(8,128)(2,1)} %get-tuple-element.1600), channel_id=1, source_target_pairs={{8,0},{16,8},{24,16},{9,1},{17,9},{25,17},{10,2},{18,10},{26,18},{... | collective-permute-start | bytes 4718600 | tf_op jit(solution)/shard_map/while/body/eval_jaxpr/ppermute | solution.py:18
  886.9 485.8 %collective-permute-start = (bf16[1024,768]{1,0:T(8,128)(2,1)}, bf16[1024,768]{1,0:T(8,128)(2,1)}, u32[]{:S(2)}, u32[]{:S(2)}) collective-permute-start(bf16[1024,768]{1,0:T(8,128)(2,1)} %get-tuple-element.1600), channel_id=1, source_target_pairs={{8,0},{16,8},{24,16},{9,1},{17,9},{25,17},{10,2},{18,10},{26,18},{... | collective-permute-start | bytes 4718600 | tf_op jit(solution)/shard_map/while/body/eval_jaxpr/ppermute | solution.py:18
  909.6 463.1 %copy-start.36 = (f32[2,2304]{1,0:T(2,128)S(1)}, f32[2,2304]{1,0:T(2,128)}, u32[]{:S(2)}) copy-start(f32[2,2304]{1,0:T(2,128)} %scatter.34) | copy-start | bytes 55300 | tf_op jit(solution)/shard_map/while
  909.6 463.1 %copy-start.66 = (s32[2]{0:T(128)S(1)}, s32[2]{0:T(128)}, u32[]{:S(2)}) copy-start(s32[2]{0:T(128)} %copy-done.65) | copy-start | bytes 28 | tf_op jit(solution)/shard_map/while
  1411.7 67.6 %copy-start.46 = (f32[1024]{0:T(1024)S(1)}, f32[1024]{0:T(1024)}, u32[]{:S(2)}) copy-start(f32[1024]{0:T(1024)} %copy-done.45) | copy-start | bytes 12292 | tf_op jit(solution)/shard_map/while/body/eval_jaxpr/cond
  1411.7 67.6 %copy-start.52 = (f32[768]{0:T(1024)S(1)}, f32[768]{0:T(1024)}, u32[]{:S(2)}) copy-start(f32[768]{0:T(1024)} %get-tuple-element.1276) | copy-start | bytes 9220 | tf_op jit(solution)/shard_map/while/body/eval_jaxpr/cond
  1709.8 35.2 %collective-permute-start = (bf16[1024,768]{1,0:T(8,128)(2,1)}, bf16[1024,768]{1,0:T(8,128)(2,1)}, u32[]{:S(2)}, u32[]{:S(2)}) collective-permute-start(bf16[1024,768]{1,0:T(8,128)(2,1)} %get-tuple-element.1600), channel_id=1, source_target_pairs={{8,0},{16,8},{24,16},{9,1},{17,9},{25,17},{10,2},{18,10},{26,18},{... | collective-permute-start | bytes 4718600 | tf_op jit(solution)/shard_map/while/body/eval_jaxpr/ppermute | solution.py:18
  1784.6 67.6 %copy-start.46 = (f32[1024]{0:T(1024)S(1)}, f32[1024]{0:T(1024)}, u32[]{:S(2)}) copy-start(f32[1024]{0:T(1024)} %copy-done.45) | copy-start | bytes 12292 | tf_op jit(solution)/shard_map/while/body/eval_jaxpr/cond
  1784.6 67.6 %copy-start.52 = (f32[768]{0:T(1024)S(1)}, f32[768]{0:T(1024)}, u32[]{:S(2)}) copy-start(f32[768]{0:T(1024)} %get-tuple-element.1276) | copy-start | bytes 9220 | tf_op jit(solution)/shard_map/while/body/eval_jaxpr/cond
  2082.5 33.8 %collective-permute-start = (bf16[1024,768]{1,0:T(8,128)(2,1)}, bf16[1024,768]{1,0:T(8,128)(2,1)}, u32[]{:S(2)}, u32[]{:S(2)}) collective-permute-start(bf16[1024,768]{1,0:T(8,128)(2,1)} %get-tuple-element.1600), channel_id=1, source_target_pairs={{8,0},{16,8},{24,16},{9,1},{17,9},{25,17},{10,2},{18,10},{26,18},{... | collective-permute-start | bytes 4718600 | tf_op jit(solution)/shard_map/while/body/eval_jaxpr/ppermute | solution.py:18
  2125.3 126.2 %reduce-scatter.6.cloned.1.call-start = ((), (), s32[]{:S(2)}) async-start(), calls=%async_computation.5 | async-start | bytes 3932160 | tf_op jit(solution)/shard_map/reduce_scatter | solution.py:356
  2129.4 169.4 %reduce-scatter.14.cloned.1.call-start = ((), (), s32[]{:S(2)}) async-start(), calls=%async_computation.9 | async-start | bytes 5308416 | tf_op jit(solution)/shard_map/reduce_scatter | solution.py:351
  2132.6 74.9 %collective-permute-start.3 = (bf16[1536,768]{1,0:T(8,128)(2,1)S(1)}, bf16[1536,768]{1,0:T(8,128)(2,1)S(1)}, u32[]{:S(2)}, u32[]{:S(2)}) collective-permute-start(bf16[1536,768]{1,0:T(8,128)(2,1)S(1)} %select_convert_fusion.2), channel_id=1, source_target_pairs={{8,0},{16,8},{24,16},{9,1},{17,9},{25,17},{10,2},{18,10},{26,18},{... | collective-permute-start | bytes 7077896 | tf_op jit(solution)/shard_map/ppermute | solution.py:18
  2212.8 164.3 %reduce-scatter.10.cloned.1.call-start = ((), (), s32[]{:S(2)}) async-start(), calls=%async_computation.7 | async-start | bytes 7962624 | tf_op jit(solution)/shard_map/reduce_scatter | solution.py:348
  2218.6 259.1 %reduce-scatter.12.cloned.1.call-start = ((), (), s32[]{:S(2)}) async-start(), calls=%async_computation.8 | async-start | bytes 10616832 | tf_op jit(solution)/shard_map/reduce_scatter | solution.py:350
  2219.2 258.5 %copy-start.1 = (bf16[1,768,2304]{2,1,0:T(8,128)(2,1)S(1)}, bf16[1,768,2304]{2,1,0:T(8,128)(2,1)}, u32[]{:S(2)}) copy-start(bf16[1,768,2304]{2,1,0:T(8,128)(2,1)} %param.36) | copy-start | bytes 10616836
  (173 other events, 1162.7 us)
Sparse Core Ops, SparseCore 0:
  2125.4 67.0 reduce-scatter.7
  2196.1 44.7 reduce-scatter.5
  2243.8 54.9 reduce-scatter.13
  2301.5 75.5 reduce-scatter.9
  2379.8 97.8 reduce-scatter.11
where the time goes:
time: 2510 us; the launch traced here: 2480 us
  waiting for transfers between devices  960 us (38%)
  other arithmetic  525 us (21%)
  matrix products  481 us (19%)
  local copies, waits for them, and re-layouts  254 us (10%)
  starting transfers between devices  189 us (8%)
  loops' own time  34.6 us (1%)
  blocking collectives  25.9 us (1%)
    ppermute x12, waiting for transfers between devices, shifted(): return lax.ppermute(value, axis, pairs)  733 us
    ppermute x12, starting transfers between devices, shifted(): return lax.ppermute(value, axis, pairs)  189 us
    dot_general x12, matrix products, attend_block(): jnp.einsum('qhd,khd->hqk', query_block, keys_rot, preferred_element_type=...  121 us
    sub x4, other arithmetic, attend_block(): exp_scores = jnp.exp(scores - largest)  116 us
    reduce_scatter x1, waiting for transfers between devices, local(): lax.psum_scatter(first_grad, 'dp', scatter_dimension=0, tiled=True)  101 us
    convert_element_type x4, other arithmetic, attend_block(): score_grad = (weights_soft * (prob_grad - row_terms)).astype(jnp.bfloat16)  86.2 us
    dot_general x8, matrix products, attend_block(): jnp.einsum('hqk,khd->qhd', weights_soft, values, preferred_element_type=j...  86 us
    reduce_scatter x1, waiting for transfers between devices, local(): lax.psum_scatter(mod_w_grad, 'dp', scatter_dimension=0, tiled=True)  78.4 us
  transfers between devices with their start and end apart: 17, of which 14 were waited for; matrix products, arithmetic and copies ran while one was open for 8% of the time, Pallas kernels for 0%

commit v1 on v0

v1 whole, which is shorter than its diff:
```python
import functools
import math

import jax
import jax.numpy as jnp
import numpy as np
from jax import lax
from jax.experimental import pallas as pl
from jax.experimental.pallas import tpu as pltpu
from jax.sharding import PartitionSpec as P

D = 768
HEADS = 12
HEAD_DIM = 64
FF = 3072
SEQ_LEN = 1024
BLK = 256
HALF = SEQ_LEN // 2
MB = 4
XS, QS, AT, BR, NM, GB, DQ = range(7)
VLIM = 56 << 20
bf16, f32, i32 = jnp.bfloat16, jnp.float32, jnp.int32


def dot(a, b):
    return lax.dot_general(a, b, (((1,), (0,)), ((), ())), preferred_element_type=f32)


def dot_nt(a, b):
    return lax.dot_general(a, b, (((1,), (1,)), ((), ())), preferred_element_type=f32)


def dot_tn(a, b):
    return lax.dot_general(a, b, (((0,), (0,)), ((), ())), preferred_element_type=f32)


def block_rows(b):
    return pl.ds(pl.multiple_of(b * BLK, BLK), BLK)


def lanes(p):
    return pl.ds(pl.multiple_of(p * 128, 128), 128)


def norm_parts(x):
    center = x - jnp.mean(x, axis=-1, keepdims=True)
    rstd = lax.rsqrt(jnp.mean(center * center, axis=-1, keepdims=True) + 1e-06)
    return center * rstd, rstd


def norm_back(d_normed, n, rstd, scl):
    dn = d_normed * scl
    return (
        dn - jnp.mean(dn, axis=-1, keepdims=True) - n * jnp.mean(dn * n, axis=-1, keepdims=True)
    ) * rstd


def turn(v, cosine, sine):
    lane = lax.broadcasted_iota(i32, v.shape, 1)
    partner = jnp.where(lane % 64 < 32, pltpu.roll(v, 96, 1), pltpu.roll(v, 32, 1))
    return v * cosine + partner * sine


def live_column(rows, c, length, first=0):
    r = lax.broadcasted_iota(i32, (rows, 1), 0) + first
    position = r + BLK * c + jnp.where(r >= BLK, BLK, 0)
    return position < length


def counts(length, c):
    nk = lax.shift_right_logical(length + (BLK - 1), 8)
    return nk, lax.shift_right_logical(nk - c + 1, 1)


class Copies:
    def __init__(self, sems):
        self.sems, self.started = sems, []

    def add(self, src, dst):
        copy = pltpu.make_async_copy(src, dst, self.sems.at[len(self.started)])
        copy.start()
        self.started.append(copy)

    def wait(self):
        for copy in self.started:
            copy.wait()


def att_f_kernel(sc, tt, hop_own, hop_oth, own_x, rcv_x, w, cos, sin, mod, st_i, kv_i, lse_i,
                 out, st, kv, lse,
                 xv, nv, wv, kvv, vv, qv, av, bv, ov, lv, cv, sv, sem, osem):
    role = sc[0]
    mb = tt[role]

    @pl.when(mb >= 0)
    def _():
        c, length, idx = sc[1], sc[2 + mb], sc[6 + mb]
        nk, ns = counts(length, c)
        mine = lax.rem(mb, 2) == c

        @pl.when((role == 0) & mine)
        def _():
            pltpu.make_async_copy(own_x.at[idx], xv, sem.at[0]).start()

        @pl.when((role == 0) & jnp.logical_not(mine))
        def _():
            pltpu.make_async_copy(rcv_x.at[idx], xv, sem.at[0]).start()

        @pl.when(role != 0)
        def _():
            for j in range(2):
                rows = pl.ds(j * BLK, BLK)
                pltpu.make_async_copy(
                    hop_own.at[rows], xv.at[block_rows(c + 2 * j)], sem.at[0]
                ).start()
                pltpu.make_async_copy(
                    hop_oth.at[rows], xv.at[block_rows(1 - c + 2 * j)], sem.at[0]
                ).start()

        wcopies = []
        for part in (1, 2, 0, 3):
            cols = pl.ds(part * D, D)
            copy = pltpu.make_async_copy(w.at[:, cols], wv.at[:, cols], sem.at[1 + part])
            copy.start()
            wcopies.append(copy)
        tables = [
            pltpu.make_async_copy(cos, cv, sem.at[5]),
            pltpu.make_async_copy(sin, sv, sem.at[6]),
        ]
        for copy in tables:
            copy.start()
        off, scl, gat = mod[mb, 0:1, :], 1.0 + mod[mb, 1:2, :], mod[mb, 2:3, :]
        pltpu.make_async_copy(own_x.at[0], xv, sem.at[0]).wait()

        def norm_block(b, carry):
            rows = block_rows(b)
            n, _ = norm_parts(xv[rows, :].astype(f32))
            nv[rows, :] = (n * scl + off).astype(bf16)
            return carry

        lax.fori_loop(0, nk, norm_block, 0)
        for copy in tables:
            copy.wait()
        wcopies[0].wait()
        wcopies[1].wait()

        def kv_block(b, carry):
            rows = block_rows(b)
            n = nv[rows, :]
            cosine, sine = cv[rows, :], sv[rows, :]
            kk = dot(n, wv[:, D : 2 * D])
            for p in range(6):
                kvv[rows, p * 128 : (p + 1) * 128] = turn(
                    kk[:, p * 128 : (p + 1) * 128], cosine, sine
                ).astype(bf16)
            vv[rows, :] = dot(n, wv[:, 2 * D : 3 * D]).astype(bf16)
            return carry

        lax.fori_loop(0, nk, kv_block, 0)
        wcopies[2].wait()

        def q_block(j, carry):
            nat = block_rows(c + 2 * j)
            rows = block_rows(j)
            cosine, sine = cv[nat, :] * 0.125, sv[nat, :] * 0.125
            qq = dot(nv[nat, :], wv[:, 0:D])
            for p in range(6):
                qv[rows, p * 128 : (p + 1) * 128] = turn(
                    qq[:, p * 128 : (p + 1) * 128], cosine, sine
                ).astype(bf16)
            return carry

        lax.fori_loop(0, ns, q_block, 0)
        sends = Copies(osem)
        sends.add(qv, st.at[QS, mb])
        sends.add(kvv, kv.at[0, mb])
        sends.add(vv, kv.at[1, mb])
        for j in range(2):
            sends.add(xv.at[block_rows(c + 2 * j)], st.at[XS, mb, pl.ds(j * BLK, BLK)])

        lane = lax.broadcasted_iota(i32, (BLK, 128), 1)

        def attend(keys, masked):
            if masked:
                position = lax.broadcasted_iota(i32, (1, keys), 1)
                bias = jnp.where(position < length, 0.0, -1e30).astype(f32)

            def slot(j, carry):
                rows = block_rows(j)
                lv[rows, :] = jnp.zeros((BLK, 128), f32)

                def pair(hp, carry):
                    ls = lanes(hp)
                    k2, v2, q2 = kvv[0:keys, ls], vv[0:keys, ls], qv[rows, ls]
                    outs, stats = [], lv[rows, :]
                    for a in range(2):
                        s = dot_nt(jnp.where((lane < 64) == (a == 0), q2, jnp.zeros_like(q2)), k2)
                        if masked:
                            s = s + bias
                        m = jnp.max(s, axis=1, keepdims=True)
                        e = jnp.exp(s - m)
                        total = jnp.sum(e, axis=1, keepdims=True)
                        outs.append(dot(e.astype(bf16), v2) / total)
                        stats = jnp.where(lane == 2 * hp + a, m + jnp.log(total), stats)
                    av[rows, ls] = jnp.where(lane < 64, outs[0], outs[1]).astype(bf16)
                    lv[rows, :] = stats
                    return carry

                return lax.fori_loop(0, HEADS // 2, pair, carry)

            lax.fori_loop(0, ns, slot, 0)

        pl.when(length == SEQ_LEN)(lambda: attend(SEQ_LEN, False))
        for blocks in range(1, 5):
            pl.when((nk == blocks) & (length < SEQ_LEN))(
                functools.partial(attend, blocks * BLK, True)
            )
        wcopies[3].wait()

        def out_block(j, carry):
            rows = block_rows(j)
            branch = dot(av[rows, :], wv[:, 3 * D : 4 * D])
            live = live_column(BLK, c, length, j * BLK)
            x = xv[block_rows(c + 2 * j), :].astype(f32)
            ov[rows, :] = (x + jnp.where(live, gat * branch, 0.0)).astype(bf16)
            bv[rows, :] = branch.astype(bf16)
            return carry

        lax.fori_loop(0, ns, out_block, 0)
        sends.add(ov, out)
        sends.add(av, st.at[AT, mb])
        sends.add(bv, st.at[BR, mb])
        sends.add(lv, lse.at[mb])
        sends.wait()


def load_ff_weights(c, w1, prt_own, prt_oth, rows2, w1v, w2v, sem):
    half = FF // 4
    ups = []
    for part in range(4):
        cols = pl.ds(part * D, D)
        ups.append(pltpu.make_async_copy(w1.at[:, cols], w1v.at[:, cols], sem.at[part]))
        ups[-1].start()
        if part == 0:
            mine = pl.ds(pl.multiple_of(c * half, half), half)
            other = pl.ds(pl.multiple_of((1 - c) * half, half), half)
            pltpu.make_async_copy(prt_own, w2v.at[mine], sem.at[4]).start()
            pltpu.make_async_copy(prt_oth, w2v.at[other], sem.at[4]).start()
    tail = pl.ds(2 * half, 2 * half)
    second = pltpu.make_async_copy(rows2, w2v.at[tail], sem.at[5])
    second.start()

    def wait(part):
        ups[part].wait()
        if part == 0:
            pltpu.make_async_copy(rows2, w2v.at[tail], sem.at[4]).wait()
        if part == 2:
            second.wait()

    return wait


def gelu_parts(u):
    u2 = u * u
    t = jnp.tanh(0.7978845608028654 * (u * (1.0 + 0.044715 * u2)))
    return t, u2


def ff_f_kernel(sc, tt, hop, w1, prt_own, prt_oth, rows2, mod, st_i,
                out, st, xv, nv, w1v, w2v, ov, bv, sem, osem):
    role = sc[0]
    mb = tt[role]

    @pl.when(mb >= 0)
    def _():
        c, length = sc[1], sc[2 + mb]
        _, ns = counts(length, c)
        load = pltpu.make_async_copy(hop, xv, sem.at[6])
        load.start()
        wait = load_ff_weights(c, w1, prt_own, prt_oth, rows2, w1v, w2v, sem)
        off, scl, gat = mod[mb, 0:1, :], 1.0 + mod[mb, 1:2, :], mod[mb, 2:3, :]
        load.wait()
        sends = Copies(osem)
        sends.add(xv, st.at[XS, mb])

        def norm_block(j, carry):
            rows = block_rows(j)
            n, _ = norm_parts(xv[rows, :].astype(f32))
            nv[rows, :] = (n * scl + off).astype(bf16)
            return carry

        lax.fori_loop(0, ns, norm_block, 0)
        for part in range(4):
            wait(part)

        def body(rows):
            acc = jnp.zeros((rows, D), f32)
            for part in range(4):
                u = dot(nv[0:rows, :], w1v[:, part * D : (part + 1) * D])
                t, _ = gelu_parts(u)
                act = (0.5 * u * (1.0 + t)).astype(bf16)
                acc = acc + dot(act, w2v[part * D : (part + 1) * D, :])
            live = live_column(rows, c, length)
            x = xv[0:rows, :].astype(f32)
            ov[0:rows, :] = (x + jnp.where(live, gat * acc, 0.0)).astype(bf16)
            bv[0:rows, :] = acc.astype(bf16)

        pl.when(ns == 2)(lambda: body(HALF))
        pl.when(ns == 1)(lambda: body(BLK))
        sends.add(ov, out)
        sends.add(bv, st.at[BR, mb])
        sends.wait()


def ff_b_kernel(sc, tt, hop, own_c, rcv_c, w1, prt_own, prt_oth, rows2, mod, st_i, y_i, act_i, dm_i,
                out, st, y, act, dm,
                xv, gv, brv, nv, gbv, w1v, w2v, duv, actv, ov, dmv, sem, osem):
    role = sc[0]
    mb = tt[role]

    @pl.when(mb >= 0)
    def _():
        c, length, idx = sc[1], sc[2 + mb], sc[6 + mb]
        _, ns = counts(length, c)
        mine = lax.rem(mb, 2) == c

        @pl.when(role == 1)
        def _():
            pltpu.make_async_copy(hop, gv, sem.at[6]).start()

        for pick, source in ((mine, own_c), (jnp.logical_not(mine), rcv_c)):

            @pl.when((role == 3) & pick)
            def _():
                for j in range(2):
                    pltpu.make_async_copy(
                        source.at[idx, block_rows(c + 2 * j)], gv.at[pl.ds(j * BLK, BLK)], sem.at[6]
                    ).start()

        loads = [
            pltpu.make_async_copy(st.at[XS, mb], xv, sem.at[7]),
            pltpu.make_async_copy(st.at[BR, mb], brv, sem.at[8]),
        ]
        for copy in loads:
            copy.start()
        wait = load_ff_weights(c, w1, prt_own, prt_oth, rows2, w1v, w2v, sem)
        off, scl, gat = mod[mb, 0:1, :], 1.0 + mod[mb, 1:2, :], mod[mb, 2:3, :]
        dmv[...] = jnp.zeros((8, D), f32)
        pltpu.make_async_copy(hop, gv, sem.at[6]).wait()
        for copy in loads:
            copy.wait()

        def norm_block(j, carry):
            rows = block_rows(j)
            n, _ = norm_parts(xv[rows, :].astype(f32))
            nv[rows, :] = (n * scl + off).astype(bf16)
            live = live_column(BLK, c, length, j * BLK)
            gl = jnp.where(live, gv[rows, :].astype(f32), 0.0)
            gbv[rows, :] = (gl * gat).astype(bf16)
            dmv[2:3, :] += jnp.sum(gl * brv[rows, :].astype(f32), axis=0, keepdims=True)
            return carry

        lax.fori_loop(0, ns, norm_block, 0)
        sends = Copies(osem)
        sends.add(nv, st.at[NM, mb])
        sends.add(gbv, st.at[GB, mb])
        for part in range(4):
            wait(part)

        def body(rows):
            acc = jnp.zeros((rows, D), f32)
            for part in range(4):
                cols = slice(part * D, (part + 1) * D)
                u = dot(nv[0:rows, :], w1v[:, cols])
                t, u2 = gelu_parts(u)
                half = 0.5 * (1.0 + t)
                actv[0:rows, cols] = (u * half).astype(bf16)
                slope = half + 0.5 * u * (1.0 - t * t) * (
                    0.7978845608028654 * (1.0 + 3 * 0.044715 * u2)
                )
                du = (dot_nt(gbv[0:rows, :], w2v[cols, :]) * slope).astype(bf16)
                duv[0:rows, cols] = du
                acc = acc + dot_nt(du, w1v[:, cols])
            n, rstd = norm_parts(xv[0:rows, :].astype(f32))
            dmv[0:1, :] = jnp.sum(acc, axis=0, keepdims=True)
            dmv[1:2, :] = jnp.sum(acc * n, axis=0, keepdims=True)
            ov[0:rows, :] = (
                gv[0:rows, :].astype(f32) + norm_back(acc, n, rstd, scl)
            ).astype(bf16)

        pl.when(ns == 2)(lambda: body(HALF))
        pl.when(ns == 1)(lambda: body(BLK))
        sends.add(ov, out)
        sends.add(duv, y.at[mb])
        sends.add(actv, act.at[mb])
        sends.add(dmv, dm.at[mb])
        sends.wait()


def att_b1_kernel(sc, tt, hop0, hop2, w, mod, kv, lse, st_i, y_i,
                  own, snd, st, y,
                  gv, atv, qv, kvv, vv, wo, lv, gbv, dov, dqv, dkt, dvt, sem, osem):
    role = sc[0]
    mb = tt[role]

    @pl.when(mb >= 0)
    def _():
        c, length = sc[1], sc[2 + mb]
        nk, ns = counts(length, c)
        for who, hop in ((0, hop0), (2, hop2)):
            pl.when(role == who)(lambda: pltpu.make_async_copy(hop, gv, sem.at[0]).start())
        loads = [
            pltpu.make_async_copy(w.at[:, pl.ds(3 * D, D)], wo, sem.at[1]),
            pltpu.make_async_copy(st.at[QS, mb], qv, sem.at[2]),
            pltpu.make_async_copy(kv.at[0, mb], kvv, sem.at[3]),
            pltpu.make_async_copy(kv.at[1, mb], vv, sem.at[4]),
            pltpu.make_async_copy(st.at[AT, mb], atv, sem.at[5]),
            pltpu.make_async_copy(lse.at[mb], lv, sem.at[6]),
        ]
        for copy in loads:
            copy.start()
        gat = mod[mb, 2:3, :]
        pltpu.make_async_copy(hop0, gv, sem.at[0]).wait()
        loads[0].wait()

        def grad_block(j, carry):
            rows = block_rows(j)
            live = live_column(BLK, c, length, j * BLK)
            gb = jnp.where(live, gv[rows, :].astype(f32) * gat, 0.0).astype(bf16)
            gbv[rows, :] = gb
            dov[rows, :] = dot_nt(gb, wo[...]).astype(bf16)
            return carry

        lax.fori_loop(0, ns, grad_block, 0)
        sends = Copies(osem)
        sends.add(gbv, y.at[mb, :, pl.ds(3 * D, D)])
        for copy in loads[1:]:
            copy.wait()

        def attend(rows, keys, masked):
            lane = lax.broadcasted_iota(i32, (rows, 128), 1)
            if masked:
                position = lax.broadcasted_iota(i32, (1, keys), 1)
                bias = jnp.where(position < length, 0.0, -1e30).astype(f32)

            def pair(hp, carry):
                ls = lanes(hp)
                k2, v2 = kvv[0:keys, ls], vv[0:keys, ls]
                q2, do2 = qv[0:rows, ls], dov[0:rows, ls]
                q2t, do2t = q2.T, do2.T
                both = do2.astype(f32) * atv[0:rows, ls].astype(f32)
                stats = lv[0:rows, :]
                dqs = []
                for a in range(2):
                    head = (lane < 64) == (a == 0)
                    zero = jnp.zeros_like(q2)
                    s = dot_nt(jnp.where(head, q2, zero), k2)
                    if masked:
                        s = s + bias
                    base = jnp.sum(jnp.where(lane == 2 * hp + a, stats, 0.0), axis=1, keepdims=True)
                    p = jnp.exp(s - base)
                    dp = dot_nt(jnp.where(head, do2, zero), v2)
                    delta = jnp.sum(jnp.where(head, both, 0.0), axis=1, keepdims=True)
                    ds = (p * (dp - delta)).astype(bf16)
                    dqs.append(dot(ds, k2))
                    at = pl.ds(pl.multiple_of(hp * 128 + a * 64, 64), 64)
                    dkt[at, 0:keys] = dot(q2t[a * 64 : (a + 1) * 64, :], ds).astype(bf16)
                    dvt[at, 0:keys] = dot(do2t[a * 64 : (a + 1) * 64, :], p.astype(bf16)).astype(
                        bf16
                    )
                dqv[0:rows, ls] = jnp.where(lane < 64, dqs[0], dqs[1]).astype(bf16)
                return carry

            lax.fori_loop(0, HEADS // 2, pair, 0)

        pl.when(length == SEQ_LEN)(lambda: attend(HALF, SEQ_LEN, False))
        for slots, blocks in ((1, 1), (1, 2), (1, 3), (2, 3), (2, 4)):
            pl.when((ns == slots) & (nk == blocks) & (length < SEQ_LEN))(
                functools.partial(attend, slots * BLK, blocks * BLK, True)
            )

        @pl.when(ns == 0)
        def _():
            dkt[:, 0:BLK] = jnp.zeros((D, BLK), bf16)
            dvt[:, 0:BLK] = jnp.zeros((D, BLK), bf16)

        sends.add(dqv, st.at[DQ, mb])
        for part, grad in enumerate((dkt, dvt)):
            for j in range(2):
                cols = pl.ds(j * BLK, BLK)
                sends.add(grad.at[:, block_rows(c + 2 * j)], own.at[part, :, cols])
                sends.add(grad.at[:, block_rows(1 - c + 2 * j)], snd.at[part, :, cols])
        sends.wait()


def att_b2_kernel(sc, tt, hop0, hop2, own, rcv, w, cos, sin, mod, st_i, y_i, dm_i,
                  out, st, y, dm,
                  gv, xv, brv, dqv, ownv, rcvv, wv, cv, sv, nv, dpv, ov, dmv, sem, osem):
    role = sc[0]
    mb = tt[role]

    @pl.when(mb >= 0)
    def _():
        c, length = sc[1], sc[2 + mb]
        _, ns = counts(length, c)
        for who, hop in ((0, hop0), (2, hop2)):
            pl.when(role == who)(lambda: pltpu.make_async_copy(hop, gv, sem.at[0]).start())
        loads = [
            pltpu.make_async_copy(own, ownv, sem.at[1]),
            pltpu.make_async_copy(rcv, rcvv, sem.at[2]),
            pltpu.make_async_copy(st.at[DQ, mb], dqv, sem.at[3]),
            pltpu.make_async_copy(st.at[XS, mb], xv, sem.at[4]),
            pltpu.make_async_copy(st.at[BR, mb], brv, sem.at[5]),
            pltpu.make_async_copy(cos, cv, sem.at[6]),
            pltpu.make_async_copy(sin, sv, sem.at[7]),
            pltpu.make_async_copy(w.at[:, pl.ds(0, 3 * D)], wv, sem.at[8]),
        ]
        for copy in loads:
            copy.start()
        off, scl = mod[mb, 0:1, :], 1.0 + mod[mb, 1:2, :]
        dmv[...] = jnp.zeros((8, D), f32)
        pltpu.make_async_copy(hop0, gv, sem.at[0]).wait()
        for copy in loads[:-1]:
            copy.wait()

        def first(j, carry):
            rows, nat = block_rows(j), block_rows(c + 2 * j)
            cosine, sine = cv[nat, :], -sv[nat, :]
            for p in range(6):
                ls = slice(p * 128, (p + 1) * 128)
                dpv[rows, ls] = (turn(dqv[rows, ls].astype(f32), cosine, sine) * 0.125).astype(bf16)
                for part in range(2):
                    total = ownv[part, ls, rows].astype(f32) + rcvv[part, ls, rows].astype(f32)
                    grad = total.T
                    if part == 0:
                        grad = turn(grad.astype(bf16).astype(f32), cosine, sine)
                    dpv[rows, (part + 1) * D + p * 128 : (part + 1) * D + (p + 1) * 128] = (
                        grad.astype(bf16)
                    )
            return carry

        lax.fori_loop(0, ns, first, 0)
        sends = Copies(osem)
        sends.add(dpv, y.at[mb, :, pl.ds(0, 3 * D)])
        loads[-1].wait()

        def second(j, carry):
            rows = block_rows(j)
            acc = dot_nt(dpv[rows, :], wv[...])
            n, rstd = norm_parts(xv[rows, :].astype(f32))
            nv[rows, :] = (n * scl + off).astype(bf16)
            g = gv[rows, :].astype(f32)
            live = live_column(BLK, c, length, j * BLK)
            gl = jnp.where(live, g, 0.0)
            dmv[0:1, :] += jnp.sum(acc, axis=0, keepdims=True)
            dmv[1:2, :] += jnp.sum(acc * n, axis=0, keepdims=True)
            dmv[2:3, :] += jnp.sum(gl * brv[rows, :].astype(f32), axis=0, keepdims=True)
            ov[rows, :] = (g + norm_back(acc, n, rstd, scl)).astype(bf16)
            return carry

        lax.fori_loop(0, ns, second, 0)
        sends.add(ov, out)
        sends.add(nv, st.at[NM, mb])
        sends.add(dmv, dm.at[mb])
        sends.wait()


def first_grad_kernel(sc, x1, x2, y, out, acc):
    c = sc[1]
    acc[...] = jnp.zeros((D, D), f32)
    second = (lax.rem(sc[0], 2) == 0) & (pl.program_id(0) == 3)
    for mb in range(MB):
        _, ns = counts(sc[2 + mb], c)
        for slots in (1, 2):
            rows = slots * BLK

            @pl.when((ns == slots) & second)
            def _():
                acc[...] += dot_tn(x2[0, mb, 0:rows, :], y[mb, 0:rows, :])

            @pl.when((ns == slots) & jnp.logical_not(second))
            def _():
                acc[...] += dot_tn(x1[0, mb, 0:rows, :], y[mb, 0:rows, :])

    out[...] = acc[...].astype(bf16)


def down_grad_kernel(sc, act, gb, out, acc):
    c = sc[1]

    @pl.when(lax.rem(sc[0], 2) == 1)
    def _():
        acc[...] = jnp.zeros((D, D), f32)
        for mb in range(MB):
            _, ns = counts(sc[2 + mb], c)
            for slots in (1, 2):
                rows = slots * BLK

                @pl.when(ns == slots)
                def _():
                    acc[...] += dot_tn(act[mb, 0:rows, :], gb[0, mb, 0:rows, :])

        out[...] = acc[...].astype(bf16)


ANY = pl.BlockSpec(memory_space=pl.ANY)
VMEM = pl.BlockSpec(memory_space=pltpu.VMEM)


def shape(dims, dtype=bf16):
    return jax.ShapeDtypeStruct(dims, dtype)


ROWS = shape((HALF, D))
ST = shape((7, MB, HALF, D))
KV = shape((2, MB, SEQ_LEN, D))
LSE = shape((MB, HALF, 128), f32)
YS = shape((MB, HALF, FF))
DM = shape((MB, 8, D), f32)
DKV = shape((2, D, HALF))


def vm(dims, dtype=bf16):
    return pltpu.VMEM(dims, dtype)


HV, FV = vm((HALF, D)), vm((SEQ_LEN, D))


def call(kernel, scalars, operands, vmem_at, outs, aliases, scratch, sems, name):
    specs = [VMEM if i in vmem_at else ANY for i in range(len(operands))]
    return pl.pallas_call(
        kernel,
        grid_spec=pltpu.PrefetchScalarGridSpec(
            num_scalar_prefetch=2,
            grid=(1,),
            in_specs=specs,
            out_specs=[ANY] * len(outs),
            scratch_shapes=list(scratch)
            + [pltpu.SemaphoreType.DMA((9,)), pltpu.SemaphoreType.DMA((sems,))],
        ),
        out_shape=list(outs),
        input_output_aliases={i + 2: o for i, o in aliases.items()},
        compiler_params=pltpu.CompilerParams(vmem_limit_bytes=VLIM),
        name=name,
    )(*scalars, *operands)


def allocate(outs):
    return pl.pallas_call(
        lambda *refs: None,
        out_shape=list(outs),
        out_specs=[ANY] * len(outs),
        name="allocate",
    )()


def time_cond(steps):
    half_width = D // 2
    frequency = jnp.exp(
        jnp.arange(half_width, dtype=f32) * (-math.log(10000.0) / half_width)
    )
    angles = steps.astype(f32)[:, None] * frequency[None, :]
    return jax.nn.silu(jnp.concatenate([jnp.cos(angles), jnp.sin(angles)], axis=1))


def rope_tables():
    inverse = np.exp(np.arange(32, dtype=np.float32) * np.float32(-math.log(10000.0) / 32))
    angles = np.arange(SEQ_LEN, dtype=np.float32)[:, None] * inverse[None, :]
    cosine, sine = np.cos(angles), np.sin(angles)
    return (
        np.concatenate([cosine] * 4, axis=1).astype(np.float32),
        np.concatenate([-sine, sine, -sine, sine], axis=1).astype(np.float32),
    )


def local(block_input, cotangent, lengths, steps, mod_weight, mod_bias, first_weight, down_rows):
    ndp = lax.axis_size("dp")
    seg, dp = lax.axis_index("segment"), lax.axis_index("dp")
    core = dp % 2
    w, rows2 = first_weight[0], down_rows[0]

    def swap(value):
        return lax.ppermute(value, "dp", [(i, i ^ 1) for i in range(ndp)])

    def hop(value, pairs):
        return lax.ppermute(value, "segment", pairs)

    info = jnp.stack([lengths, steps])
    other_info = swap(info)
    other_x = swap(block_input)
    half_rows = lax.dynamic_slice_in_dim(rows2, core * (FF // 4), FF // 4, axis=0)
    prt_own = hop(half_rows, [(0, 1), (2, 3)])
    prt_oth = swap(prt_own)
    other_c = swap(cotangent)

    info0 = jnp.where(core == 0, info, other_info)
    info1 = jnp.where(core == 0, other_info, info)
    full0 = (info0[0, 1] > info0[0, 0]).astype(i32)
    full1 = (info1[0, 1] > info1[0, 0]).astype(i32)
    places = jnp.stack([full0, full1, 1 - full0, 1 - full1])
    chip = jnp.stack([info0[:, full0], info1[:, full1], info0[:, 1 - full0], info1[:, 1 - full1]])
    sc = jnp.concatenate([jnp.stack([seg, core]), chip[:, 0], places, jnp.zeros((6,), i32)]).astype(i32)
    conditions = time_cond(chip[:, 1]).astype(bf16)
    modulation = jnp.dot(conditions, mod_weight[0], preferred_element_type=f32)
    modulation = modulation + mod_bias[0].astype(f32)
    mod = jnp.pad(modulation.reshape(MB, 3, D), ((0, 0), (0, 5), (0, 0)))
    cos, sin = (jnp.asarray(t) for t in rope_tables())

    st, kv, lse, y, act, dm, blank = allocate([ST, KV, LSE, YS, YS, DM, ROWS])

    def table(turns):
        return np.array([t if 0 <= t < MB else -1 for t in turns], np.int32)

    def att_f(turns, own, oth, st, kv, lse):
        return call(
            att_f_kernel,
            (sc, table(turns)),
            (own, oth, block_input, other_x, w, cos, sin, mod, st, kv, lse),
            (7,),
            (ROWS, ST, KV, LSE),
            {8: 1, 9: 2, 10: 3},
            (FV, FV, vm((D, FF)), FV, FV, HV, HV, HV, HV, vm((HALF, 128), f32),
             vm((SEQ_LEN, 128), f32), vm((SEQ_LEN, 128), f32)),
            9,
            "attention_forward",
        )

    def ff_f(turns, x, st):
        return call(
            ff_f_kernel,
            (sc, table(turns)),
            (x, w, prt_own, prt_oth, rows2, mod, st),
            (5,),
            (ROWS, ST),
            {6: 1},
            (HV, HV, vm((D, FF)), vm((FF, D)), HV, HV),
            3,
            "feedforward_forward",
        )

    def ff_b(turns, g, st, y, act, dm):
        return call(
            ff_b_kernel,
            (sc, table(turns)),
            (g, cotangent, other_c, w, prt_own, prt_oth, rows2, mod, st, y, act, dm),
            (7,),
            (ROWS, ST, YS, YS, DM),
            {8: 1, 9: 2, 10: 3, 11: 4},
            (HV, HV, HV, HV, HV, vm((D, FF)), vm((FF, D)), vm((HALF, FF)), vm((HALF, FF)), HV,
             vm((8, D), f32)),
            6,
            "feedforward_backward",
        )

    def att_b1(turns, g0, g2, st, y):
        return call(
            att_b1_kernel,
            (sc, table(turns)),
            (g0, g2, w, mod, kv, lse, st, y),
            (3,),
            (DKV, DKV, ST, YS),
            {6: 2, 7: 3},
            (HV, HV, HV, FV, FV, vm((D, D)), vm((HALF, 128), f32), HV, HV, HV,
             vm((D, SEQ_LEN)), vm((D, SEQ_LEN))),
            10,
            "attention_backward",
        )

    def att_b2(turns, g0, g2, own, rcv, st, y, dm):
        return call(
            att_b2_kernel,
            (sc, table(turns)),
            (g0, g2, own, rcv, w, cos, sin, mod, st, y, dm),
            (7,),
            (ROWS, ST, YS, DM),
            {8: 1, 9: 2, 10: 3},
            (HV, HV, HV, HV, vm((2, D, HALF)), vm((2, D, HALF)), vm((D, 3 * D)),
             vm((SEQ_LEN, 128), f32), vm((SEQ_LEN, 128), f32), HV, vm((HALF, 3 * D)), HV,
             vm((8, D), f32)),
            4,
            "projection_backward",
        )

    into_ff, into_att = blank, blank
    finals, returned = [], []
    for t in range(7):
        ff_out = att_out = None
        if t >= 1:
            turns = (-1, t - 1, -1, t - 3)
            ff_out, st = ff_f(turns, into_ff, st)
        if t <= 5:
            other = swap(into_att) if 2 <= t else blank
            att_out, st, kv, lse = att_f((t, -1, t - 2, -1), into_att, other, st, kv, lse)
        if t >= 3:
            finals.append(ff_out)
        into_att_next = hop(ff_out, [(1, 2)]) if 1 <= t <= 4 else blank
        into_ff_next = blank
        if t <= 5:
            pairs = [(0, 1)] * (t <= 3) + [(2, 3)] * (t >= 2)
            into_ff_next = hop(att_out, pairs)
        if t >= 3:
            grad, st, y, act, dm = ff_b((-1, -1, -1, t - 3), blank, st, y, act, dm)
            returned.append(hop(grad, [(3, 2)]))
        into_ff, into_att = into_ff_next, into_att_next

    into_ff, into_att = blank, blank
    inputs = []
    for u in range(6):
        if 1 <= u <= 4:
            grad, st, y, act, dm = ff_b((-1, u - 1, -1, -1), into_ff, st, y, act, dm)
        g2 = returned[u] if u < MB else blank
        turns = (u - 2, -1, u, -1)
        own, snd, st, y = att_b1(turns, into_att, g2, st, y)
        rcv = swap(snd)
        gout, st, y, dm = att_b2(turns, into_att, g2, own, rcv, st, y, dm)
        if u >= 2:
            inputs.append(gout)
        into_att = hop(grad, [(1, 0)]) if 1 <= u <= 4 else blank
        into_ff = hop(gout, [(2, 1)]) if u <= 3 else blank

    def weight_call(kernel, operands, specs, out, out_spec, name):
        return pl.pallas_call(
            kernel,
            grid_spec=pltpu.PrefetchScalarGridSpec(
                num_scalar_prefetch=1,
                grid=(4,),
                in_specs=specs,
                out_specs=out_spec,
                scratch_shapes=[vm((D, D), f32)],
            ),
            out_shape=out,
            compiler_params=pltpu.CompilerParams(vmem_limit_bytes=VLIM),
            name=name,
        )(sc, *operands)

    def kept(kind):
        return pl.BlockSpec((1, MB, HALF, D), lambda j, s: (kind, 0, 0, 0))

    wide = pl.BlockSpec((MB, HALF, D), lambda j, s: (0, 0, j))
    down_grad = weight_call(
        down_grad_kernel, (act, st), [wide, kept(GB)], shape((FF, D)),
        pl.BlockSpec((D, D), lambda j, s: (j, 0)), "down_gradient",
    )
    first_grad = weight_call(
        first_grad_kernel, (st, st, y), [kept(NM), kept(AT), wide], shape((D, FF)),
        pl.BlockSpec((D, D), lambda j, s: (0, j)), "first_gradient",
    )
    half = FF // 2
    incoming = hop(down_grad[:half], [(1, 0), (3, 2)])
    rows_grad = jnp.where(seg % 2 == 1, down_grad[half:], incoming)
    first_sum = lax.psum_scatter(first_grad, "dp", scatter_dimension=0, tiled=True)
    rows_sum = lax.psum_scatter(rows_grad, "dp", scatter_dimension=0, tiled=True)

    mod_rows = dm[:, :3, :].reshape(MB, 3 * D)
    all_rows = lax.all_gather(mod_rows, "dp", axis=0, tiled=True)
    all_steps = lax.all_gather(chip[:, 1], "dp", axis=0, tiled=True)
    all_conditions = time_cond(all_steps).astype(bf16).astype(f32)
    depth = D // ndp
    mine = lax.dynamic_slice_in_dim(all_conditions, dp * depth, depth, axis=1)
    mod_w_sum = jnp.dot(mine.T, all_rows, precision=lax.Precision.HIGHEST, preferred_element_type=f32)
    width = 3 * D // ndp
    mod_b_sum = jnp.sum(lax.dynamic_slice_in_dim(all_rows, dp * width, width, axis=1), axis=0)

    def spread(halves, source):
        halves = jnp.stack(halves)
        got = jnp.where((seg == source) & (core == source % 2),
                        lax.slice_in_dim(halves, (source // 2) * BLK, (source // 2 + 1) * BLK, axis=1),
                        jnp.zeros((MB, BLK, D), bf16))
        for target in range(4):
            if target == source:
                continue
            piece = lax.slice_in_dim(halves, (target // 2) * BLK, (target // 2 + 1) * BLK, axis=1)
            pairs = [(source * ndp + d, target * ndp + d) for d in range(ndp) if d % 2 == target % 2]
            got = got + lax.ppermute(piece, ("segment", "dp"), pairs)
        pair = got.reshape(2, 2, BLK, D)
        keep = lax.dynamic_index_in_dim(pair, core, axis=1, keepdims=False)
        give = lax.dynamic_index_in_dim(pair, 1 - core, axis=1, keepdims=False)
        both = jnp.where(core == seg % 2, keep, swap(give))
        full = jnp.where(core == 0, full0, full1)
        return jnp.where(full == 0, both, both[::-1])

    live = (seg * BLK + jnp.arange(BLK))[None, :, None] < lengths[:, None, None]
    x_part = lax.dynamic_slice_in_dim(block_input, seg * BLK, BLK, axis=1)
    c_part = lax.dynamic_slice_in_dim(cotangent, seg * BLK, BLK, axis=1)
    block_output = jnp.where(live, spread(finals, 3), x_part)
    input_grad = jnp.where(live, spread(inputs, 0), c_part).astype(f32)
    return (
        block_output,
        input_grad,
        mod_w_sum[None],
        mod_b_sum[None],
        first_sum.astype(f32)[None],
        rows_sum.astype(f32)[None],
    )


def solution(mesh):
    in_specs = (
        P("dp", None, None),
        P("dp", None, None),
        P("dp"),
        P("dp"),
        P("segment", None, None),
        P("segment", None),
        P("segment", None, None),
        P("segment", None, None),
    )
    out_specs = (
        P("dp", "segment", None),
        P("dp", "segment", None),
        P("segment", "dp", None),
        P("segment", "dp"),
        P("segment", "dp", None),
        P("segment", "dp", None),
    )
    return jax.shard_map(local, mesh=mesh, in_specs=in_specs, out_specs=out_specs, check_vma=False)
```

time: 2510 us -> 872 us (0.35)
  waiting for transfers between devices: 960 us -> 314 us
  other arithmetic: 525 us -> 26.2 us
  matrix products: 481 us -> 2.14 us
  Pallas kernels: 0 us -> 372 us
  local copies, waits for them, and re-layouts: 254 us -> 42.2 us
  starting transfers between devices: 189 us -> 54.4 us
  loops' own time: 34.6 us -> 0 us
    dot_general x54 -> x2, matrix products: 481 us -> 2.14 us  [the longest x1 1.56 us: local(): jnp.dot(mine.T, all_rows, precision=lax.Precision.HIGHEST, preferred_elem...]
    ppermute x12 -> x46, waiting for transfers between devices: 733 us -> 314 us  [the longest x24 283 us: hop(): return lax.ppermute(value, 'segment', pairs)]
    pallas_call x0 -> x35, Pallas kernels: none -> 372 us  [the longest x32 344 us: call(): pl.pallas_call(kernel, grid_spec=pltpu.PrefetchScalarGridSpec(num_scalar_...]
    ppermute x12 -> x46, starting transfers between devices: 189 us -> 54 us  [the longest x24 30.9 us: hop(): return lax.ppermute(value, 'segment', pairs)]
    convert_element_type x34 -> x3, other arithmetic: 129 us -> 3.51 us  [the longest x1 3.31 us: local(): input_grad = jnp.where(live, spread(inputs, 0), c_part).astype(f32)]
    reduce_scatter x4 -> x1, waiting for transfers between devices: 126 us -> 0.01 us  [local(): lax.psum_scatter(rows_grad, 'dp', scatter_dimension=0, tiled=True)]
    sub x4 -> x0, other arithmetic: 116 us -> none  [attend_block(): exp_scores = jnp.exp(scores - largest)]
    add x13 -> x4, other arithmetic: 122 us -> 6.27 us  [the longest x2 5.53 us: spread(): got = got + lax.ppermute(piece, ('segment', 'dp'), pairs)]
  transfers between devices with their start and end apart: 17 -> 48, of which waited for: 14 -> 17; matrix products, arithmetic and copies ran while one was open for 8% -> 4% of each run, Pallas kernels for 0% -> 27%
where the time goes in v1:
time: 872 us; the launch traced here: 857 us
  Pallas kernels  372 us (43%)
  waiting for transfers between devices  314 us (36%)
  starting transfers between devices  54.4 us (6%)
  local copies, waits for them, and re-layouts  42.2 us (5%)
  blocking collectives  26.5 us (3%)
  other arithmetic  26.2 us (3%)
  between operations  19.1 us (2%)
    pallas_call x32, Pallas kernels, call(): pl.pallas_call(kernel, grid_spec=pltpu.PrefetchScalarGridSpec(num_scalar_...  344 us
    ppermute x24, waiting for transfers between devices, hop(): return lax.ppermute(value, 'segment', pairs)  283 us
    ppermute x24, starting transfers between devices, hop(): return lax.ppermute(value, 'segment', pairs)  30.9 us
    pallas_call x2, Pallas kernels, weight_call(): pl.pallas_call(kernel, grid_spec=pltpu.PrefetchScalarGridSpec(num_scalar_...  27.3 us
    unnamed x119, local copies, waits for them, and re-layouts  25.8 us
    ppermute x16, waiting for transfers between devices, swap(): return lax.ppermute(value, 'dp', [(i, i ^ 1) for i in range(ndp)])  20.1 us
  transfers between devices with their start and end apart: 48, of which 17 were waited for; matrix products, arithmetic and copies ran while one was open for 4% of the time, Pallas kernels for 27%

profile of v1, /device:TPU:0, one launch (start us, length us, event | category | flops | bytes accessed | tf_op | source)
XLA Modules:
  0.0 856.6 jit_solution(11210355519149817688)
XLA Ops:
  26.2 14.8 %collective-permute-done.3.prt_own = bf16[768,768]{1,0:T(8,128)(2,1)} collective-permute-done((bf16[768,768]{1,0:T(8,128)(2,1)}, bf16[768,768]{1,0:T(8,128)(2,1)}, u32[]{:S(2)}, u32[]{:S(2)}) %collective-permute-start.3) | collective-permute-done | bytes 1179680 | tf_op jit(solution)/shard_map/ppermute | solution.py:687
  43.6 25.4 %attention_forward.6 = (bf16[512,768]{1,0:T(8,128)(2,1)}, bf16[7,4,512,768]{3,2,1,0:T(8,128)(2,1)}, bf16[2,4,1024,768]{3,2,1,0:T(8,128)(2,1)}, f32[4,512,128]{2,1,0:T(8,128)}) custom-call(s32[16]{0:T(128)} %concatenate.9.sc, s32[4]{0:T(128)} %constant.124.clone.tt, ...), custom_call_target="tpu_custom_call", output_to_operand_aliasing={{1}: (10, {}), {2}: (11, {}), {3}: (12, {})} | custom-call | tf_op jit(solution)/shard_map/attention_forward/pallas_call | solution.py:632
  70.4 18.0 %collective-permute-done.2.hop = bf16[512,768]{1,0:T(8,128)(2,1)S(1)} collective-permute-done((bf16[512,768]{1,0:T(8,128)(2,1)}, bf16[512,768]{1,0:T(8,128)(2,1)S(1)}, u32[]{:S(2)}, u32[]{:S(2)}) %collective-permute-start.2) | collective-permute-done | bytes 786464 | tf_op jit(solution)/shard_map/ppermute | solution.py:687
  89.2 10.1 %feedforward_forward.6 = (bf16[512,768]{1,0:T(8,128)(2,1)}, bf16[7,4,512,768]{3,2,1,0:T(8,128)(2,1)}) custom-call(s32[16]{0:T(128)} %concatenate.9.sc, s32[4]{0:T(128)} %constant.125.clone.tt, bf16[512,768]{1,0:T(8,128)(2,1)} %copy-done.42, bf16[768,3072]{1,0:T(8,128)(2,1)} %bitcast.53, ...), custom_call_target="tpu_custom_call", output_to_operand_aliasing={{1}: (8, {})} | custom-call | tf_op jit(solution)/shard_map/feedforward_forward/pallas_call | solution.py:632
  100.1 25.6 %attention_forward.7 = (bf16[512,768]{1,0:T(8,128)(2,1)}, bf16[7,4,512,768]{3,2,1,0:T(8,128)(2,1)}, bf16[2,4,1024,768]{3,2,1,0:T(8,128)(2,1)}, f32[4,512,128]{2,1,0:T(8,128)}) custom-call(s32[16]{0:T(128)} %concatenate.9.sc, s32[4]{0:T(128)} %constant.126.clone.tt, ...), custom_call_target="tpu_custom_call", output_to_operand_aliasing={{1}: (10, {}), {2}: (11, {}), {3}: (12, {})} | custom-call | tf_op jit(solution)/shard_map/attention_forward/pallas_call | solution.py:632
  127.7 16.8 %collective-permute-done.7.hop = bf16[512,768]{1,0:T(8,128)(2,1)S(1)} collective-permute-done((bf16[512,768]{1,0:T(8,128)(2,1)}, bf16[512,768]{1,0:T(8,128)(2,1)S(1)}, u32[]{:S(2)}, u32[]{:S(2)}) %collective-permute-start.7) | collective-permute-done | bytes 786464 | tf_op jit(solution)/shard_map/ppermute | solution.py:687
  145.4 10.3 %feedforward_forward.7 = (bf16[512,768]{1,0:T(8,128)(2,1)}, bf16[7,4,512,768]{3,2,1,0:T(8,128)(2,1)}) custom-call(s32[16]{0:T(128)} %concatenate.9.sc, s32[4]{0:T(128)} %constant.127.clone.tt, bf16[512,768]{1,0:T(8,128)(2,1)} %copy-done.40, bf16[768,3072]{1,0:T(8,128)(2,1)} %bitcast.55, ...), custom_call_target="tpu_custom_call", output_to_operand_aliasing={{1}: (8, {})} | custom-call | tf_op jit(solution)/shard_map/feedforward_forward/pallas_call | solution.py:632
  156.5 12.6 %attention_forward.8 = (bf16[512,768]{1,0:T(8,128)(2,1)}, bf16[7,4,512,768]{3,2,1,0:T(8,128)(2,1)}, bf16[2,4,1024,768]{3,2,1,0:T(8,128)(2,1)}, f32[4,512,128]{2,1,0:T(8,128)}) custom-call(s32[16]{0:T(128)} %concatenate.9.sc, s32[4]{0:T(128)} %constant.128.clone.tt, ...), custom_call_target="tpu_custom_call", output_to_operand_aliasing={{1}: (10, {}), {2}: (11, {}), {3}: (12, {})} | custom-call | tf_op jit(solution)/shard_map/attention_forward/pallas_call | solution.py:632
  173.4 16.5 %collective-permute-done.8.hop = bf16[512,768]{1,0:T(8,128)(2,1)S(1)} collective-permute-done((bf16[512,768]{1,0:T(8,128)(2,1)}, bf16[512,768]{1,0:T(8,128)(2,1)S(1)}, u32[]{:S(2)}, u32[]{:S(2)}) %collective-permute-start.8) | collective-permute-done | bytes 786464 | tf_op jit(solution)/shard_map/ppermute | solution.py:687
  198.9 23.4 %attention_forward.9 = (bf16[512,768]{1,0:T(8,128)(2,1)}, bf16[7,4,512,768]{3,2,1,0:T(8,128)(2,1)}, bf16[2,4,1024,768]{3,2,1,0:T(8,128)(2,1)}, f32[4,512,128]{2,1,0:T(8,128)}) custom-call(s32[16]{0:T(128)} %concatenate.9.sc, s32[4]{0:T(128)} %constant.130.clone.tt, ...), custom_call_target="tpu_custom_call", output_to_operand_aliasing={{1}: (10, {}), {2}: (11, {}), {3}: (12, {})} | custom-call | tf_op jit(solution)/shard_map/attention_forward/pallas_call | solution.py:632
  226.4 11.8 %feedforward_backward.8 = (bf16[512,768]{1,0:T(8,128)(2,1)}, bf16[7,4,512,768]{3,2,1,0:T(8,128)(2,1)}, bf16[4,512,3072]{2,1,0:T(8,128)(2,1)}, bf16[4,512,3072]{2,1,0:T(8,128)(2,1)}, f32[4,8,768]{2,1,0:T(8,128)}) custom-call(s32[16]{0:T(128)} %concatenate.9.sc, ...), custom_call_target="tpu_custom_call", output_to_operand_aliasing={{1}: (10, {}), {2}: (11, {}), {3}: (12, {}), {4}: (13, {})} | custom-call | tf_op jit(solution)/shard_map/feedforward_backward/pallas_call | solution.py:632
  246.8 12.5 %feedforward_backward.9 = (bf16[512,768]{1,0:T(8,128)(2,1)}, bf16[7,4,512,768]{3,2,1,0:T(8,128)(2,1)}, bf16[4,512,3072]{2,1,0:T(8,128)(2,1)}, bf16[4,512,3072]{2,1,0:T(8,128)(2,1)}, f32[4,8,768]{2,1,0:T(8,128)}) custom-call(s32[16]{0:T(128)} %concatenate.9.sc, ...), custom_call_target="tpu_custom_call", output_to_operand_aliasing={{1}: (10, {}), {2}: (11, {}), {3}: (12, {}), {4}: (13, {})} | custom-call | tf_op jit(solution)/shard_map/feedforward_backward/pallas_call | solution.py:632
  279.5 15.9 %feedforward_backward.11 = (bf16[512,768]{1,0:T(8,128)(2,1)}, bf16[7,4,512,768]{3,2,1,0:T(8,128)(2,1)}, bf16[4,512,3072]{2,1,0:T(8,128)(2,1)}, bf16[4,512,3072]{2,1,0:T(8,128)(2,1)}, f32[4,8,768]{2,1,0:T(8,128)}) custom-call(s32[16]{0:T(128)} %concatenate.9.sc, ...), custom_call_target="tpu_custom_call", output_to_operand_aliasing={{1}: (10, {}), {2}: (11, {}), {3}: (12, {}), {4}: (13, {})} | custom-call | tf_op jit(solution)/shard_map/feedforward_backward/pallas_call | solution.py:632
  307.4 10.6 %feedforward_backward.12 = (bf16[512,768]{1,0:T(8,128)(2,1)}, bf16[7,4,512,768]{3,2,1,0:T(8,128)(2,1)}, bf16[4,512,3072]{2,1,0:T(8,128)(2,1)}, bf16[4,512,3072]{2,1,0:T(8,128)(2,1)}, f32[4,8,768]{2,1,0:T(8,128)}) custom-call(s32[16]{0:T(128)} %concatenate.9.sc, ...), custom_call_target="tpu_custom_call", output_to_operand_aliasing={{1}: (10, {}), {2}: (11, {}), {3}: (12, {}), {4}: (13, {})} | custom-call | tf_op jit(solution)/shard_map/feedforward_backward/pallas_call | solution.py:632
  331.0 10.6 %feedforward_backward.13 = (bf16[512,768]{1,0:T(8,128)(2,1)}, bf16[7,4,512,768]{3,2,1,0:T(8,128)(2,1)}, bf16[4,512,3072]{2,1,0:T(8,128)(2,1)}, bf16[4,512,3072]{2,1,0:T(8,128)(2,1)}, f32[4,8,768]{2,1,0:T(8,128)}) custom-call(s32[16]{0:T(128)} %concatenate.9.sc, ...), custom_call_target="tpu_custom_call", output_to_operand_aliasing={{1}: (10, {}), {2}: (11, {}), {3}: (12, {}), {4}: (13, {})} | custom-call | tf_op jit(solution)/shard_map/feedforward_backward/pallas_call | solution.py:632
  341.7 113.1 %collective-permute-done.26.hop0 = bf16[512,768]{1,0:T(8,128)(2,1)S(1)} collective-permute-done((bf16[512,768]{1,0:T(8,128)(2,1)S(1)}, bf16[512,768]{1,0:T(8,128)(2,1)S(1)}, u32[]{:S(2)}, u32[]{:S(2)}) %collective-permute-start.26) | collective-permute-done | bytes 786464 | tf_op jit(solution)/shard_map/ppermute | solution.py:687
  455.7 23.0 %attention_backward.8 = (bf16[2,768,512]{2,1,0:T(8,128)(2,1)}, bf16[2,768,512]{2,1,0:T(8,128)(2,1)}, bf16[7,4,512,768]{3,2,1,0:T(8,128)(2,1)}, bf16[4,512,3072]{2,1,0:T(8,128)(2,1)}) custom-call(s32[16]{0:T(128)} %concatenate.9.sc, s32[4]{0:T(128)} %constant.140.clone.tt, bf16[512,768]{1,0:T(8,128)(2,1)} %copy-done.14, ...), custom_call_target="tpu_custom_call", output_to_operand_aliasing={{2}: (8, {}), {3}: (9, {})} | custom-call | tf_op jit(solution)/shard_map/attention_backward/pallas_call | solution.py:632
  483.5 11.1 %projection_backward.8 = (bf16[512,768]{1,0:T(8,128)(2,1)}, bf16[7,4,512,768]{3,2,1,0:T(8,128)(2,1)}, bf16[4,512,3072]{2,1,0:T(8,128)(2,1)}, f32[4,8,768]{2,1,0:T(8,128)}) custom-call(s32[16]{0:T(128)} %concatenate.9.sc, s32[4]{0:T(128)} %constant.140.clone.tt, ...), custom_call_target="tpu_custom_call", output_to_operand_aliasing={{1}: (10, {}), {2}: (11, {}), {3}: (12, {})} | custom-call | tf_op jit(solution)/shard_map/projection_backward/pallas_call | solution.py:632
  498.2 10.6 %feedforward_backward.14 = (bf16[512,768]{1,0:T(8,128)(2,1)}, bf16[7,4,512,768]{3,2,1,0:T(8,128)(2,1)}, bf16[4,512,3072]{2,1,0:T(8,128)(2,1)}, bf16[4,512,3072]{2,1,0:T(8,128)(2,1)}, f32[4,8,768]{2,1,0:T(8,128)}) custom-call(s32[16]{0:T(128)} %concatenate.9.sc, ...), custom_call_target="tpu_custom_call", output_to_operand_aliasing={{1}: (10, {}), {2}: (11, {}), {3}: (12, {}), {4}: (13, {})} | custom-call | tf_op jit(solution)/shard_map/feedforward_backward/pallas_call | solution.py:632
  508.8 16.5 %collective-permute-done.32.hop0 = bf16[512,768]{1,0:T(8,128)(2,1)S(1)} collective-permute-done((bf16[512,768]{1,0:T(8,128)(2,1)S(1)}, bf16[512,768]{1,0:T(8,128)(2,1)S(1)}, u32[]{:S(2)}, u32[]{:S(2)}) %collective-permute-start.32) | collective-permute-done | bytes 786464 | tf_op jit(solution)/shard_map/ppermute | solution.py:687
  526.2 23.0 %attention_backward.9 = (bf16[2,768,512]{2,1,0:T(8,128)(2,1)}, bf16[2,768,512]{2,1,0:T(8,128)(2,1)}, bf16[7,4,512,768]{3,2,1,0:T(8,128)(2,1)}, bf16[4,512,3072]{2,1,0:T(8,128)(2,1)}) custom-call(s32[16]{0:T(128)} %concatenate.9.sc, s32[4]{0:T(128)} %constant.142.clone.tt, bf16[512,768]{1,0:T(8,128)(2,1)} %copy-done.16, ...), custom_call_target="tpu_custom_call", output_to_operand_aliasing={{2}: (8, {}), {3}: (9, {})} | custom-call | tf_op jit(solution)/shard_map/attention_backward/pallas_call | solution.py:632
  554.0 11.1 %projection_backward.9 = (bf16[512,768]{1,0:T(8,128)(2,1)}, bf16[7,4,512,768]{3,2,1,0:T(8,128)(2,1)}, bf16[4,512,3072]{2,1,0:T(8,128)(2,1)}, f32[4,8,768]{2,1,0:T(8,128)}) custom-call(s32[16]{0:T(128)} %concatenate.9.sc, s32[4]{0:T(128)} %constant.142.clone.tt, ...), custom_call_target="tpu_custom_call", output_to_operand_aliasing={{1}: (10, {}), {2}: (11, {}), {3}: (12, {})} | custom-call | tf_op jit(solution)/shard_map/projection_backward/pallas_call | solution.py:632
  568.0 10.7 %feedforward_backward.15 = (bf16[512,768]{1,0:T(8,128)(2,1)}, bf16[7,4,512,768]{3,2,1,0:T(8,128)(2,1)}, bf16[4,512,3072]{2,1,0:T(8,128)(2,1)}, bf16[4,512,3072]{2,1,0:T(8,128)(2,1)}, f32[4,8,768]{2,1,0:T(8,128)}) custom-call(s32[16]{0:T(128)} %concatenate.9.sc, ...), custom_call_target="tpu_custom_call", output_to_operand_aliasing={{1}: (10, {}), {2}: (11, {}), {3}: (12, {}), {4}: (13, {})} | custom-call | tf_op jit(solution)/shard_map/feedforward_backward/pallas_call | solution.py:632
  588.2 11.0 %attention_backward.10 = (bf16[2,768,512]{2,1,0:T(8,128)(2,1)}, bf16[2,768,512]{2,1,0:T(8,128)(2,1)}, bf16[7,4,512,768]{3,2,1,0:T(8,128)(2,1)}, bf16[4,512,3072]{2,1,0:T(8,128)(2,1)}) custom-call(s32[16]{0:T(128)} %concatenate.9.sc, s32[4]{0:T(128)} %constant.144.clone.tt, ...), custom_call_target="tpu_custom_call", output_to_operand_aliasing={{2}: (8, {}), {3}: (9, {})} | custom-call | tf_op jit(solution)/shard_map/attention_backward/pallas_call | solution.py:632
  612.8 27.0 %collective-permute-done.39.hop0 = bf16[512,768]{1,0:T(8,128)(2,1)S(1)} collective-permute-done((bf16[512,768]{1,0:T(8,128)(2,1)S(1)}, bf16[512,768]{1,0:T(8,128)(2,1)S(1)}, u32[]{:S(2)}, u32[]{:S(2)}) %collective-permute-start.39) | collective-permute-done | bytes 786464 | tf_op jit(solution)/shard_map/ppermute | solution.py:687
  640.6 18.8 %attention_backward.11 = (bf16[2,768,512]{2,1,0:T(8,128)(2,1)}, bf16[2,768,512]{2,1,0:T(8,128)(2,1)}, bf16[7,4,512,768]{3,2,1,0:T(8,128)(2,1)}, bf16[4,512,3072]{2,1,0:T(8,128)(2,1)}) custom-call(s32[16]{0:T(128)} %concatenate.9.sc, s32[4]{0:T(128)} %constant.145.clone.tt, ...), custom_call_target="tpu_custom_call", output_to_operand_aliasing={{2}: (8, {}), {3}: (9, {})} | custom-call | tf_op jit(solution)/shard_map/attention_backward/pallas_call | solution.py:632
  664.3 11.0 %projection_backward.11 = (bf16[512,768]{1,0:T(8,128)(2,1)}, bf16[7,4,512,768]{3,2,1,0:T(8,128)(2,1)}, bf16[4,512,3072]{2,1,0:T(8,128)(2,1)}, f32[4,8,768]{2,1,0:T(8,128)}) custom-call(s32[16]{0:T(128)} %concatenate.9.sc, s32[4]{0:T(128)} %constant.145.clone.tt, ...), custom_call_target="tpu_custom_call", output_to_operand_aliasing={{1}: (10, {}), {2}: (11, {}), {3}: (12, {})} | custom-call | tf_op jit(solution)/shard_map/projection_backward/pallas_call | solution.py:632
  688.1 51.9 %collective-permute-done.45 = bf16[1536,768]{1,0:T(8,128)(2,1)S(1)} collective-permute-done((bf16[1536,768]{1,0:T(8,128)(2,1)}, bf16[1536,768]{1,0:T(8,128)(2,1)S(1)}, u32[]{:S(2)}, u32[]{:S(2)}) %collective-permute-start.45) | collective-permute-done | bytes 2359328 | tf_op jit(solution)/shard_map/ppermute | solution.py:687
  743.6 19.1 %first_gradient.1 = bf16[768,3072]{1,0:T(8,128)(2,1)} custom-call(s32[16]{0:T(128)} %concatenate.9.sc, bf16[7,4,512,768]{3,2,1,0:T(8,128)(2,1)} %get-tuple-element.265.x1.x2.gb, bf16[7,4,512,768]{3,2,1,0:T(8,128)(2,1)} %get-tuple-element.265.x1.x2.gb, bf16[4,512,3072]{2,1,0:T(8,128)(2,1)} %get-tuple-element.266.y), custom_call_target="tpu_custom_call" | custom-call | tf_op jit(solution)/shard_map/first_gradient/pallas_call | solution.py:823
  779.1 11.2 %collective-permute-done.19 = bf16[4,256,768]{2,1,0:T(8,128)(2,1)} collective-permute-done((bf16[4,256,768]{2,1,0:T(8,128)(2,1)}, bf16[4,256,768]{2,1,0:T(8,128)(2,1)}, u32[]{:S(2)}, u32[]{:S(2)}) %collective-permute-start.19) | collective-permute-done | bytes 1572896 | tf_op jit(solution)/shard_map/ppermute | solution.py:875
  809.2 11.1 %all-reduce.1 = s32[32]{0:T(128)S(1)} all-reduce(s32[32]{0:T(128)S(1)} %dynamic-update-slice), channel_id=2, replica_groups=mesh['segment'=4,'dp'=8] {'dp'}, use_global_device_ids=true, to_apply=%add.1 | all-reduce | flops 32 | bytes 256
  822.7 15.5 %all-gather.1 = f32[8,4,2304]{2,1,0:T(4,128)S(1)} all-gather(f32[1,4,2304]{2,1,0:T(4,128)S(1)} %reshape.86), channel_id=1, replica_groups=mesh['segment'=4,'dp'=8] {'dp'}, dimensions={0}, use_global_device_ids=true | all-gather | bytes 331776 | tf_op jit(solution)/shard_map/all_gather | solution.py:856
  (262 shorter events, 207.2 us)
Async XLA Ops:
  7.2 838.1 %reduce-scatter.5.cloned.1.call-start = ((), (), s32[]{:S(2)}) async-start(), calls=%async_computation.3 | async-start | bytes 2654208 | tf_op jit(solution)/shard_map/reduce_scatter | solution.py:853
  7.2 36.4 %collective-permute-start.1 = (bf16[2,1024,768]{2,1,0:T(8,128)(2,1)}, bf16[2,1024,768]{2,1,0:T(8,128)(2,1)}, u32[]{:S(2)}, u32[]{:S(2)}) collective-permute-start(bf16[2,1024,768]{2,1,0:T(8,128)(2,1)} %own_x.11), channel_id=1, source_target_pairs={{0,1},{1,0},{2,3},{3,2},{4,5},{5,4},{6,7},{7,6},{8,9},{9,8},{10,11... | collective-permute-start | bytes 9437192 | tf_op jit(solution)/shard_map/ppermute | solution.py:684
  10.4 30.6 %collective-permute-start.3 = (bf16[768,768]{1,0:T(8,128)(2,1)}, bf16[768,768]{1,0:T(8,128)(2,1)}, u32[]{:S(2)}, u32[]{:S(2)}) collective-permute-start(bf16[768,768]{1,0:T(8,128)(2,1)} %dynamic-slice_bitcast_fusion), channel_id=1, source_target_pairs={{0,8},{16,24},{1,9},{17,25},{2,10},{18,26},{3,11},{19,27},{4,12},{... | collective-permute-start | bytes 3538952 | tf_op jit(solution)/shard_map/ppermute | solution.py:687
  41.0 29.4 %collective-permute-start.4 = (bf16[768,768]{1,0:T(8,128)(2,1)}, bf16[768,768]{1,0:T(8,128)(2,1)}, u32[]{:S(2)}, u32[]{:S(2)}) collective-permute-start(bf16[768,768]{1,0:T(8,128)(2,1)} %collective-permute-done.3.prt_own), channel_id=1, source_target_pairs={{0,1},{1,0},{2,3},{3,2},{4,5},{5,4},{6,7},{7,6},{8,9},{9,8},{10,11... | collective-permute-start | bytes 3538952 | tf_op jit(solution)/shard_map/ppermute | solution.py:684
  69.0 19.4 %collective-permute-start.2 = (bf16[512,768]{1,0:T(8,128)(2,1)}, bf16[512,768]{1,0:T(8,128)(2,1)S(1)}, u32[]{:S(2)}, u32[]{:S(2)}) collective-permute-start(bf16[512,768]{1,0:T(8,128)(2,1)} %get-tuple-element.141), channel_id=1, source_target_pairs={{0,8},{1,9},{2,10},{3,11},{4,12},{5,13},{6,14},{7,15}} | collective-permute-start | bytes 2359304 | tf_op jit(solution)/shard_map/ppermute | solution.py:687
  99.4 27.8 %collective-permute-start.5 = (bf16[512,768]{1,0:T(8,128)(2,1)}, bf16[512,768]{1,0:T(8,128)(2,1)S(1)}, u32[]{:S(2)}, u32[]{:S(2)}) collective-permute-start(bf16[512,768]{1,0:T(8,128)(2,1)} %get-tuple-element.143), channel_id=1, source_target_pairs={{8,16},{9,17},{10,18},{11,19},{12,20},{13,21},{14,22},{15,23}} | collective-permute-start | bytes 2359304 | tf_op jit(solution)/shard_map/ppermute | solution.py:687
  125.8 18.8 %collective-permute-start.7 = (bf16[512,768]{1,0:T(8,128)(2,1)}, bf16[512,768]{1,0:T(8,128)(2,1)S(1)}, u32[]{:S(2)}, u32[]{:S(2)}) collective-permute-start(bf16[512,768]{1,0:T(8,128)(2,1)} %get-tuple-element.147), channel_id=1, source_target_pairs={{0,8},{1,9},{2,10},{3,11},{4,12},{5,13},{6,14},{7,15}} | collective-permute-start | bytes 2359304 | tf_op jit(solution)/shard_map/ppermute | solution.py:687
  127.1 97.4 %collective-permute-start.12 = (bf16[2,1024,768]{2,1,0:T(8,128)(2,1)S(1)}, bf16[2,1024,768]{2,1,0:T(8,128)(2,1)S(1)}, u32[]{:S(2)}, u32[]{:S(2)}) collective-permute-start(bf16[2,1024,768]{2,1,0:T(8,128)(2,1)S(1)} %copy-done.2), channel_id=1, source_target_pairs={{0,1},{1,0},{2,3},{3,2},{4,5},{5,4},{6,7},{7,6},{8,9},{9,8},{10,11... | collective-permute-start | bytes 9437192 | tf_op jit(solution)/shard_map/ppermute | solution.py:684
  127.2 29.2 %collective-permute-start.6 = (bf16[512,768]{1,0:T(8,128)(2,1)S(1)}, bf16[512,768]{1,0:T(8,128)(2,1)}, u32[]{:S(2)}, u32[]{:S(2)}) collective-permute-start(bf16[512,768]{1,0:T(8,128)(2,1)S(1)} %collective-permute-done.5.hop_own), channel_id=1, source_target_pairs={{0,1},{1,0},{2,3},{3,2},{4,5},{5,4},{6,7},{7,6},{8,9},{9,8},{10,11... | collective-permute-start | bytes 2359304 | tf_op jit(solution)/shard_map/ppermute | solution.py:684
  155.7 17.6 %collective-permute-start.9 = (bf16[512,768]{1,0:T(8,128)(2,1)}, bf16[512,768]{1,0:T(8,128)(2,1)S(1)}, u32[]{:S(2)}, u32[]{:S(2)}) collective-permute-start(bf16[512,768]{1,0:T(8,128)(2,1)} %get-tuple-element.155), channel_id=1, source_target_pairs={{8,16},{9,17},{10,18},{11,19},{12,20},{13,21},{14,22},{15,23}} | collective-permute-start | bytes 2359304 | tf_op jit(solution)/shard_map/ppermute | solution.py:687
  169.0 20.9 %collective-permute-start.8 = (bf16[512,768]{1,0:T(8,128)(2,1)}, bf16[512,768]{1,0:T(8,128)(2,1)S(1)}, u32[]{:S(2)}, u32[]{:S(2)}) collective-permute-start(bf16[512,768]{1,0:T(8,128)(2,1)} %get-tuple-element.152), channel_id=1, source_target_pairs={{0,8},{16,24},{1,9},{17,25},{2,10},{18,26},{3,11},{19,27},{4,12},{... | collective-permute-start | bytes 2359304 | tf_op jit(solution)/shard_map/ppermute | solution.py:687
  173.3 25.6 %collective-permute-start.10 = (bf16[512,768]{1,0:T(8,128)(2,1)S(1)}, bf16[512,768]{1,0:T(8,128)(2,1)}, u32[]{:S(2)}, u32[]{:S(2)}) collective-permute-start(bf16[512,768]{1,0:T(8,128)(2,1)S(1)} %collective-permute-done.9.hop_own), channel_id=1, source_target_pairs={{0,1},{1,0},{2,3},{3,2},{4,5},{5,4},{6,7},{7,6},{8,9},{9,8},{10,11... | collective-permute-start | bytes 2359304 | tf_op jit(solution)/shard_map/ppermute | solution.py:684
  198.1 26.4 %collective-permute-start.13 = (bf16[512,768]{1,0:T(8,128)(2,1)}, bf16[512,768]{1,0:T(8,128)(2,1)S(1)}, u32[]{:S(2)}, u32[]{:S(2)}) collective-permute-start(bf16[512,768]{1,0:T(8,128)(2,1)} %get-tuple-element.154), channel_id=1, source_target_pairs={{8,16},{9,17},{10,18},{11,19},{12,20},{13,21},{14,22},{15,23}} | collective-permute-start | bytes 2359304 | tf_op jit(solution)/shard_map/ppermute | solution.py:687
  222.3 15.8 %collective-permute-start.11 = (bf16[512,768]{1,0:T(8,128)(2,1)}, bf16[512,768]{1,0:T(8,128)(2,1)}, u32[]{:S(2)}, u32[]{:S(2)}) collective-permute-start(bf16[512,768]{1,0:T(8,128)(2,1)} %get-tuple-element.159), channel_id=1, source_target_pairs={{0,8},{16,24},{1,9},{17,25},{2,10},{18,26},{3,11},{19,27},{4,12},{... | collective-permute-start | bytes 2359304 | tf_op jit(solution)/shard_map/ppermute | solution.py:687
  224.5 16.0 %collective-permute-start.14 = (bf16[512,768]{1,0:T(8,128)(2,1)S(1)}, bf16[512,768]{1,0:T(8,128)(2,1)S(1)}, u32[]{:S(2)}, u32[]{:S(2)}) collective-permute-start(bf16[512,768]{1,0:T(8,128)(2,1)S(1)} %collective-permute-done.13.hop_own), channel_id=1, source_target_pairs={{0,1},{1,0},{2,3},{3,2},{4,5},{5,4},{6,7},{7,6},{8,9},{9,8},{10,11... | collective-permute-start | bytes 2359304 | tf_op jit(solution)/shard_map/ppermute | solution.py:684
  245.5 13.8 %collective-permute-start.15 = (bf16[512,768]{1,0:T(8,128)(2,1)}, bf16[512,768]{1,0:T(8,128)(2,1)S(1)}, u32[]{:S(2)}, u32[]{:S(2)}) collective-permute-start(bf16[512,768]{1,0:T(8,128)(2,1)} %get-tuple-element.169), channel_id=1, source_target_pairs={{16,24},{17,25},{18,26},{19,27},{20,28},{21,29},{22,30},{23,31}} | collective-permute-start | bytes 2359304 | tf_op jit(solution)/shard_map/ppermute | solution.py:687
  246.3 15.6 %collective-permute-start.17 = (bf16[512,768]{1,0:T(8,128)(2,1)S(1)}, bf16[512,768]{1,0:T(8,128)(2,1)S(1)}, u32[]{:S(2)}, u32[]{:S(2)}) collective-permute-start(bf16[512,768]{1,0:T(8,128)(2,1)S(1)} %collective-permute-done.16.hop_own), channel_id=1, source_target_pairs={{0,1},{1,0},{2,3},{3,2},{4,5},{5,4},{6,7},{7,6},{8,9},{9,8},{10,11... | collective-permute-start | bytes 2359304 | tf_op jit(solution)/shard_map/ppermute | solution.py:684
  267.5 28.0 %collective-permute-start.23 = (bf16[512,768]{1,0:T(8,128)(2,1)S(1)}, bf16[512,768]{1,0:T(8,128)(2,1)S(1)}, u32[]{:S(2)}, u32[]{:S(2)}) collective-permute-start(bf16[512,768]{1,0:T(8,128)(2,1)S(1)} %copy-done.51), channel_id=1, source_target_pairs={{24,16},{25,17},{26,18},{27,19},{28,20},{29,21},{30,22},{31,23}} | collective-permute-start | bytes 2359304 | tf_op jit(solution)/shard_map/ppermute | solution.py:687
  328.1 13.6 %collective-permute-start.27 = (bf16[512,768]{1,0:T(8,128)(2,1)S(1)}, bf16[512,768]{1,0:T(8,128)(2,1)S(1)}, u32[]{:S(2)}, u32[]{:S(2)}) collective-permute-start(bf16[512,768]{1,0:T(8,128)(2,1)S(1)} %copy-done.49), channel_id=1, source_target_pairs={{24,16},{25,17},{26,18},{27,19},{28,20},{29,21},{30,22},{31,23}} | collective-permute-start | bytes 2359304 | tf_op jit(solution)/shard_map/ppermute | solution.py:687
  328.9 125.9 %collective-permute-start.26 = (bf16[512,768]{1,0:T(8,128)(2,1)S(1)}, bf16[512,768]{1,0:T(8,128)(2,1)S(1)}, u32[]{:S(2)}, u32[]{:S(2)}) collective-permute-start(bf16[512,768]{1,0:T(8,128)(2,1)S(1)} %copy-done.53), channel_id=1, source_target_pairs={{8,0},{9,1},{10,2},{11,3},{12,4},{13,5},{14,6},{15,7}} | collective-permute-start | bytes 2359304 | tf_op jit(solution)/shard_map/ppermute | solution.py:687
  496.0 29.3 %collective-permute-start.32 = (bf16[512,768]{1,0:T(8,128)(2,1)S(1)}, bf16[512,768]{1,0:T(8,128)(2,1)S(1)}, u32[]{:S(2)}, u32[]{:S(2)}) collective-permute-start(bf16[512,768]{1,0:T(8,128)(2,1)S(1)} %copy-done.52), channel_id=1, source_target_pairs={{8,0},{9,1},{10,2},{11,3},{12,4},{13,5},{14,6},{15,7}} | collective-permute-start | bytes 2359304 | tf_op jit(solution)/shard_map/ppermute | solution.py:687
  565.8 21.5 %collective-permute-start.36 = (bf16[512,768]{1,0:T(8,128)(2,1)S(1)}, bf16[512,768]{1,0:T(8,128)(2,1)S(1)}, u32[]{:S(2)}, u32[]{:S(2)}) collective-permute-start(bf16[512,768]{1,0:T(8,128)(2,1)S(1)} %copy-done.54), channel_id=1, source_target_pairs={{8,0},{9,1},{10,2},{11,3},{12,4},{13,5},{14,6},{15,7}} | collective-permute-start | bytes 2359304 | tf_op jit(solution)/shard_map/ppermute | solution.py:687
  599.2 40.5 %collective-permute-start.39 = (bf16[512,768]{1,0:T(8,128)(2,1)S(1)}, bf16[512,768]{1,0:T(8,128)(2,1)S(1)}, u32[]{:S(2)}, u32[]{:S(2)}) collective-permute-start(bf16[512,768]{1,0:T(8,128)(2,1)S(1)} %copy-done.55), channel_id=1, source_target_pairs={{8,0},{9,1},{10,2},{11,3},{12,4},{13,5},{14,6},{15,7}} | collective-permute-start | bytes 2359304 | tf_op jit(solution)/shard_map/ppermute | solution.py:687
  686.8 53.2 %collective-permute-start.45 = (bf16[1536,768]{1,0:T(8,128)(2,1)}, bf16[1536,768]{1,0:T(8,128)(2,1)S(1)}, u32[]{:S(2)}, u32[]{:S(2)}) collective-permute-start(bf16[1536,768]{1,0:T(8,128)(2,1)} %slice.62), channel_id=1, source_target_pairs={{8,0},{24,16},{9,1},{25,17},{10,2},{26,18},{11,3},{27,19},{12,4},{... | collective-permute-start | bytes 7077896 | tf_op jit(solution)/shard_map/ppermute | solution.py:687
  743.3 103.8 %reduce-scatter.3.cloned.1.call-start = ((), (), s32[]{:S(2)}) async-start(), calls=%async_computation.2 | async-start | bytes 5308416 | tf_op jit(solution)/shard_map/reduce_scatter | solution.py:852
  766.6 23.6 %collective-permute-start.19 = (bf16[4,256,768]{2,1,0:T(8,128)(2,1)}, bf16[4,256,768]{2,1,0:T(8,128)(2,1)}, u32[]{:S(2)}, u32[]{:S(2)}) collective-permute-start(bf16[4,256,768]{2,1,0:T(8,128)(2,1)} %get-tuple-element.276), channel_id=1, source_target_pairs={{24,0},{26,2},{28,4},{30,6}} | collective-permute-start | bytes 4718600 | tf_op jit(solution)/shard_map/ppermute | solution.py:875
  768.1 24.4 %collective-permute-start.20 = (bf16[4,256,768]{2,1,0:T(8,128)(2,1)}, bf16[4,256,768]{2,1,0:T(8,128)(2,1)}, u32[]{:S(2)}, u32[]{:S(2)}) collective-permute-start(bf16[4,256,768]{2,1,0:T(8,128)(2,1)} %get-tuple-element.276), channel_id=1, source_target_pairs={{25,9},{27,11},{29,13},{31,15}} | collective-permute-start | bytes 4718600 | tf_op jit(solution)/shard_map/ppermute | solution.py:875
  769.9 22.6 %collective-permute-start.21 = (bf16[4,256,768]{2,1,0:T(8,128)(2,1)}, bf16[4,256,768]{2,1,0:T(8,128)(2,1)}, u32[]{:S(2)}, u32[]{:S(2)}) collective-permute-start(bf16[4,256,768]{2,1,0:T(8,128)(2,1)} %get-tuple-element.277), channel_id=1, source_target_pairs={{24,16},{26,18},{28,20},{30,22}} | collective-permute-start | bytes 4718600 | tf_op jit(solution)/shard_map/ppermute | solution.py:875
  774.9 21.6 %collective-permute-start.41 = (bf16[4,256,768]{2,1,0:T(8,128)(2,1)}, bf16[4,256,768]{2,1,0:T(8,128)(2,1)}, u32[]{:S(2)}, u32[]{:S(2)}) collective-permute-start(bf16[4,256,768]{2,1,0:T(8,128)(2,1)} %get-tuple-element.274), channel_id=1, source_target_pairs={{1,9},{3,11},{5,13},{7,15}} | collective-permute-start | bytes 4718600 | tf_op jit(solution)/shard_map/ppermute | solution.py:875
  776.7 19.8 %collective-permute-start.42 = (bf16[4,256,768]{2,1,0:T(8,128)(2,1)}, bf16[4,256,768]{2,1,0:T(8,128)(2,1)}, u32[]{:S(2)}, u32[]{:S(2)}) collective-permute-start(bf16[4,256,768]{2,1,0:T(8,128)(2,1)} %get-tuple-element.275), channel_id=1, source_target_pairs={{0,16},{2,18},{4,20},{6,22}} | collective-permute-start | bytes 4718600 | tf_op jit(solution)/shard_map/ppermute | solution.py:875
  796.4 24.2 %collective-permute-start.22 = (bf16[2,256,768]{2,1,0:T(8,128)(2,1)}, bf16[2,256,768]{2,1,0:T(8,128)(2,1)}, u32[]{:S(2)}, u32[]{:S(2)}) collective-permute-start(bf16[2,256,768]{2,1,0:T(8,128)(2,1)} %dynamic-slice_bitcast_fusion.2), channel_id=1, source_target_pairs={{0,1},{1,0},{2,3},{3,2},{4,5},{5,4},{6,7},{7,6},{8,9},{9,8},{10,11... | collective-permute-start | bytes 2359304 | tf_op jit(solution)/shard_map/ppermute | solution.py:684
  799.3 41.3 %collective-permute-start.44 = (bf16[2,256,768]{2,1,0:T(8,128)(2,1)S(1)}, bf16[2,256,768]{2,1,0:T(8,128)(2,1)}, u32[]{:S(2)}, u32[]{:S(2)}) collective-permute-start(bf16[2,256,768]{2,1,0:T(8,128)(2,1)S(1)} %dynamic-slice_bitcast_fusion.1), channel_id=1, source_target_pairs={{0,1},{1,0},{2,3},{3,2},{4,5},{5,4},{6,7},{7,6},{8,9},{9,8},{10,11... | collective-permute-start | bytes 2359304 | tf_op jit(solution)/shard_map/ppermute | solution.py:684
  (73 other events, 663.2 us)
Sparse Core Ops, SparseCore 0:
  743.4 34.6 reduce-scatter.4
  780.4 56.2 reduce-scatter.2

commit v2 on v1

v2 whole, which is shorter than its diff:
```python
import functools
import math

import jax
import jax.numpy as jnp
import numpy as np
from jax import lax
from jax.experimental import pallas as pl
from jax.experimental.pallas import tpu as pltpu
from jax.sharding import PartitionSpec as P

D = 768
HEADS = 12
HEAD_DIM = 64
FF = 3072
SEQ_LEN = 1024
BLK = 256
HALF = SEQ_LEN // 2
MB = 4
XS, QS, AT, BR, NM, DQ, XF, BF, NF, GB = range(10)
VLIM = 56 << 20
bf16, f32, i32 = jnp.bfloat16, jnp.float32, jnp.int32


def dot(a, b):
    return lax.dot_general(a, b, (((1,), (0,)), ((), ())), preferred_element_type=f32)


def dot_nt(a, b):
    return lax.dot_general(a, b, (((1,), (1,)), ((), ())), preferred_element_type=f32)


def dot_tn(a, b):
    return lax.dot_general(a, b, (((0,), (0,)), ((), ())), preferred_element_type=f32)


def block_rows(b):
    return pl.ds(pl.multiple_of(b * BLK, BLK), BLK)


def lanes(p):
    return pl.ds(pl.multiple_of(p * 128, 128), 128)


def norm_parts(x):
    center = x - jnp.mean(x, axis=-1, keepdims=True)
    rstd = lax.rsqrt(jnp.mean(center * center, axis=-1, keepdims=True) + 1e-06)
    return center * rstd, rstd


def norm_back(d_normed, n, rstd, scl):
    dn = d_normed * scl
    return (
        dn - jnp.mean(dn, axis=-1, keepdims=True) - n * jnp.mean(dn * n, axis=-1, keepdims=True)
    ) * rstd


def turn(v, cosine, sine):
    lane = lax.broadcasted_iota(i32, v.shape, 1)
    partner = jnp.where(lane % 64 < 32, pltpu.roll(v, 96, 1), pltpu.roll(v, 32, 1))
    return v * cosine + partner * sine


def live_column(rows, c, length, first=0):
    r = lax.broadcasted_iota(i32, (rows, 1), 0) + first
    position = r + BLK * c + jnp.where(r >= BLK, BLK, 0)
    return position < length


def counts(length, c):
    nk = lax.shift_right_logical(length + (BLK - 1), 8)
    return nk, lax.shift_right_logical(nk - c + 1, 1)


class Copies:
    def __init__(self, sems):
        self.sems, self.started = sems, []

    def add(self, src, dst):
        copy = pltpu.make_async_copy(src, dst, self.sems.at[len(self.started)])
        copy.start()
        self.started.append(copy)

    def wait(self):
        for copy in self.started:
            copy.wait()


def load_shared(c, borrowed, w, wx_own, wx_oth, cols, wv, sem, into=None):
    into = cols if into is None else into
    whole = pltpu.make_async_copy(w.at[:, cols], wv.at[:, into], sem)
    pl.when(jnp.logical_not(borrowed))(lambda: whole.start())
    half = D // 2

    @pl.when(borrowed)
    def _():
        for source, at in ((wx_own, c), (wx_oth, 1 - c)):
            rows = pl.ds(pl.multiple_of(at * half, half), half)
            pltpu.make_async_copy(source.at[:, cols], wv.at[rows, into], sem).start()

    return whole


def att_f_kernel(sc, tt, own2, oth2, own3, oth3, own_x, rcv_full, rcv_short, w, wx_own, wx_oth,
                 cos, sin, mod,
                 st_i, kv_i, lse_i,
                 out, st, kv, lse,
                 xv, nv, wv, kvv, vv, qv, av, bv, ov, lv, cv, sv, sem, osem):
    role = sc[0]
    mb = tt[role]

    @pl.when(mb >= 0)
    def _():
        c, length, idx = sc[1], sc[2 + mb], sc[6 + mb]
        nk, ns = counts(length, c)
        mine = lax.rem(mb, 2) == c

        @pl.when((role == 0) & mine)
        def _():
            pltpu.make_async_copy(own_x.at[idx], xv, sem.at[0]).start()

        for pick, source in ((mb < 2, rcv_full), (mb >= 2, rcv_short)):

            @pl.when((role == 0) & jnp.logical_not(mine) & pick)
            def _():
                pltpu.make_async_copy(source, xv, sem.at[0]).start()

        for who, own, oth in ((2, own2, oth2), (3, own3, oth3)):

            @pl.when(role == who)
            def _():
                for j in range(2):
                    rows = pl.ds(j * BLK, BLK)
                    pltpu.make_async_copy(
                        own.at[rows], xv.at[block_rows(c + 2 * j)], sem.at[0]
                    ).start()
                    pltpu.make_async_copy(
                        oth.at[rows], xv.at[block_rows(1 - c + 2 * j)], sem.at[0]
                    ).start()

        wcopies = []
        for part in (1, 2, 0, 3):
            wcopies.append(
                load_shared(c, role == 3, w, wx_own, wx_oth, pl.ds(part * D, D), wv, sem.at[1 + part])
            )
        tables = [
            pltpu.make_async_copy(cos, cv, sem.at[5]),
            pltpu.make_async_copy(sin, sv, sem.at[6]),
        ]
        for copy in tables:
            copy.start()
        off, scl, gat = mod[mb, 0:1, :], 1.0 + mod[mb, 1:2, :], mod[mb, 2:3, :]
        pltpu.make_async_copy(own_x.at[0], xv, sem.at[0]).wait()

        def norm_block(b, carry):
            rows = block_rows(b)
            n, _ = norm_parts(xv[rows, :].astype(f32))
            nv[rows, :] = (n * scl + off).astype(bf16)
            return carry

        lax.fori_loop(0, nk, norm_block, 0)
        for copy in tables:
            copy.wait()
        wcopies[0].wait()
        wcopies[1].wait()

        def kv_block(b, carry):
            rows = block_rows(b)
            n = nv[rows, :]
            cosine, sine = cv[rows, :], sv[rows, :]
            kk = dot(n, wv[:, D : 2 * D])
            for p in range(6):
                ls = slice(p * 128, (p + 1) * 128)
                kvv[rows, ls] = turn(kk[:, ls], cosine, sine).astype(bf16)
            vv[rows, :] = dot(n, wv[:, 2 * D : 3 * D]).astype(bf16)
            return carry

        lax.fori_loop(0, nk, kv_block, 0)
        wcopies[2].wait()

        def q_block(j, carry):
            nat = block_rows(c + 2 * j)
            rows = block_rows(j)
            cosine, sine = cv[nat, :] * 0.125, sv[nat, :] * 0.125
            qq = dot(nv[nat, :], wv[:, 0:D])
            for p in range(6):
                ls = slice(p * 128, (p + 1) * 128)
                qv[rows, ls] = turn(qq[:, ls], cosine, sine).astype(bf16)
            return carry

        lax.fori_loop(0, ns, q_block, 0)

        lane = lax.broadcasted_iota(i32, (BLK, 128), 1)

        def clear_block(b):
            kvv[b * BLK : (b + 1) * BLK, :] = jnp.zeros((BLK, D), bf16)
            vv[b * BLK : (b + 1) * BLK, :] = jnp.zeros((BLK, D), bf16)

        def attend(keys):
            position = lax.broadcasted_iota(i32, (1, keys), 1)
            bias = jnp.where(position < length, 0.0, -1e30).astype(f32)

            def pair(i, carry):
                j, hp = lax.div(i, HEADS // 2), lax.rem(i, HEADS // 2)
                rows, ls = block_rows(j), lanes(hp)
                k2, v2, q2 = kvv[0:keys, ls], vv[0:keys, ls], qv[rows, ls]
                outs, stats = [], lv[rows, :]
                for a in range(2):
                    s = dot_nt(jnp.where((lane < 64) == (a == 0), q2, jnp.zeros_like(q2)), k2)
                    s = s + bias
                    m = jnp.max(s, axis=1, keepdims=True)
                    e = jnp.exp(s - m)
                    total = jnp.sum(e, axis=1, keepdims=True)
                    outs.append(dot(e.astype(bf16), v2) / total)
                    stats = jnp.where(lane == 2 * hp + a, m + jnp.log(total), stats)
                av[rows, ls] = jnp.where(lane < 64, outs[0], outs[1]).astype(bf16)
                lv[rows, :] = stats
                return carry

            lax.fori_loop(0, ns * (HEADS // 2), pair, 0)

        lv[...] = jnp.zeros((HALF, 128), f32)

        @pl.when(nk == 1)
        def _():
            clear_block(1)

        @pl.when(nk == 3)
        def _():
            clear_block(3)

        sends = Copies(osem)
        sends.add(qv, st.at[QS, mb])
        sends.add(kvv, kv.at[0, mb])
        sends.add(vv, kv.at[1, mb])
        for j in range(2):
            sends.add(xv.at[block_rows(c + 2 * j)], st.at[XS, mb, pl.ds(j * BLK, BLK)])
        pl.when(nk > 2)(lambda: attend(SEQ_LEN))
        pl.when(nk <= 2)(lambda: attend(HALF))
        wcopies[3].wait()

        def out_block(j, carry):
            rows = block_rows(j)
            branch = dot(av[rows, :], wv[:, 3 * D : 4 * D])
            live = live_column(BLK, c, length, j * BLK)
            x = xv[block_rows(c + 2 * j), :].astype(f32)
            ov[rows, :] = (x + jnp.where(live, gat * branch, 0.0)).astype(bf16)
            bv[rows, :] = branch.astype(bf16)
            return carry

        lax.fori_loop(0, ns, out_block, 0)
        sends.add(ov, out)
        sends.add(av, st.at[AT, mb])
        sends.add(bv, st.at[BR, mb])
        sends.add(lv, lse.at[mb])
        sends.wait()


def load_ff_weights(c, role, w1, wx_own, wx_oth, near, far, rows2, w1v, w2v, sem):
    quarter = FF // 4
    base = jnp.where(role == 2, 2, 0)

    def cols(part):
        return pl.ds(pl.multiple_of(part * quarter, quarter), quarter)

    def load_down(source, part):
        pltpu.make_async_copy(source, w2v.at[cols(part)], sem.at[4 + part]).start()

    ups = []
    for part in range(4):
        at = pl.ds(part * quarter, quarter)
        ups.append(load_shared(c, role == 2, w1, wx_own, wx_oth, at, w1v, sem.at[part]))
        if part < 2:
            load_down(rows2.at[cols(part)], 2 - base + part)
        if part == 0:
            for pick, halves in ((role == 1, near), (role != 1, far)):

                @pl.when(pick)
                def _():
                    load_down(halves[0], base + c)
                    load_down(halves[1], base + 1 - c)

    def wait(part):
        pltpu.make_async_copy(w1.at[:, cols(part)], w1v.at[:, cols(part)], sem.at[part]).wait()
        pltpu.make_async_copy(near[0], w2v.at[cols(part)], sem.at[4 + part]).wait()

    return wait


def gelu_parts(u):
    u2 = u * u
    t = jnp.tanh(0.7978845608028654 * (u * (1.0 + 0.044715 * u2)))
    return t, u2


def ff_f_kernel(sc, tt, hop, here, w1, wx_own, wx_oth, prt1_own, prt_own, prt1_oth, prt_oth, rows2,
                mod, st_i,
                out, st, xv, nv, w1v, w2v, ov, bv, accv, sem, osem):
    role = sc[0]
    mb = tt[role]

    @pl.when(mb >= 0)
    def _():
        c, length = sc[1], sc[2 + mb]
        _, ns = counts(length, c)
        load = pltpu.make_async_copy(hop, xv, sem.at[8])
        pl.when(role == 1)(lambda: load.start())
        pl.when(role != 1)(lambda: pltpu.make_async_copy(here, xv, sem.at[8]).start())
        wait = load_ff_weights(
            c, role, w1, wx_own, wx_oth, (prt1_own, prt1_oth), (prt_own, prt_oth), rows2, w1v, w2v, sem
        )
        off, scl, gat = mod[mb, 0:1, :], 1.0 + mod[mb, 1:2, :], mod[mb, 2:3, :]
        load.wait()
        sends = Copies(osem)
        sends.add(xv, st.at[XF, mb])

        def norm_block(j, carry):
            rows = block_rows(j)
            n, _ = norm_parts(xv[rows, :].astype(f32))
            nv[rows, :] = (n * scl + off).astype(bf16)
            return carry

        lax.fori_loop(0, ns, norm_block, 0)

        accv[...] = jnp.zeros((HALF, D), f32)

        def step(part, carry):
            wait(part)
            at = pl.ds(pl.multiple_of(part * D, D), D)

            def block(j, carry):
                rows = block_rows(j)
                u = dot(nv[rows, :], w1v[:, at])
                t, _ = gelu_parts(u)
                accv[rows, :] += dot((0.5 * u * (1.0 + t)).astype(bf16), w2v[at, :])
                return carry

            return lax.fori_loop(0, ns, block, carry)

        lax.fori_loop(0, 4, step, 0)

        def last(j, carry):
            rows = block_rows(j)
            acc = accv[rows, :]
            live = live_column(BLK, c, length, j * BLK)
            x = xv[rows, :].astype(f32)
            ov[rows, :] = (x + jnp.where(live, gat * acc, 0.0)).astype(bf16)
            bv[rows, :] = acc.astype(bf16)
            return carry

        lax.fori_loop(0, ns, last, 0)
        sends.add(ov, out)
        sends.add(bv, st.at[BF, mb])
        sends.wait()


def ff_b_kernel(sc, tt, hop, own_c, rcv_c, w1, wx_own, wx_oth, prt1_own, prt_own, prt1_oth, prt_oth,
                rows2, mod,
                 st_i, y_i, act_i, dm_i,
                out, st, y, act, dm,
                xv, gv, brv, nv, gbv, w1v, w2v, duv, actv, ov, dmv, accv, sem, osem):
    role = sc[0]
    mb = tt[role]

    @pl.when(mb >= 0)
    def _():
        c, length, idx = sc[1], sc[2 + mb], sc[6 + mb]
        _, ns = counts(length, c)
        mine = lax.rem(mb, 2) == c

        @pl.when(role == 1)
        def _():
            pltpu.make_async_copy(hop, gv, sem.at[8]).start()

        for pick, source in ((mine, own_c), (jnp.logical_not(mine), rcv_c)):

            @pl.when((role != 1) & pick)
            def _():
                for j in range(2):
                    pltpu.make_async_copy(
                        source.at[idx, block_rows(c + 2 * j)], gv.at[pl.ds(j * BLK, BLK)], sem.at[8]
                    ).start()

        loads = [
            pltpu.make_async_copy(st.at[XF, mb], xv, sem.at[9]),
            pltpu.make_async_copy(st.at[BF, mb], brv, sem.at[10]),
        ]
        for copy in loads:
            copy.start()
        wait = load_ff_weights(
            c, role, w1, wx_own, wx_oth, (prt1_own, prt1_oth), (prt_own, prt_oth), rows2, w1v, w2v, sem
        )
        off, scl, gat = mod[mb, 0:1, :], 1.0 + mod[mb, 1:2, :], mod[mb, 2:3, :]
        dmv[...] = jnp.zeros((8, D), f32)
        pltpu.make_async_copy(hop, gv, sem.at[8]).wait()
        for copy in loads:
            copy.wait()

        def norm_block(j, carry):
            rows = block_rows(j)
            n, _ = norm_parts(xv[rows, :].astype(f32))
            nv[rows, :] = (n * scl + off).astype(bf16)
            live = live_column(BLK, c, length, j * BLK)
            gl = jnp.where(live, gv[rows, :].astype(f32), 0.0)
            gbv[rows, :] = (gl * gat).astype(bf16)
            dmv[2:3, :] += jnp.sum(gl * brv[rows, :].astype(f32), axis=0, keepdims=True)
            return carry

        lax.fori_loop(0, ns, norm_block, 0)
        sends = Copies(osem)
        sends.add(nv, st.at[NF, mb])
        sends.add(gbv, st.at[GB, mb])

        accv[...] = jnp.zeros((HALF, D), f32)

        def step(part, carry):
            wait(part)
            cols = pl.ds(pl.multiple_of(part * D, D), D)

            def block(j, carry):
                rows = block_rows(j)
                u = dot(nv[rows, :], w1v[:, cols])
                t, u2 = gelu_parts(u)
                half = 0.5 * (1.0 + t)
                actv[rows, cols] = (u * half).astype(bf16)
                slope = half + 0.5 * u * (1.0 - t * t) * (
                    0.7978845608028654 * (1.0 + 3 * 0.044715 * u2)
                )
                du = (dot_nt(gbv[rows, :], w2v[cols, :]) * slope).astype(bf16)
                duv[rows, cols] = du
                accv[rows, :] += dot_nt(du, w1v[:, cols])
                return carry

            return lax.fori_loop(0, ns, block, carry)

        lax.fori_loop(0, 4, step, 0)

        def last(j, carry):
            rows = block_rows(j)
            acc = accv[rows, :]
            n, rstd = norm_parts(xv[rows, :].astype(f32))
            dmv[0:1, :] += jnp.sum(acc, axis=0, keepdims=True)
            dmv[1:2, :] += jnp.sum(acc * n, axis=0, keepdims=True)
            ov[rows, :] = (gv[rows, :].astype(f32) + norm_back(acc, n, rstd, scl)).astype(bf16)
            return carry

        lax.fori_loop(0, ns, last, 0)
        sends.add(ov, out)
        sends.add(duv, y.at[mb])
        sends.add(actv, act.at[mb])
        sends.add(dmv, dm.at[mb])
        sends.wait()


def att_b1_kernel(sc, tt, hop0, here2, here3, w, wx_own, wx_oth, mod, kv, lse, st_i, y_i,
                  own, snd, st, y,
                  gv, atv, qv, kvv, vv, wo, lv, gbv, dov, dqv, dkt, dvt, sem, osem):
    role = sc[0]
    mb = tt[role]

    @pl.when(mb >= 0)
    def _():
        c, length = sc[1], sc[2 + mb]
        nk, ns = counts(length, c)
        for who, hop in ((0, hop0), (2, here2), (3, here3)):
            pl.when(role == who)(lambda: pltpu.make_async_copy(hop, gv, sem.at[0]).start())
        out_weight = load_shared(
            c, role == 3, w, wx_own, wx_oth, pl.ds(3 * D, D), wo, sem.at[1], pl.ds(0, D)
        )
        loads = [
            pltpu.make_async_copy(st.at[QS, mb], qv, sem.at[2]),
            pltpu.make_async_copy(kv.at[0, mb], kvv, sem.at[3]),
            pltpu.make_async_copy(kv.at[1, mb], vv, sem.at[4]),
            pltpu.make_async_copy(st.at[AT, mb], atv, sem.at[5]),
            pltpu.make_async_copy(lse.at[mb], lv, sem.at[6]),
        ]
        for copy in loads:
            copy.start()
        gat = mod[mb, 2:3, :]
        pltpu.make_async_copy(hop0, gv, sem.at[0]).wait()
        out_weight.wait()

        def grad_block(j, carry):
            rows = block_rows(j)
            live = live_column(BLK, c, length, j * BLK)
            gb = jnp.where(live, gv[rows, :].astype(f32) * gat, 0.0).astype(bf16)
            gbv[rows, :] = gb
            dov[rows, :] = dot_nt(gb, wo[...]).astype(bf16)
            return carry

        lax.fori_loop(0, ns, grad_block, 0)
        sends = Copies(osem)
        sends.add(gbv, y.at[mb, :, pl.ds(3 * D, D)])
        for copy in loads:
            copy.wait()

        def attend(rows, keys):
            lane = lax.broadcasted_iota(i32, (rows, 128), 1)
            position = lax.broadcasted_iota(i32, (1, keys), 1)
            bias = jnp.where(position < length, 0.0, -1e30).astype(f32)

            def pair(hp, carry):
                ls = lanes(hp)
                k2, v2 = kvv[0:keys, ls], vv[0:keys, ls]
                q2, do2 = qv[0:rows, ls], dov[0:rows, ls]
                q2t, do2t = q2.T, do2.T
                both = do2.astype(f32) * atv[0:rows, ls].astype(f32)
                stats = lv[0:rows, :]
                dqs = []
                for a in range(2):
                    head = (lane < 64) == (a == 0)
                    zero = jnp.zeros_like(q2)
                    s = dot_nt(jnp.where(head, q2, zero), k2) + bias
                    base = jnp.sum(jnp.where(lane == 2 * hp + a, stats, 0.0), axis=1, keepdims=True)
                    p = jnp.exp(s - base)
                    dp = dot_nt(jnp.where(head, do2, zero), v2)
                    delta = jnp.sum(jnp.where(head, both, 0.0), axis=1, keepdims=True)
                    ds = (p * (dp - delta)).astype(bf16)
                    dqs.append(dot(ds, k2))
                    at = pl.ds(pl.multiple_of(hp * 128 + a * 64, 64), 64)
                    dkt[at, 0:keys] = dot(q2t[a * 64 : (a + 1) * 64, :], ds).astype(bf16)
                    dvt[at, 0:keys] = dot(do2t[a * 64 : (a + 1) * 64, :], p.astype(bf16)).astype(
                        bf16
                    )
                dqv[0:rows, ls] = jnp.where(lane < 64, dqs[0], dqs[1]).astype(bf16)
                return carry

            lax.fori_loop(0, HEADS // 2, pair, 0)

        @pl.when((ns == 1) & (nk > 2))
        def _():
            zero = jnp.zeros((BLK, D), bf16)
            qv[BLK:HALF, :], atv[BLK:HALF, :], dov[BLK:HALF, :] = zero, zero, zero
            lv[BLK:HALF, :] = jnp.zeros((BLK, 128), f32)

        pl.when(nk > 2)(lambda: attend(HALF, SEQ_LEN))
        pl.when((ns == 1) & (nk <= 2))(lambda: attend(BLK, HALF))

        @pl.when(ns == 0)
        def _():
            dkt[:, 0:BLK] = jnp.zeros((D, BLK), bf16)
            dvt[:, 0:BLK] = jnp.zeros((D, BLK), bf16)

        sends.add(dqv, st.at[DQ, mb])
        for part, grad in enumerate((dkt, dvt)):
            for j in range(2):
                cols = pl.ds(j * BLK, BLK)
                sends.add(grad.at[:, block_rows(c + 2 * j)], own.at[part, :, cols])
                sends.add(grad.at[:, block_rows(1 - c + 2 * j)], snd.at[part, :, cols])
        sends.wait()


def att_b2_kernel(sc, tt, hop0, here2, here3, own, rcv0, rcv2, rcv3, w, wx_own, wx_oth, cos, sin, mod, st_i, y_i, dm_i,
                  out, st, y, dm,
                  gv, xv, brv, dqv, ownv, rcvv, wv, cv, sv, nv, dpv, ov, dmv, sem, osem):
    role = sc[0]
    mb = tt[role]

    @pl.when(mb >= 0)
    def _():
        c, length = sc[1], sc[2 + mb]
        _, ns = counts(length, c)
        for who, hop, rcv in ((0, hop0, rcv0), (2, here2, rcv2), (3, here3, rcv3)):

            @pl.when(role == who)
            def _():
                pltpu.make_async_copy(hop, gv, sem.at[0]).start()
                pltpu.make_async_copy(rcv, rcvv, sem.at[2]).start()

        loads = [
            pltpu.make_async_copy(own, ownv, sem.at[1]),
            pltpu.make_async_copy(st.at[DQ, mb], dqv, sem.at[3]),
            pltpu.make_async_copy(st.at[XS, mb], xv, sem.at[4]),
            pltpu.make_async_copy(st.at[BR, mb], brv, sem.at[5]),
            pltpu.make_async_copy(cos, cv, sem.at[6]),
            pltpu.make_async_copy(sin, sv, sem.at[7]),
        ]
        for copy in loads:
            copy.start()
        in_weight = load_shared(c, role == 3, w, wx_own, wx_oth, pl.ds(0, 3 * D), wv, sem.at[8])
        off, scl = mod[mb, 0:1, :], 1.0 + mod[mb, 1:2, :]
        dmv[...] = jnp.zeros((8, D), f32)
        pltpu.make_async_copy(hop0, gv, sem.at[0]).wait()
        pltpu.make_async_copy(rcv0, rcvv, sem.at[2]).wait()
        for copy in loads:
            copy.wait()

        def first(j, carry):
            rows, nat = block_rows(j), block_rows(c + 2 * j)
            cosine, sine = cv[nat, :], -sv[nat, :]
            for p in range(6):
                ls = slice(p * 128, (p + 1) * 128)
                dpv[rows, ls] = (turn(dqv[rows, ls].astype(f32), cosine, sine) * 0.125).astype(bf16)
                for part in range(2):
                    total = ownv[part, ls, rows].astype(f32) + rcvv[part, ls, rows].astype(f32)
                    grad = total.T
                    if part == 0:
                        grad = turn(grad.astype(bf16).astype(f32), cosine, sine)
                    dpv[rows, (part + 1) * D + p * 128 : (part + 1) * D + (p + 1) * 128] = (
                        grad.astype(bf16)
                    )
            return carry

        lax.fori_loop(0, ns, first, 0)
        sends = Copies(osem)
        sends.add(dpv, y.at[mb, :, pl.ds(0, 3 * D)])
        in_weight.wait()

        def second(j, carry):
            rows = block_rows(j)
            acc = dot_nt(dpv[rows, :], wv[...])
            n, rstd = norm_parts(xv[rows, :].astype(f32))
            nv[rows, :] = (n * scl + off).astype(bf16)
            g = gv[rows, :].astype(f32)
            live = live_column(BLK, c, length, j * BLK)
            gl = jnp.where(live, g, 0.0)
            dmv[0:1, :] += jnp.sum(acc, axis=0, keepdims=True)
            dmv[1:2, :] += jnp.sum(acc * n, axis=0, keepdims=True)
            dmv[2:3, :] += jnp.sum(gl * brv[rows, :].astype(f32), axis=0, keepdims=True)
            ov[rows, :] = (g + norm_back(acc, n, rstd, scl)).astype(bf16)
            return carry

        lax.fori_loop(0, ns, second, 0)
        sends.add(ov, out)
        sends.add(nv, st.at[NM, mb])
        sends.add(dmv, dm.at[mb])
        sends.wait()


def weight_grad_kernel(kind, sc, tt, st, y, out, xv, xt, yv, acc, ov, xsem, ysem, osem):
    chosen, c = tt[sc[0]], sc[1]

    def tile(j):
        return y.at[:, :, pl.ds(pl.multiple_of(j * D, D), D)]

    def into(j):
        at = pl.ds(pl.multiple_of(j * D, D), D)
        return out.at[at] if kind == "down" else out.at[:, at]

    def load_x(which):
        return pltpu.make_async_copy(st.at[which], xv, xsem.at[0])

    def load_y(j):
        slot = lax.rem(j, 2)
        return pltpu.make_async_copy(tile(j), yv.at[slot], ysem.at[slot])

    def store(j):
        slot = lax.rem(j, 2)
        return pltpu.make_async_copy(ov.at[slot], into(j), osem.at[slot])

    def live(mb):
        _, ns = counts(sc[2 + mb], c)
        picked = lax.rem(lax.shift_right_logical(chosen, mb), 2) == 1
        return jnp.where(picked, ns, 0)

    def transpose_rows(x):
        def step(mb, carry):
            def block(j, carry):
                xt[:, block_rows(2 * mb + j)] = x[mb, block_rows(j), :].T
                return carry

            return lax.fori_loop(0, live(mb), block, carry)

        lax.fori_loop(0, MB, step, 0)

    @pl.when(chosen > 0)
    def _():
        first = GB if kind == "down" else NM if kind == "attention" else NF
        load_x(first).start()
        load_y(0).start()
        load_x(first).wait()
        if kind != "down":
            transpose_rows(xv)
        if kind == "attention":
            load_x(AT).start()

        def step(j, carry):
            slot = lax.rem(j, 2)
            pl.when(j < 3)(lambda: load_y(j + 1).start())
            load_y(j).wait()
            if kind == "down":
                transpose_rows(yv.at[slot])
            if kind == "attention":

                @pl.when(j == 3)
                def _():
                    load_x(AT).wait()
                    transpose_rows(xv)

            acc[...] = jnp.zeros((D, D), f32)

            def add(mb, carry):
                for slots in (1, 2):

                    @pl.when(live(mb) == slots)
                    def _():
                        at = pl.ds(pl.multiple_of(mb * HALF, HALF), slots * BLK)
                        if kind == "down":
                            right = xv[mb, 0 : slots * BLK, :]
                        else:
                            right = yv[slot, mb, 0 : slots * BLK, :]
                        acc[...] += dot(xt[:, at], right)

                return carry

            lax.fori_loop(0, MB, add, 0)
            pl.when(j >= 2)(lambda: store(j - 2).wait())
            ov[slot] = acc[...].astype(bf16)
            store(j).start()
            return carry

        lax.fori_loop(0, 4, step, 0)
        store(2).wait()
        store(3).wait()


def reduce_kernel(roles, chips, mine, theirs, *refs):
    count, kept = len(mine[0]) + len(theirs[0]), len(mine[0])
    arrays, outs = refs[:count], refs[count : count + kept]
    near, total = refs[count + kept : 2 * count + kept], refs[2 * count + kept : 3 * count + kept]
    refs = refs[3 * count + kept :]
    paired = len(theirs[0]) > 0
    cross, refs = (refs[:kept], refs[kept:]) if paired else ((), refs)
    gathered, result, refs = refs[:kept], refs[kept : 2 * kept], refs[2 * kept :]
    load_sem, near_send, near_recv, cross_send, cross_recv, far_send, far_recv, out_sem = refs
    seg, dp = lax.axis_index("segment"), lax.axis_index("dp")
    core, place = lax.rem(dp, 2), lax.div(dp, 2)

    def device(segment, chip, at):
        return {"segment": segment, "dp": 2 * chip + at}

    def remote(src, dst, send, recv, target):
        return pltpu.make_async_remote_copy(
            src_ref=src, dst_ref=dst, send_sem=send, recv_sem=recv,
            device_id=target, device_id_type=pl.DeviceIdType.MESH,
        )

    def work(role, other, keep, give):
        barrier = pltpu.get_barrier_semaphore()
        peers = [device(role, place, 1 - core)]
        peers += [device(role, lax.rem(place + k, chips), core) for k in range(1, chips)]
        if paired:
            peers.append(device(other, place, core))
        for peer in peers:
            pl.semaphore_signal(
                barrier, inc=1, device_id=peer, device_id_type=pl.DeviceIdType.MESH
            )
        pl.semaphore_wait(barrier, len(peers))

        order = [lax.rem(place + k, chips) for k in range(1, chips)] + [place]
        nears, loads = [], []
        for z in range(chips):
            for k, at in enumerate(keep + give):
                to = remote(
                    arrays[at].at[2 * z + 1 - core], near[k].at[z],
                    near_send.at[k, z], near_recv.at[k, z], device(role, place, 1 - core),
                )
                to.start()
                nears.append(to)
                load = pltpu.make_async_copy(
                    arrays[at].at[2 * z + core], total[k].at[z], load_sem.at[k, z]
                )
                load.start()
                loads.append(load)
        crossing = []
        for z in range(chips):
            for k in list(range(kept, count)) + list(range(kept)):
                loads[z * count + k].wait()
                nears[z * count + k].wait()
                total[k][z] = total[k][z] + near[k][z]
                if k >= kept:
                    to = remote(
                        total[k].at[z], cross[k - kept].at[z],
                        cross_send.at[k - kept, z], cross_recv.at[k - kept, z],
                        device(other, place, core),
                    )
                    to.start()
                    crossing.append(to)
        far = []
        for z in range(chips):
            for k in range(kept):
                if paired:
                    crossing[z * kept + k].wait()
                    total[k][z] = total[k][z] + cross[k][z]
                far.append(
                    remote(
                        total[k].at[z], gathered[k].at[place],
                        far_send.at[k, z], far_recv.at[k, place], device(role, z, core),
                    )
                )
                pl.when(place != z)(far[-1].start)
        for k in range(kept):
            result[k][...] = total[k][place].astype(f32)
        for z in order[:-1]:
            for k in range(kept):
                remote(
                    total[k].at[z], gathered[k].at[z],
                    far_send.at[k, z], far_recv.at[k, z], device(role, z, core),
                ).wait_recv()
                result[k][...] += gathered[k][z].astype(f32)
        copies = []
        for k in range(kept):
            copies.append(pltpu.make_async_copy(result[k], outs[k], out_sem.at[k]))
            copies[-1].start()
        for z in range(chips):
            for k in range(kept):
                pl.when(place != z)(far[z * kept + k].wait_send)
        for copy in copies:
            copy.wait()

    for index, role in enumerate(roles):
        other = roles[1 - index] if paired else role
        pl.when(seg == role)(functools.partial(work, role, other, mine[index], theirs[index]))


def gather_kernel(size, rows, out, own_sem, send, recv):
    seg, dp = lax.axis_index("segment"), lax.axis_index("dp")

    def peer(k):
        return {"segment": seg, "dp": lax.rem(dp + k, size)}

    barrier = pltpu.get_barrier_semaphore()
    for k in range(1, size):
        pl.semaphore_signal(
            barrier, inc=1, device_id=peer(k), device_id_type=pl.DeviceIdType.MESH
        )
    pl.semaphore_wait(barrier, size - 1)
    own = pltpu.make_async_copy(rows, out.at[dp], own_sem)
    own.start()

    def copy(k, slot):
        return pltpu.make_async_remote_copy(
            src_ref=rows, dst_ref=out.at[slot], send_sem=send.at[k], recv_sem=recv.at[slot],
            device_id=peer(k), device_id_type=pl.DeviceIdType.MESH,
        )

    for k in range(1, size):
        copy(k, dp).start()
    own.wait()
    for k in range(1, size):
        copy(k, dp).wait_send()
        copy(k, lax.rem(dp + k, size)).wait_recv()


def gathered_rows(rows, size, number):
    return pl.pallas_call(
        functools.partial(gather_kernel, size),
        out_shape=jax.ShapeDtypeStruct((size, *rows.shape), rows.dtype),
        in_specs=[VMEM],
        out_specs=VMEM,
        scratch_shapes=[
            pltpu.SemaphoreType.DMA,
            pltpu.SemaphoreType.DMA((size,)),
            pltpu.SemaphoreType.DMA((size,)),
        ],
        compiler_params=pltpu.CompilerParams(
            vmem_limit_bytes=VLIM, collective_id=number, has_side_effects=True
        ),
        name="gather_sums",
    )(rows)


def reduced(arrays, roles, mine, theirs, chips, number, name):
    dims = [a.shape[1:] for a in arrays]
    kept, count = len(mine[0]), len(mine[0]) + len(theirs[0])
    order = mine[0] + theirs[0]
    every = [vm((chips, *dims[k])) for k in order]
    keeps = [vm((chips, *dims[k])) for k in mine[0]]
    pairs = pltpu.SemaphoreType.DMA((count, chips))
    return pl.pallas_call(
        functools.partial(reduce_kernel, roles, chips, mine, theirs),
        out_shape=[jax.ShapeDtypeStruct(dims[k], f32) for k in mine[0]],
        in_specs=[ANY] * len(arrays),
        out_specs=[ANY] * kept,
        scratch_shapes=every + every + (keeps if theirs[0] else []) + keeps
        + [vm(dims[k], f32) for k in mine[0]]
        + [pairs] * 7 + [pltpu.SemaphoreType.DMA((kept,))],
        compiler_params=pltpu.CompilerParams(
            vmem_limit_bytes=VLIM, collective_id=number, has_side_effects=True
        ),
        cost_estimate=cost(60),
        name=name,
    )(*arrays)


ANY = pl.BlockSpec(memory_space=pl.ANY)
VMEM = pl.BlockSpec(memory_space=pltpu.VMEM)


def shape(dims, dtype=bf16):
    return jax.ShapeDtypeStruct(dims, dtype)


ROWS = shape((HALF, D))
ST = shape((10, MB, HALF, D))
KV = shape((2, MB, SEQ_LEN, D))
LSE = shape((MB, HALF, 128), f32)
YS = shape((MB, HALF, FF))
DM = shape((MB, 8, D), f32)
DKV = shape((2, D, HALF))


def vm(dims, dtype=bf16):
    return pltpu.VMEM(dims, dtype)


HV, FV = vm((HALF, D)), vm((SEQ_LEN, D))


def cost(micros):
    return pl.CostEstimate(flops=int(micros * 1e9), bytes_accessed=1 << 20, transcendentals=0)


def call(kernel, scalars, operands, vmem_at, outs, aliases, scratch, sems, name, micros):
    specs = [VMEM if i in vmem_at else ANY for i in range(len(operands))]
    return pl.pallas_call(
        kernel,
        grid_spec=pltpu.PrefetchScalarGridSpec(
            num_scalar_prefetch=2,
            grid=(1,),
            in_specs=specs,
            out_specs=[ANY] * len(outs),
            scratch_shapes=list(scratch)
            + [pltpu.SemaphoreType.DMA((11,)), pltpu.SemaphoreType.DMA((sems,))],
        ),
        out_shape=list(outs),
        input_output_aliases={i + 2: o for i, o in aliases.items()},
        compiler_params=pltpu.CompilerParams(vmem_limit_bytes=VLIM),
        cost_estimate=cost(micros),
        name=name,
    )(*scalars, *operands)


def allocate(outs):
    return pl.pallas_call(
        lambda *refs: None,
        out_shape=list(outs),
        out_specs=[ANY] * len(outs),
        name="allocate",
    )()


def time_cond(steps):
    half_width = D // 2
    frequency = jnp.exp(
        jnp.arange(half_width, dtype=f32) * (-math.log(10000.0) / half_width)
    )
    angles = steps.astype(f32)[:, None] * frequency[None, :]
    return jax.nn.silu(jnp.concatenate([jnp.cos(angles), jnp.sin(angles)], axis=1))


def rope_tables():
    inverse = np.exp(np.arange(32, dtype=np.float32) * np.float32(-math.log(10000.0) / 32))
    angles = np.arange(SEQ_LEN, dtype=np.float32)[:, None] * inverse[None, :]
    cosine, sine = np.cos(angles), np.sin(angles)
    return (
        np.concatenate([cosine] * 4, axis=1).astype(np.float32),
        np.concatenate([-sine, sine, -sine, sine], axis=1).astype(np.float32),
    )


def local(block_input, cotangent, lengths, steps, mod_weight, mod_bias, first_weight, down_rows):
    ndp = lax.axis_size("dp")
    seg, dp = lax.axis_index("segment"), lax.axis_index("dp")
    core, chips, place = dp % 2, ndp // 2, dp // 2
    w, rows2 = first_weight[0], down_rows[0]

    def across(value, moves):
        pairs = [
            (r * ndp + 2 * i + c, q * ndp + 2 * i + e) for (r, c), (q, e) in moves for i in range(chips)
        ]
        return lax.ppermute(value, ("segment", "dp"), pairs)

    def swap(value, roles=(0, 1, 2, 3)):
        return across(value, [((r, c), (r, 1 - c)) for r in roles for c in range(2)])

    def hop(value, pairs):
        return lax.ppermute(value, "segment", pairs)

    def after(value, other):
        return lax.optimization_barrier((value, other))[0]

    quarter = FF // 4
    rows_half = lax.dynamic_slice_in_dim(rows2, core * quarter, quarter, axis=0)
    prt1 = hop(rows_half, [(0, 1)])
    full = (lengths[1] > lengths[0]).astype(i32)
    block_input = after(block_input, rows_half)
    other_info = swap(jnp.stack([lengths, steps]))
    other_full = swap(lax.dynamic_index_in_dim(block_input, full, keepdims=False), (0,))
    info = jnp.stack([lengths, steps])
    info0 = jnp.where(core == 0, info, other_info)
    info1 = jnp.where(core == 0, other_info, info)
    full0 = (info0[0, 1] > info0[0, 0]).astype(i32)
    full1 = (info1[0, 1] > info1[0, 0]).astype(i32)
    places = jnp.stack([full0, full1, 1 - full0, 1 - full1])
    chip = jnp.stack([info0[:, full0], info1[:, full1], info0[:, 1 - full0], info1[:, 1 - full1]])
    sc = jnp.concatenate([jnp.stack([seg, core]), chip[:, 0], places, jnp.zeros((6,), i32)]).astype(i32)
    conditions = time_cond(chip[:, 1]).astype(bf16)
    modulation = jnp.dot(conditions, mod_weight[0], preferred_element_type=f32)
    modulation = modulation + mod_bias[0].astype(f32)
    mod = jnp.pad(modulation.reshape(MB, 3, D), ((0, 0), (0, 5), (0, 0)))
    cos, sin = (jnp.asarray(t) for t in rope_tables())
    st, kv, lse, y, yf, act, dma, dmf, blank = allocate([ST, KV, LSE, YS, YS, YS, DM, DM, ROWS])

    w_half = lax.dynamic_slice_in_dim(after(w, rows_half), core * (D // 2), D // 2, axis=0)
    prt23 = hop(rows_half, [(2, 3), (3, 2)])
    wx_own = hop(w_half, [(2, 3), (3, 2)])
    prt_own = (prt1, prt23)
    wx_oth, prt_oth = wx_own, prt_own
    other_full = after(other_full, prt1)

    other_mod = hop(mod, [(2, 3), (3, 2)])
    mod_att = jnp.where(seg == 3, other_mod, mod)
    mod_ff = jnp.where(seg == 2, other_mod, mod)

    def table(turns):
        return np.array([turns.get(r, -1) for r in range(4)], np.int32)

    def att_f(turns, from2, from3, short, st, kv, lse):
        return call(
            att_f_kernel,
            (sc, table(turns)),
            (*from2, *from3, block_input, other_full, short, w, wx_own, wx_oth, cos, sin, mod_att,
             st, kv, lse),
            (12,),
            (ROWS, ST, KV, LSE),
            {13: 1, 14: 2, 15: 3},
            (FV, FV, vm((D, FF)), FV, FV, HV, HV, HV, HV, vm((HALF, 128), f32),
             vm((SEQ_LEN, 128), f32), vm((SEQ_LEN, 128), f32)),
            9,
            "attention_forward",
            20,
        )

    def ff_f(turns, x, here, st):
        return call(
            ff_f_kernel,
            (sc, table(turns)),
            (x, here, w, wx_own, wx_oth, *prt_own, *prt_oth, rows2, mod_ff, st),
            (10,),
            (ROWS, ST),
            {11: 1},
            (HV, HV, vm((D, FF)), vm((FF, D)), HV, HV, vm((HALF, D), f32)),
            3,
            "feedforward_forward",
            10,
        )

    def ff_b(turns, g, st, yf, act, dm):
        return call(
            ff_b_kernel,
            (sc, table(turns)),
            (g, cotangent, other_c, w, wx_own, wx_oth, *prt_own, *prt_oth, rows2, mod_ff, st, yf, act,
             dm),
            (11,),
            (ROWS, ST, YS, YS, DM),
            {12: 1, 13: 2, 14: 3, 15: 4},
            (HV, HV, HV, HV, HV, vm((D, FF)), vm((FF, D)), vm((HALF, FF)), vm((HALF, FF)), HV,
             vm((8, D), f32), vm((HALF, D), f32)),
            6,
            "feedforward_backward",
            16,
        )

    def att_b(turns, g0, g2, g3, st, y, dm):
        own, snd, st, y = call(
            att_b1_kernel,
            (sc, table(turns)),
            (g0, g2, g3, w, wx_own, wx_oth, mod_att, kv, lse, st, y),
            (6,),
            (DKV, DKV, ST, YS),
            {9: 2, 10: 3},
            (HV, HV, HV, FV, FV, vm((D, D)), vm((HALF, 128), f32), HV, HV, HV,
             vm((D, SEQ_LEN)), vm((D, SEQ_LEN))),
            10,
            "attention_backward",
            22,
        )
        near = swap(snd, (0,)) if 0 in turns else snd
        far = [swap(snd, (r,)) if r in turns else snd for r in (2, 3)]
        return call(
            att_b2_kernel,
            (sc, table(turns)),
            (g0, g2, g3, own, near, *far, w, wx_own, wx_oth, cos, sin, mod_att, st, y, dm),
            (12,),
            (ROWS, ST, YS, DM),
            {13: 1, 14: 2, 15: 3},
            (HV, HV, HV, HV, vm((2, D, HALF)), vm((2, D, HALF)), vm((D, 3 * D)),
             vm((SEQ_LEN, 128), f32), vm((SEQ_LEN, 128), f32), HV, vm((HALF, 3 * D)), HV,
             vm((8, D), f32)),
            4,
            "projection_backward",
            9,
        )

    depth, wide_rows = D // ndp, FF // 2 // ndp

    def weight_grad(kind, chosen, right):
        turns = np.array([chosen.get(r, 0) for r in range(4)], np.int32)
        pairs = pltpu.SemaphoreType.DMA((2,))
        return pl.pallas_call(
            functools.partial(weight_grad_kernel, kind),
            grid_spec=pltpu.PrefetchScalarGridSpec(
                num_scalar_prefetch=2,
                grid=(1,),
                in_specs=[ANY, ANY],
                out_specs=ANY,
                scratch_shapes=[
                    vm((MB, HALF, D)), vm((D, MB * HALF)), vm((2, MB, HALF, D)), vm((D, D), f32),
                    vm((2, D, D)), pairs, pairs, pairs,
                ],
            ),
            out_shape=shape((FF, D) if kind == "down" else (D, FF)),
            compiler_params=pltpu.CompilerParams(vmem_limit_bytes=VLIM),
            cost_estimate=cost(12),
            name=kind + "_gradient",
        )(sc, turns, st, right)

    def ff_grads(chosen):
        up = weight_grad("up", chosen, yf)
        down = weight_grad("down", chosen, act).reshape(2 * ndp, wide_rows, D)
        return up.reshape(ndp, depth, FF), down[:ndp], down[ndp:]

    def owned(ac, bd):
        keep = jnp.where(core == 0, ac, bd)
        give = jnp.where(core == 0, bd, ac)
        return jnp.where(core == seg % 2, keep, swap(give))

    def spread_last(one, two):
        first_one = across(one[:BLK], [((2, c), (c, c)) for c in range(2)])
        first_two = across(two[:BLK], [((3, c), (c, c)) for c in range(2)])
        mid = jnp.where(seg == 2, one[BLK:], two[BLK:])
        crossed = across(mid, [((2, 1), (3, 1)), ((3, 0), (2, 0))])
        return owned(
            jnp.where(seg < 2, first_one, jnp.where(seg == 2, mid, crossed)),
            jnp.where(seg < 2, first_two, jnp.where(seg == 2, crossed, mid)),
        )

    nothing = (blank, blank)
    a, b, cc, d = range(MB)

    out, st, kv, lse = att_f({0: a}, nothing, nothing, other_full, st, kv, lse)
    hop_a = hop(out, [(0, 1)])
    short = swap(lax.dynamic_index_in_dim(after(block_input, out), 1 - full, keepdims=False), (0,))
    other_c = swap(after(cotangent, out), (2, 3))
    prt_oth = (swap(after(prt1, out), (1,)), prt23)

    out, st, kv, lse = att_f({0: b}, nothing, nothing, other_full, st, kv, lse)
    ff_a, st = ff_f({1: a}, hop_a, blank, st)
    to_a = hop(ff_a, [(1, 2)])
    hop_b = hop(after(out, ff_a), [(0, 1)])
    wx_oth = swap(after(wx_own, ff_a), (2, 3))
    prt_oth = (prt_oth[0], swap(after(prt23, ff_a), (2, 3)))
    short = after(short, hop_b)

    att_a, st, kv, lse = att_f({0: cc, 2: a}, (to_a, swap(to_a, (2,))), nothing, short, st, kv, lse)
    ff_b1, st = ff_f({1: b}, hop_b, blank, st)
    to_b = hop(ff_b1, [(1, 3)])
    hop_c = hop(after(att_a, ff_b1), [(0, 1)])

    att_bb, st, kv, lse = att_f({0: d, 3: b}, nothing, (to_b, swap(to_b, (3,))), short, st, kv, lse)
    out_a, st = ff_f({1: cc, 2: a}, hop_c, att_a, st)
    hop_d = hop(after(att_bb, out_a), [(0, 1)])
    grad_a, st, yf, act, dmf = ff_b({2: a}, blank, st, yf, act, dmf)
    out_b, st = ff_f({1: d, 3: b}, hop_d, att_bb, st)
    to_c = hop(after(out_a, out_b), [(1, 2)])
    grad_b, st, yf, act, dmf = ff_b({3: b}, blank, st, yf, act, dmf)
    to_d = hop(after(out_b, grad_b), [(1, 3)])

    early = spread_last(after(out_a, grad_b), out_b)

    masks = {2: 5, 3: 10}
    back, st, y, dma = att_b({2: a, 3: b}, blank, grad_a, grad_b, st, y, dma)
    back_a = hop(back, [(2, 1)])
    to_c = hop(after(out_a, back), [(1, 2)])
    grad_1a, st, yf, act, dmf = ff_b({1: a}, back_a, st, yf, act, dmf)
    end_a = hop(grad_1a, [(1, 0)])
    back_b = hop(after(back, grad_1a), [(3, 1)])
    to_d = hop(after(out_b, grad_1a), [(1, 3)])
    att_cd, st, kv, lse = att_f(
        {2: cc, 3: d}, (to_c, swap(to_c, (2,))), (to_d, swap(to_d, (3,))), short, st, kv, lse
    )
    out_cd, st = ff_f({2: cc, 3: d}, blank, att_cd, st)
    grad_cd, st, yf, act, dmf = ff_b({1: b, 2: cc, 3: d}, back_b, st, yf, act, dmf)
    end_b = hop(grad_cd, [(1, 0)])
    back, st, y, dma = att_b({0: a, 2: cc, 3: d}, end_a, grad_cd, grad_cd, st, y, dma)
    in_a = back
    back_c = hop(back, [(2, 1)])
    grad_1c, st, yf, act, dmf = ff_b({1: cc}, after(back_c, end_b), st, yf, act, dmf)
    end_c = hop(grad_1c, [(1, 0)])
    back_d = hop(after(back, grad_1c), [(3, 1)])
    grad_1d, st, yf, act, dmf = ff_b({1: d}, after(back_d, end_c), st, yf, act, dmf)
    end_d = hop(grad_1d, [(1, 0)])
    att_23 = weight_grad("attention", masks, y).reshape(ndp, depth, FF)
    up_x, low_x, high_x = ff_grads({1: 15, **masks})
    in_b, st, y, dma = att_b({0: b}, end_b, blank, blank, st, y, dma)
    in_c, st, y, dma = att_b({0: cc}, end_c, blank, blank, st, y, dma)
    in_d, st, y, dma = att_b({0: d}, end_d, blank, blank, st, y, dma)
    att_23, up_x, low_x, high_x, _ = lax.optimization_barrier((att_23, up_x, low_x, high_x, in_d))
    first_23, rows_23 = reduced(
        (att_23, up_x, low_x, high_x), (2, 3), ([0, 2], [1, 3]), ([1, 3], [0, 2]), chips, 1,
        "second_layer_sums",
    )
    up_1, low_1, high_1 = reduced(
        (up_x, low_x, high_x), (1,), ([0, 1, 2],), ([],), chips, 2, "feedforward_sums"
    )
    st, _ = lax.optimization_barrier((st, (first_23, up_1)))
    att_0 = weight_grad("attention", {0: 15}, y).reshape(ndp, depth, FF)
    (first_0,) = reduced((att_0,), (0,), ([0],), ([],), chips, 3, "attention_sums")
    low_0 = hop(after(low_1, first_0), [(1, 0)])
    even = seg % 2 == 0
    first_sum = jnp.where(seg == 0, first_0, jnp.where(seg == 1, up_1, first_23))
    rows_sum = jnp.where(seg == 0, low_0, jnp.where(seg == 1, high_1, rows_23))

    late = spread_last(after(out_cd, up_1), out_cd)
    outs = jnp.stack([early, late])
    halves = after(jnp.stack([in_a, in_c, in_b, in_d]), up_1)
    to_one = across(halves[:, :BLK], [((0, 1), (1, 1))])
    to_others = across(halves[:, BLK:], [((0, 0), (2, 0)), ((0, 1), (3, 1))])
    got = jnp.where(seg == 0, halves[:, :BLK], jnp.where(seg == 1, to_one, to_others))
    grads = owned(got[:2], got[2:])

    mine = np.array([[True] * 4, [True] * 4, [True, False] * 2, [False, True] * 2])
    mine = jnp.asarray(mine)[seg][:, None, None]
    dma, dmf = (jnp.where(mine, m[:, :3], 0.0) for m in (dma, dmf))
    sums = jnp.where(even, dma, dmf) + hop(jnp.where(even, dmf, dma), [(2, 3), (3, 2)])
    mod_rows = jnp.concatenate([sums.reshape(MB, 3 * D), conditions.astype(f32)], axis=1)
    all_rows = gathered_rows(mod_rows.reshape(-1, 128), ndp, 4).reshape(ndp * MB, 4 * D)
    mine = lax.dynamic_slice_in_dim(all_rows, 3 * D + dp * depth, depth, axis=1)
    all_rows = all_rows[:, : 3 * D]
    mod_w_sum = jnp.dot(mine.T, all_rows, precision=lax.Precision.HIGHEST, preferred_element_type=f32)
    width = 3 * D // ndp
    mod_b_sum = jnp.sum(lax.dynamic_slice_in_dim(all_rows, dp * width, width, axis=1), axis=0)

    def placed(both, part):
        both = jnp.where(full == 0, both, both[::-1])
        live = (seg * BLK + jnp.arange(BLK))[None, :, None] < lengths[:, None, None]
        return jnp.where(live, both, lax.dynamic_slice_in_dim(part, seg * BLK, BLK, axis=1))

    return (
        placed(outs, block_input),
        placed(grads, cotangent).astype(f32),
        mod_w_sum[None],
        mod_b_sum[None],
        first_sum.astype(f32)[None],
        rows_sum.astype(f32)[None],
    )


def solution(mesh):
    in_specs = (
        P("dp", None, None),
        P("dp", None, None),
        P("dp"),
        P("dp"),
        P("segment", None, None),
        P("segment", None),
        P("segment", None, None),
        P("segment", None, None),
    )
    out_specs = (
        P("dp", "segment", None),
        P("dp", "segment", None),
        P("segment", "dp", None),
        P("segment", "dp"),
        P("segment", "dp", None),
        P("segment", "dp", None),
    )
    return jax.shard_map(local, mesh=mesh, in_specs=in_specs, out_specs=out_specs, check_vma=False)
```

time: 872 us -> 750 us (0.86)
  waiting for transfers between devices: 314 us -> 194 us
  starting transfers between devices: 54.4 us -> 117 us
  blocking collectives: 26.5 us -> 0 us
  Pallas kernels: 372 us -> 355 us
  between operations: 19.1 us -> 6.3 us
    pallas_call x32 -> x26, Pallas kernels: 344 us -> 216 us  [call(): pl.pallas_call(kernel, grid_spec=pltpu.PrefetchScalarGridSpec(num_scalar_...]
    pallas_call x2 -> x8, Pallas kernels: 27.3 us -> 138 us  [the longest x3 68.6 us: reduced(): pl.pallas_call(functools.partial(reduce_kernel, roles, chips, mine, their...]
    ppermute x24 -> x22, waiting for transfers between devices: 283 us -> 188 us  [hop(): return lax.ppermute(value, 'segment', pairs)]
    ppermute x24 -> x22, starting transfers between devices: 30.9 us -> 68.7 us  [hop(): return lax.ppermute(value, 'segment', pairs)]
    ppermute x22 -> x30, waiting for transfers between devices: 31.2 us -> 5.63 us  [across(): return lax.ppermute(value, ('segment', 'dp'), pairs)]
    ppermute x22 -> x30, starting transfers between devices: 23.2 us -> 47.9 us  [across(): return lax.ppermute(value, ('segment', 'dp'), pairs)]
    all_gather x1 -> x0, blocking collectives: 15.5 us -> none  [local(): all_rows = lax.all_gather(mod_rows, 'dp', axis=0, tiled=True)]
    unnamed x1 -> x0, blocking collectives: 11.1 us -> none
  transfers between devices with their start and end apart: 48 -> 52, of which waited for: 17 -> 12; matrix products, arithmetic and copies ran while one was open for 4% -> 4% of each run, Pallas kernels for 27% -> 23%
where the time goes in v2:
time: 750 us; the launch traced here: 738 us
  Pallas kernels  355 us (47%)
  waiting for transfers between devices  194 us (26%)
  starting transfers between devices  117 us (16%)
  local copies, waits for them, and re-layouts  45.3 us (6%)
  other arithmetic  19.1 us (3%)
    pallas_call x26, Pallas kernels, call(): pl.pallas_call(kernel, grid_spec=pltpu.PrefetchScalarGridSpec(num_scalar_...  216 us
    ppermute x22, waiting for transfers between devices, hop(): return lax.ppermute(value, 'segment', pairs)  188 us
    ppermute x22, starting transfers between devices, hop(): return lax.ppermute(value, 'segment', pairs)  68.7 us
    pallas_call x3, Pallas kernels, reduced(): pl.pallas_call(functools.partial(reduce_kernel, roles, chips, mine, their...  68.6 us
    pallas_call x1, Pallas kernels, gathered_rows(): pl.pallas_call(functools.partial(gather_kernel, size), out_shape=jax.Shap...  49.9 us
    ppermute x30, starting transfers between devices, across(): return lax.ppermute(value, ('segment', 'dp'), pairs)  47.9 us
    unnamed x153, local copies, waits for them, and re-layouts  24.5 us
    pallas_call x4, Pallas kernels, weight_grad(): pl.pallas_call(functools.partial(weight_grad_kernel, kind), grid_spec=plt...  19.6 us
  transfers between devices with their start and end apart: 52, of which 12 were waited for; matrix products, arithmetic and copies ran while one was open for 4% of the time, Pallas kernels for 23%

profile of v2, /device:TPU:0, one launch (start us, length us, event | category | flops | bytes accessed | tf_op | source)
XLA Modules:
  0.0 738.1 jit_solution(7415214539294586957)
XLA Ops:
  3.2 3.3 constant_dynamic-slice_fusion.1
  8.6 5.9 collective-permute-start.2
  35.6 3.3 collective-permute-done.2.prt1_own
  38.9 25.8 %attention_forward.5 = (bf16[512,768]{1,0:T(8,128)(2,1)}, bf16[10,4,512,768]{3,2,1,0:T(8,128)(2,1)}, bf16[2,4,1024,768]{3,2,1,0:T(8,128)(2,1)}, f32[4,512,128]{2,1,0:T(8,128)}) custom-call(s32[16]{0:T(128)} %concatenate.9.sc, s32[4]{0:T(128)} %constant.125.clone.tt, ...), custom_call_target="tpu_custom_call", output_to_operand_aliasing={{1}: (15, {}), {2}: (16, {}), {3}: (17, {})} | custom-call | flops 20000000000 | bytes 1048576 | tf_op jit(solution)/shard_map/attention_forward/pallas_call | solution.py:916
  66.8 25.8 %attention_forward.6 = (bf16[512,768]{1,0:T(8,128)(2,1)}, bf16[10,4,512,768]{3,2,1,0:T(8,128)(2,1)}, bf16[2,4,1024,768]{3,2,1,0:T(8,128)(2,1)}, f32[4,512,128]{2,1,0:T(8,128)}) custom-call(s32[16]{0:T(128)} %concatenate.9.sc, s32[4]{0:T(128)} %constant.126.clone.tt, ...), custom_call_target="tpu_custom_call", output_to_operand_aliasing={{1}: (15, {}), {2}: (16, {}), {3}: (17, {})} | custom-call | flops 20000000000 | bytes 1048576 | tf_op jit(solution)/shard_map/attention_forward/pallas_call | solution.py:916
  95.7 10.5 %collective-permute-start.12 = (bf16[384,3072]{1,0:T(8,128)(2,1)}, bf16[384,3072]{1,0:T(8,128)(2,1)S(1)}, u32[]{:S(2)}, u32[]{:S(2)}) collective-permute-start(bf16[384,3072]{1,0:T(8,128)(2,1)} %collective-permute-done.3.wx_own.wx_oth), channel_id=1, source_target_pairs={{16,17},{18,19},{20,21},{22,23},{17,16},{19,18},{21,20},{23,22},{2... | collective-permute-start | bytes 7077896 | tf_op jit(solution)/shard_map/ppermute | solution.py:972
  110.5 9.6 %collective-permute-start.11 = (bf16[512,768]{1,0:T(8,128)(2,1)S(1)}, bf16[512,768]{1,0:T(8,128)(2,1)S(1)}, u32[]{:S(2)}, u32[]{:S(2)}) collective-permute-start(bf16[512,768]{1,0:T(8,128)(2,1)S(1)} %copy-done.63), channel_id=1, source_target_pairs={{0,8},{1,9},{2,10},{3,11},{4,12},{5,13},{6,14},{7,15}} | collective-permute-start | bytes 2359304 | tf_op jit(solution)/shard_map/ppermute | solution.py:978
  121.5 15.3 %collective-permute-done.11.hop = bf16[512,768]{1,0:T(8,128)(2,1)S(1)} collective-permute-done((bf16[512,768]{1,0:T(8,128)(2,1)S(1)}, bf16[512,768]{1,0:T(8,128)(2,1)S(1)}, u32[]{:S(2)}, u32[]{:S(2)}) %collective-permute-start.11) | collective-permute-done | bytes 786464 | tf_op jit(solution)/shard_map/ppermute | solution.py:978
  139.2 13.8 %attention_forward.7 = (bf16[512,768]{1,0:T(8,128)(2,1)}, bf16[10,4,512,768]{3,2,1,0:T(8,128)(2,1)}, bf16[2,4,1024,768]{3,2,1,0:T(8,128)(2,1)}, f32[4,512,128]{2,1,0:T(8,128)}) custom-call(s32[16]{0:T(128)} %concatenate.9.sc, s32[4]{0:T(128)} %constant.128.clone.tt, ...), custom_call_target="tpu_custom_call", output_to_operand_aliasing={{1}: (15, {}), {2}: (16, {}), {3}: (17, {})} | custom-call | flops 20000000000 | bytes 1048576 | tf_op jit(solution)/shard_map/attention_forward/pallas_call | solution.py:916
  158.7 22.1 %collective-permute-start.14 = (bf16[512,768]{1,0:T(8,128)(2,1)S(1)}, bf16[512,768]{1,0:T(8,128)(2,1)S(1)}, u32[]{:S(2)}, u32[]{:S(2)}) collective-permute-start(bf16[512,768]{1,0:T(8,128)(2,1)S(1)} %copy-done.40), channel_id=1, source_target_pairs={{0,8},{1,9},{2,10},{3,11},{4,12},{5,13},{6,14},{7,15}} | collective-permute-start | bytes 2359304 | tf_op jit(solution)/shard_map/ppermute | solution.py:978
  181.7 13.8 %attention_forward.8 = (bf16[512,768]{1,0:T(8,128)(2,1)}, bf16[10,4,512,768]{3,2,1,0:T(8,128)(2,1)}, bf16[2,4,1024,768]{3,2,1,0:T(8,128)(2,1)}, f32[4,512,128]{2,1,0:T(8,128)}) custom-call(s32[16]{0:T(128)} %concatenate.9.sc, s32[4]{0:T(128)} %constant.130.clone.tt, ...), custom_call_target="tpu_custom_call", output_to_operand_aliasing={{1}: (15, {}), {2}: (16, {}), {3}: (17, {})} | custom-call | flops 20000000000 | bytes 1048576 | tf_op jit(solution)/shard_map/attention_forward/pallas_call | solution.py:916
  199.6 12.4 %collective-permute-start.18 = (bf16[512,768]{1,0:T(8,128)(2,1)S(1)}, bf16[512,768]{1,0:T(8,128)(2,1)S(1)}, u32[]{:S(2)}, u32[]{:S(2)}) collective-permute-start(bf16[512,768]{1,0:T(8,128)(2,1)S(1)} %copy-done.42), channel_id=1, source_target_pairs={{0,8},{1,9},{2,10},{3,11},{4,12},{5,13},{6,14},{7,15}} | collective-permute-start | bytes 2359304 | tf_op jit(solution)/shard_map/ppermute | solution.py:978
  215.4 11.7 %collective-permute-done.18.hop = bf16[512,768]{1,0:T(8,128)(2,1)S(1)} collective-permute-done((bf16[512,768]{1,0:T(8,128)(2,1)S(1)}, bf16[512,768]{1,0:T(8,128)(2,1)S(1)}, u32[]{:S(2)}, u32[]{:S(2)}) %collective-permute-start.18) | collective-permute-done | bytes 786464 | tf_op jit(solution)/shard_map/ppermute | solution.py:978
  254.5 85.9 %collective-permute-done.30.hop0 = bf16[512,768]{1,0:T(8,128)(2,1)S(1)} collective-permute-done((bf16[512,768]{1,0:T(8,128)(2,1)}, bf16[512,768]{1,0:T(8,128)(2,1)S(1)}, u32[]{:S(2)}, u32[]{:S(2)}) %collective-permute-start.30) | collective-permute-done | bytes 786464 | tf_op jit(solution)/shard_map/ppermute | solution.py:978
  341.3 23.2 %attention_backward.6 = (bf16[2,768,512]{2,1,0:T(8,128)(2,1)}, bf16[2,768,512]{2,1,0:T(8,128)(2,1)}, bf16[10,4,512,768]{3,2,1,0:T(8,128)(2,1)}, bf16[4,512,3072]{2,1,0:T(8,128)(2,1)}) custom-call(s32[16]{0:T(128)} %concatenate.9.sc, s32[4]{0:T(128)} %constant.138.clone.tt, ...), custom_call_target="tpu_custom_call", output_to_operand_aliasing={{2}: (11, {}), {3}: (12, {})} | custom-call | flops 22000001024 | bytes 1048576 | tf_op jit(solution)/shard_map/attention_backward/pallas_call | solution.py:916
  372.1 10.8 %projection_backward.6 = (bf16[512,768]{1,0:T(8,128)(2,1)}, bf16[10,4,512,768]{3,2,1,0:T(8,128)(2,1)}, bf16[4,512,3072]{2,1,0:T(8,128)(2,1)}, f32[4,8,768]{2,1,0:T(8,128)}) custom-call(s32[16]{0:T(128)} %concatenate.9.sc, s32[4]{0:T(128)} %constant.138.clone.tt, ...), custom_call_target="tpu_custom_call", output_to_operand_aliasing={{1}: (15, {}), {2}: (16, {}), {3}: (17, {})} | custom-call | flops 8999999488 | bytes 1048576 | tf_op jit(solution)/shard_map/projection_backward/pallas_call | solution.py:916
  383.7 6.6 collective-permute-done.36.hop0
  395.1 37.9 %collective-permute-done.38.hop0 = bf16[512,768]{1,0:T(8,128)(2,1)S(1)} collective-permute-done((bf16[512,768]{1,0:T(8,128)(2,1)}, bf16[512,768]{1,0:T(8,128)(2,1)S(1)}, u32[]{:S(2)}, u32[]{:S(2)}) %collective-permute-start.38) | collective-permute-done | bytes 786464 | tf_op jit(solution)/shard_map/ppermute | solution.py:978
  437.2 23.1 %attention_backward.7 = (bf16[2,768,512]{2,1,0:T(8,128)(2,1)}, bf16[2,768,512]{2,1,0:T(8,128)(2,1)}, bf16[10,4,512,768]{3,2,1,0:T(8,128)(2,1)}, bf16[4,512,3072]{2,1,0:T(8,128)(2,1)}) custom-call(s32[16]{0:T(128)} %concatenate.9.sc, s32[4]{0:T(128)} %constant.126.clone.tt, ...), custom_call_target="tpu_custom_call", output_to_operand_aliasing={{2}: (11, {}), {3}: (12, {})} | custom-call | flops 22000001024 | bytes 1048576 | tf_op jit(solution)/shard_map/attention_backward/pallas_call | solution.py:916
  462.2 3.6 collective-permute-done.40.rcv0
  467.0 10.8 %projection_backward.7 = (bf16[512,768]{1,0:T(8,128)(2,1)}, bf16[10,4,512,768]{3,2,1,0:T(8,128)(2,1)}, bf16[4,512,3072]{2,1,0:T(8,128)(2,1)}, f32[4,8,768]{2,1,0:T(8,128)}) custom-call(s32[16]{0:T(128)} %concatenate.9.sc, s32[4]{0:T(128)} %constant.126.clone.tt, ...), custom_call_target="tpu_custom_call", output_to_operand_aliasing={{1}: (15, {}), {2}: (16, {}), {3}: (17, {})} | custom-call | flops 8999999488 | bytes 1048576 | tf_op jit(solution)/shard_map/projection_backward/pallas_call | solution.py:916
  477.8 13.8 %attention_backward.8 = (bf16[2,768,512]{2,1,0:T(8,128)(2,1)}, bf16[2,768,512]{2,1,0:T(8,128)(2,1)}, bf16[10,4,512,768]{3,2,1,0:T(8,128)(2,1)}, bf16[4,512,3072]{2,1,0:T(8,128)(2,1)}) custom-call(s32[16]{0:T(128)} %concatenate.9.sc, s32[4]{0:T(128)} %constant.143.clone.tt, ...), custom_call_target="tpu_custom_call", output_to_operand_aliasing={{2}: (11, {}), {3}: (12, {})} | custom-call | flops 22000001024 | bytes 1048576 | tf_op jit(solution)/shard_map/attention_backward/pallas_call | solution.py:916
  500.5 8.6 %projection_backward.8 = (bf16[512,768]{1,0:T(8,128)(2,1)}, bf16[10,4,512,768]{3,2,1,0:T(8,128)(2,1)}, bf16[4,512,3072]{2,1,0:T(8,128)(2,1)}, f32[4,8,768]{2,1,0:T(8,128)}) custom-call(s32[16]{0:T(128)} %concatenate.9.sc, s32[4]{0:T(128)} %constant.143.clone.tt, ...), custom_call_target="tpu_custom_call", output_to_operand_aliasing={{1}: (15, {}), {2}: (16, {}), {3}: (17, {})} | custom-call | flops 8999999488 | bytes 1048576 | tf_op jit(solution)/shard_map/projection_backward/pallas_call | solution.py:916
  509.1 15.5 %collective-permute-done.39.hop0 = bf16[512,768]{1,0:T(8,128)(2,1)S(1)} collective-permute-done((bf16[512,768]{1,0:T(8,128)(2,1)}, bf16[512,768]{1,0:T(8,128)(2,1)S(1)}, u32[]{:S(2)}, u32[]{:S(2)}) %collective-permute-start.39) | collective-permute-done | bytes 786464 | tf_op jit(solution)/shard_map/ppermute | solution.py:978
  525.6 12.4 %attention_backward.9 = (bf16[2,768,512]{2,1,0:T(8,128)(2,1)}, bf16[2,768,512]{2,1,0:T(8,128)(2,1)}, bf16[10,4,512,768]{3,2,1,0:T(8,128)(2,1)}, bf16[4,512,3072]{2,1,0:T(8,128)(2,1)}) custom-call(s32[16]{0:T(128)} %concatenate.9.sc, s32[4]{0:T(128)} %constant.144.clone.tt, ...), custom_call_target="tpu_custom_call", output_to_operand_aliasing={{2}: (11, {}), {3}: (12, {})} | custom-call | flops 22000001024 | bytes 1048576 | tf_op jit(solution)/shard_map/attention_backward/pallas_call | solution.py:916
  549.8 8.6 %projection_backward.9 = (bf16[512,768]{1,0:T(8,128)(2,1)}, bf16[10,4,512,768]{3,2,1,0:T(8,128)(2,1)}, bf16[4,512,3072]{2,1,0:T(8,128)(2,1)}, f32[4,8,768]{2,1,0:T(8,128)}) custom-call(s32[16]{0:T(128)} %concatenate.9.sc, s32[4]{0:T(128)} %constant.144.clone.tt, ...), custom_call_target="tpu_custom_call", output_to_operand_aliasing={{1}: (15, {}), {2}: (16, {}), {3}: (17, {})} | custom-call | flops 8999999488 | bytes 1048576 | tf_op jit(solution)/shard_map/projection_backward/pallas_call | solution.py:916
  560.4 17.4 %attention_gradient.3 = bf16[768,3072]{1,0:T(8,128)(2,1)} custom-call(s32[16]{0:T(128)} %concatenate.9.sc, s32[4]{0:T(128)} %constant.145.clone.tt, bf16[10,4,512,768]{3,2,1,0:T(8,128)(2,1)} %get-tuple-element.282.st, bf16[4,512,3072]{2,1,0:T(8,128)(2,1)} %get-tuple-element.283.y), custom_call_target="tpu_custom_call" | custom-call | flops 12000000000 | bytes 1048576 | tf_op jit(solution)/shard_map/attention_gradient/pallas_call | solution.py:1101
  577.8 66.5 %attention_sums.1 = f32[96,3072]{1,0:T(8,128)} custom-call(bf16[8,96,3072]{2,1,0:T(8,128)(2,1)} %bitcast.96), custom_call_target="tpu_custom_call" | custom-call | flops 60000002048 | bytes 1048576 | tf_op jit(solution)/shard_map/attention_sums/pallas_call | solution.py:870
  653.4 6.4 collective-permute-start.48
  663.0 49.9 %gather_sums.1 = f32[8,96,128]{2,1,0:T(8,128)} custom-call(f32[96,128]{1,0:T(8,128)} %reshape.93.rows), custom_call_target="tpu_custom_call" | custom-call | tf_op jit(solution)/shard_map/gather_sums/pallas_call | solution.py:846
  722.0 10.7 %collective-permute-done.51 = f32[192,768]{1,0:T(8,128)S(1)} collective-permute-done((f32[192,768]{1,0:T(8,128)}, f32[192,768]{1,0:T(8,128)S(1)}, u32[]{:S(2)}, u32[]{:S(2)}) %collective-permute-start.51) | collective-permute-done | bytes 589856 | tf_op jit(solution)/shard_map/ppermute | solution.py:978
  734.3 3.5 fusion.7
  (312 shorter events, 143.1 us)
Async XLA Ops:
  6.5 32.4 %collective-permute-start.3 = (bf16[384,3072]{1,0:T(8,128)(2,1)}, bf16[384,3072]{1,0:T(8,128)(2,1)}, u32[]{:S(2)}, u32[]{:S(2)}) collective-permute-start(bf16[384,3072]{1,0:T(8,128)(2,1)} %constant_dynamic-slice_fusion.1), channel_id=1, source_target_pairs={{16,24},{24,16},{17,25},{25,17},{18,26},{26,18},{19,27},{27,19},{2... | collective-permute-start | bytes 7077896 | tf_op jit(solution)/shard_map/ppermute | solution.py:978
  8.6 30.4 %collective-permute-start.2 = (bf16[768,768]{1,0:T(8,128)(2,1)}, bf16[768,768]{1,0:T(8,128)(2,1)}, u32[]{:S(2)}, u32[]{:S(2)}) collective-permute-start(bf16[768,768]{1,0:T(8,128)(2,1)} %dynamic-slice_bitcast_fusion.2), channel_id=1, source_target_pairs={{0,8},{1,9},{2,10},{3,11},{4,12},{5,13},{6,14},{7,15}} | collective-permute-start | bytes 3538952 | tf_op jit(solution)/shard_map/ppermute | solution.py:978
  14.5 78.2 %collective-permute-start.6 = (bf16[768,768]{1,0:T(8,128)(2,1)}, bf16[768,768]{1,0:T(8,128)(2,1)}, u32[]{:S(2)}, u32[]{:S(2)}) collective-permute-start(bf16[768,768]{1,0:T(8,128)(2,1)} %dynamic-slice_bitcast_fusion.2), channel_id=1, source_target_pairs={{16,24},{24,16},{17,25},{25,17},{18,26},{26,18},{19,27},{27,19},{2... | collective-permute-start | bytes 3538952 | tf_op jit(solution)/shard_map/ppermute | solution.py:978
  20.7 18.2 %collective-permute-start.1 = (bf16[1024,768]{1,0:T(8,128)(2,1)}, bf16[1024,768]{1,0:T(8,128)(2,1)}, u32[]{:S(2)}, u32[]{:S(2)}) collective-permute-start(bf16[1024,768]{1,0:T(8,128)(2,1)} %dynamic-slice_bitcast_fusion.1), channel_id=1, source_target_pairs={{0,1},{2,3},{4,5},{6,7},{1,0},{3,2},{5,4},{7,6}} | collective-permute-start | bytes 4718600 | tf_op jit(solution)/shard_map/ppermute | solution.py:972
  64.8 27.9 %collective-permute-start.5 = (bf16[512,768]{1,0:T(8,128)(2,1)}, bf16[512,768]{1,0:T(8,128)(2,1)S(1)}, u32[]{:S(2)}, u32[]{:S(2)}) collective-permute-start(bf16[512,768]{1,0:T(8,128)(2,1)} %get-tuple-element.154), channel_id=1, source_target_pairs={{0,8},{1,9},{2,10},{3,11},{4,12},{5,13},{6,14},{7,15}} | collective-permute-start | bytes 2359304 | tf_op jit(solution)/shard_map/ppermute | solution.py:978
  66.1 26.6 %collective-permute-start.7 = (bf16[768,768]{1,0:T(8,128)(2,1)}, bf16[768,768]{1,0:T(8,128)(2,1)S(1)}, u32[]{:S(2)}, u32[]{:S(2)}) collective-permute-start(bf16[768,768]{1,0:T(8,128)(2,1)} %collective-permute-done.2.prt1_own), channel_id=1, source_target_pairs={{8,9},{10,11},{12,13},{14,15},{9,8},{11,10},{13,12},{15,14}} | collective-permute-start | bytes 3538952 | tf_op jit(solution)/shard_map/ppermute | solution.py:972
  95.7 41.2 %collective-permute-start.12 = (bf16[384,3072]{1,0:T(8,128)(2,1)}, bf16[384,3072]{1,0:T(8,128)(2,1)S(1)}, u32[]{:S(2)}, u32[]{:S(2)}) collective-permute-start(bf16[384,3072]{1,0:T(8,128)(2,1)} %collective-permute-done.3.wx_own.wx_oth), channel_id=1, source_target_pairs={{16,17},{18,19},{20,21},{22,23},{17,16},{19,18},{21,20},{23,22},{2... | collective-permute-start | bytes 7077896 | tf_op jit(solution)/shard_map/ppermute | solution.py:972
  107.8 13.7 %collective-permute-start.10 = (bf16[1024,768]{1,0:T(8,128)(2,1)S(1)}, bf16[1024,768]{1,0:T(8,128)(2,1)S(1)}, u32[]{:S(2)}, u32[]{:S(2)}) collective-permute-start(bf16[1024,768]{1,0:T(8,128)(2,1)S(1)} %dynamic-slice_bitcast_fusion), channel_id=1, source_target_pairs={{0,1},{2,3},{4,5},{6,7},{1,0},{3,2},{5,4},{7,6}} | collective-permute-start | bytes 4718600 | tf_op jit(solution)/shard_map/ppermute | solution.py:972
  110.5 26.4 %collective-permute-start.11 = (bf16[512,768]{1,0:T(8,128)(2,1)S(1)}, bf16[512,768]{1,0:T(8,128)(2,1)S(1)}, u32[]{:S(2)}, u32[]{:S(2)}) collective-permute-start(bf16[512,768]{1,0:T(8,128)(2,1)S(1)} %copy-done.63), channel_id=1, source_target_pairs={{0,8},{1,9},{2,10},{3,11},{4,12},{5,13},{6,14},{7,15}} | collective-permute-start | bytes 2359304 | tf_op jit(solution)/shard_map/ppermute | solution.py:978
  120.0 16.8 %collective-permute-start.9 = (bf16[512,768]{1,0:T(8,128)(2,1)S(1)}, bf16[512,768]{1,0:T(8,128)(2,1)S(1)}, u32[]{:S(2)}, u32[]{:S(2)}) collective-permute-start(bf16[512,768]{1,0:T(8,128)(2,1)S(1)} %collective-permute-done.8.own2), channel_id=1, source_target_pairs={{16,17},{18,19},{20,21},{22,23},{17,16},{19,18},{21,20},{23,22}} | collective-permute-start | bytes 2359304 | tf_op jit(solution)/shard_map/ppermute | solution.py:972
  120.8 32.3 %collective-permute-start.13 = (bf16[768,768]{1,0:T(8,128)(2,1)}, bf16[768,768]{1,0:T(8,128)(2,1)S(1)}, u32[]{:S(2)}, u32[]{:S(2)}) collective-permute-start(bf16[768,768]{1,0:T(8,128)(2,1)} %collective-permute-done.6.prt_own.prt_oth), channel_id=1, source_target_pairs={{16,17},{18,19},{20,21},{22,23},{17,16},{19,18},{21,20},{23,22},{2... | collective-permute-start | bytes 3538952 | tf_op jit(solution)/shard_map/ppermute | solution.py:972
  157.1 23.8 %collective-permute-start.16 = (bf16[512,768]{1,0:T(8,128)(2,1)S(1)}, bf16[512,768]{1,0:T(8,128)(2,1)S(1)}, u32[]{:S(2)}, u32[]{:S(2)}) collective-permute-start(bf16[512,768]{1,0:T(8,128)(2,1)S(1)} %collective-permute-done.15.own3), channel_id=1, source_target_pairs={{24,25},{26,27},{28,29},{30,31},{25,24},{27,26},{29,28},{31,30}} | collective-permute-start | bytes 2359304 | tf_op jit(solution)/shard_map/ppermute | solution.py:972
  157.8 54.2 %collective-permute-start.17 = (bf16[2,1024,768]{2,1,0:T(8,128)(2,1)S(1)}, bf16[2,1024,768]{2,1,0:T(8,128)(2,1)S(1)}, u32[]{:S(2)}, u32[]{:S(2)}) collective-permute-start(bf16[2,1024,768]{2,1,0:T(8,128)(2,1)S(1)} %copy-done.4), channel_id=1, source_target_pairs={{16,17},{18,19},{20,21},{22,23},{17,16},{19,18},{21,20},{23,22},{2... | collective-permute-start | bytes 9437192 | tf_op jit(solution)/shard_map/ppermute | solution.py:972
  158.7 37.8 %collective-permute-start.14 = (bf16[512,768]{1,0:T(8,128)(2,1)S(1)}, bf16[512,768]{1,0:T(8,128)(2,1)S(1)}, u32[]{:S(2)}, u32[]{:S(2)}) collective-permute-start(bf16[512,768]{1,0:T(8,128)(2,1)S(1)} %copy-done.40), channel_id=1, source_target_pairs={{0,8},{1,9},{2,10},{3,11},{4,12},{5,13},{6,14},{7,15}} | collective-permute-start | bytes 2359304 | tf_op jit(solution)/shard_map/ppermute | solution.py:978
  199.6 27.5 %collective-permute-start.18 = (bf16[512,768]{1,0:T(8,128)(2,1)S(1)}, bf16[512,768]{1,0:T(8,128)(2,1)S(1)}, u32[]{:S(2)}, u32[]{:S(2)}) collective-permute-start(bf16[512,768]{1,0:T(8,128)(2,1)S(1)} %copy-done.42), channel_id=1, source_target_pairs={{0,8},{1,9},{2,10},{3,11},{4,12},{5,13},{6,14},{7,15}} | collective-permute-start | bytes 2359304 | tf_op jit(solution)/shard_map/ppermute | solution.py:978
  244.9 95.6 %collective-permute-start.30 = (bf16[512,768]{1,0:T(8,128)(2,1)}, bf16[512,768]{1,0:T(8,128)(2,1)S(1)}, u32[]{:S(2)}, u32[]{:S(2)}) collective-permute-start(bf16[512,768]{1,0:T(8,128)(2,1)} %get-tuple-element.210), channel_id=1, source_target_pairs={{8,0},{9,1},{10,2},{11,3},{12,4},{13,5},{14,6},{15,7}} | collective-permute-start | bytes 2359304 | tf_op jit(solution)/shard_map/ppermute | solution.py:978
  368.0 22.3 %collective-permute-start.36 = (bf16[512,768]{1,0:T(8,128)(2,1)S(1)}, bf16[512,768]{1,0:T(8,128)(2,1)S(1)}, u32[]{:S(2)}, u32[]{:S(2)}) collective-permute-start(bf16[512,768]{1,0:T(8,128)(2,1)S(1)} %copy-done.9), channel_id=1, source_target_pairs={{8,0},{9,1},{10,2},{11,3},{12,4},{13,5},{14,6},{15,7}} | collective-permute-start | bytes 2359304 | tf_op jit(solution)/shard_map/ppermute | solution.py:978
  393.8 39.3 %collective-permute-start.38 = (bf16[512,768]{1,0:T(8,128)(2,1)}, bf16[512,768]{1,0:T(8,128)(2,1)S(1)}, u32[]{:S(2)}, u32[]{:S(2)}) collective-permute-start(bf16[512,768]{1,0:T(8,128)(2,1)} %get-tuple-element.237), channel_id=1, source_target_pairs={{8,0},{9,1},{10,2},{11,3},{12,4},{13,5},{14,6},{15,7}} | collective-permute-start | bytes 2359304 | tf_op jit(solution)/shard_map/ppermute | solution.py:978
  494.7 45.2 %collective-permute-start.19 = (bf16[256,768]{1,0:T(8,128)(2,1)}, bf16[256,768]{1,0:T(8,128)(2,1)S(1)}, u32[]{:S(2)}, u32[]{:S(2)}) collective-permute-start(bf16[256,768]{1,0:T(8,128)(2,1)} %get-tuple-element.304), channel_id=1, source_target_pairs={{16,0},{18,2},{20,4},{22,6},{17,9},{19,11},{21,13},{23,15}} | collective-permute-start | bytes 1179656 | tf_op jit(solution)/shard_map/ppermute | solution.py:972
  496.0 44.0 %collective-permute-start.20 = (bf16[256,768]{1,0:T(8,128)(2,1)S(1)}, bf16[256,768]{1,0:T(8,128)(2,1)S(1)}, u32[]{:S(2)}, u32[]{:S(2)}) collective-permute-start(bf16[256,768]{1,0:T(8,128)(2,1)S(1)} %get-tuple-element.303), channel_id=1, source_target_pairs={{17,25},{19,27},{21,29},{23,31},{24,16},{26,18},{28,20},{30,22}} | collective-permute-start | bytes 1179656 | tf_op jit(solution)/shard_map/ppermute | solution.py:972
  496.7 44.8 %collective-permute-start.21 = (bf16[256,768]{1,0:T(8,128)(2,1)}, bf16[256,768]{1,0:T(8,128)(2,1)}, u32[]{:S(2)}, u32[]{:S(2)}) collective-permute-start(bf16[256,768]{1,0:T(8,128)(2,1)} %get-tuple-element.302), channel_id=1, source_target_pairs={{24,0},{26,2},{28,4},{30,6},{25,9},{27,11},{29,13},{31,15}} | collective-permute-start | bytes 1179656 | tf_op jit(solution)/shard_map/ppermute | solution.py:972
  498.0 26.7 %collective-permute-start.39 = (bf16[512,768]{1,0:T(8,128)(2,1)}, bf16[512,768]{1,0:T(8,128)(2,1)S(1)}, u32[]{:S(2)}, u32[]{:S(2)}) collective-permute-start(bf16[512,768]{1,0:T(8,128)(2,1)} %get-tuple-element.248), channel_id=1, source_target_pairs={{8,0},{9,1},{10,2},{11,3},{12,4},{13,5},{14,6},{15,7}} | collective-permute-start | bytes 2359304 | tf_op jit(solution)/shard_map/ppermute | solution.py:978
  538.0 10.5 %collective-permute-start.42 = (bf16[2,768,512]{2,1,0:T(8,128)(2,1)}, bf16[2,768,512]{2,1,0:T(8,128)(2,1)S(1)}, u32[]{:S(2)}, u32[]{:S(2)}) collective-permute-start(bf16[2,768,512]{2,1,0:T(8,128)(2,1)} %get-tuple-element.264.rcv2.rcv3), channel_id=1, source_target_pairs={{0,1},{2,3},{4,5},{6,7},{1,0},{3,2},{5,4},{7,6}} | collective-permute-start | bytes 4718600 | tf_op jit(solution)/shard_map/ppermute | solution.py:972
  644.5 16.4 %collective-permute-start.50 = (f32[4,3,768]{2,1,0:T(4,128)S(1)}, f32[4,3,768]{2,1,0:T(4,128)S(1)}, u32[]{:S(2)}, u32[]{:S(2)}) collective-permute-start(f32[4,3,768]{2,1,0:T(4,128)S(1)} %fusion.8), channel_id=1, source_target_pairs={{16,24},{24,16},{17,25},{25,17},{18,26},{26,18},{19,27},{27,19},{2... | collective-permute-start | bytes 110600 | tf_op jit(solution)/shard_map/ppermute | solution.py:978
  646.4 68.3 %collective-permute-start.43 = (bf16[256,768]{1,0:T(8,128)(2,1)}, bf16[256,768]{1,0:T(8,128)(2,1)}, u32[]{:S(2)}, u32[]{:S(2)}) collective-permute-start(bf16[256,768]{1,0:T(8,128)(2,1)} %get-tuple-element.307), channel_id=1, source_target_pairs={{16,0},{18,2},{20,4},{22,6},{17,9},{19,11},{21,13},{23,15}} | collective-permute-start | bytes 1179656 | tf_op jit(solution)/shard_map/ppermute | solution.py:972
  647.7 68.3 %collective-permute-start.44 = (bf16[256,768]{1,0:T(8,128)(2,1)}, bf16[256,768]{1,0:T(8,128)(2,1)}, u32[]{:S(2)}, u32[]{:S(2)}) collective-permute-start(bf16[256,768]{1,0:T(8,128)(2,1)} %get-tuple-element.306), channel_id=1, source_target_pairs={{17,25},{19,27},{21,29},{23,31},{24,16},{26,18},{28,20},{30,22}} | collective-permute-start | bytes 1179656 | tf_op jit(solution)/shard_map/ppermute | solution.py:972
  651.5 66.8 %collective-permute-start.47 = (bf16[4,256,768]{2,1,0:T(8,128)(2,1)}, bf16[4,256,768]{2,1,0:T(8,128)(2,1)}, u32[]{:S(2)}, u32[]{:S(2)}) collective-permute-start(bf16[4,256,768]{2,1,0:T(8,128)(2,1)} %get-tuple-element.301), channel_id=1, source_target_pairs={{1,9},{3,11},{5,13},{7,15}} | collective-permute-start | bytes 4718600 | tf_op jit(solution)/shard_map/ppermute | solution.py:972
  653.4 64.8 %collective-permute-start.48 = (bf16[4,256,768]{2,1,0:T(8,128)(2,1)}, bf16[4,256,768]{2,1,0:T(8,128)(2,1)}, u32[]{:S(2)}, u32[]{:S(2)}) collective-permute-start(bf16[4,256,768]{2,1,0:T(8,128)(2,1)} %get-tuple-element.300), channel_id=1, source_target_pairs={{0,16},{2,18},{4,20},{6,22},{1,25},{3,27},{5,29},{7,31}} | collective-permute-start | bytes 4718600 | tf_op jit(solution)/shard_map/ppermute | solution.py:972
  661.0 55.1 %collective-permute-start.45 = (bf16[256,768]{1,0:T(8,128)(2,1)}, bf16[256,768]{1,0:T(8,128)(2,1)}, u32[]{:S(2)}, u32[]{:S(2)}) collective-permute-start(bf16[256,768]{1,0:T(8,128)(2,1)} %get-tuple-element.305), channel_id=1, source_target_pairs={{24,0},{26,2},{28,4},{30,6},{25,9},{27,11},{29,13},{31,15}} | collective-permute-start | bytes 1179656 | tf_op jit(solution)/shard_map/ppermute | solution.py:972
  714.7 18.0 %collective-permute-start.51 = (f32[192,768]{1,0:T(8,128)}, f32[192,768]{1,0:T(8,128)S(1)}, u32[]{:S(2)}, u32[]{:S(2)}) collective-permute-start(f32[192,768]{1,0:T(8,128)} %get-tuple-element.285), channel_id=1, source_target_pairs={{8,0},{9,1},{10,2},{11,3},{12,4},{13,5},{14,6},{15,7}} | collective-permute-start | bytes 1769480 | tf_op jit(solution)/shard_map/ppermute | solution.py:978
  717.5 16.2 %collective-permute-start.46 = (bf16[256,768]{1,0:T(8,128)(2,1)S(1)}, bf16[256,768]{1,0:T(8,128)(2,1)S(1)}, u32[]{:S(2)}, u32[]{:S(2)}) collective-permute-start(bf16[256,768]{1,0:T(8,128)(2,1)S(1)} %get-tuple-element.295), channel_id=1, source_target_pairs={{0,1},{2,3},{4,5},{6,7},{1,0},{3,2},{5,4},{7,6},{8,9},{10,11},{12,... | collective-permute-start | bytes 1179656 | tf_op jit(solution)/shard_map/ppermute | solution.py:972
  720.0 13.8 %collective-permute-start.49 = (bf16[2,256,768]{2,1,0:T(8,128)(2,1)S(1)}, bf16[2,256,768]{2,1,0:T(8,128)(2,1)S(1)}, u32[]{:S(2)}, u32[]{:S(2)}) collective-permute-start(bf16[2,256,768]{2,1,0:T(8,128)(2,1)S(1)} %broadcast_select_fusion), channel_id=1, source_target_pairs={{0,1},{2,3},{4,5},{6,7},{1,0},{3,2},{5,4},{7,6},{8,9},{10,11},{12,... | collective-permute-start | bytes 2359304 | tf_op jit(solution)/shard_map/ppermute | solution.py:972
  (96 other events, 949.7 us)

commit v3 on v2

v3 whole, which is shorter than its diff:
```python
import functools
import math

import jax
import jax.numpy as jnp
import numpy as np
from jax import lax
from jax.experimental import pallas as pl
from jax.experimental.pallas import tpu as pltpu
from jax.sharding import PartitionSpec as P

D = 768
HEADS = 12
HEAD_DIM = 64
FF = 3072
SEQ_LEN = 1024
BLK = 256
HALF = SEQ_LEN // 2
MB = 4
XS, QS, AT, BR, NM, DQ, XF, BF, NF, GB = range(10)
VLIM = 56 << 20
bf16, f32, i32 = jnp.bfloat16, jnp.float32, jnp.int32


def dot(a, b):
    return lax.dot_general(a, b, (((1,), (0,)), ((), ())), preferred_element_type=f32)


def dot_nt(a, b):
    return lax.dot_general(a, b, (((1,), (1,)), ((), ())), preferred_element_type=f32)


def dot_tn(a, b):
    return lax.dot_general(a, b, (((0,), (0,)), ((), ())), preferred_element_type=f32)


def block_rows(b):
    return pl.ds(pl.multiple_of(b * BLK, BLK), BLK)


def lanes(p):
    return pl.ds(pl.multiple_of(p * 128, 128), 128)


def norm_parts(x):
    center = x - jnp.mean(x, axis=-1, keepdims=True)
    rstd = lax.rsqrt(jnp.mean(center * center, axis=-1, keepdims=True) + 1e-06)
    return center * rstd, rstd


def norm_back(d_normed, n, rstd, scl):
    dn = d_normed * scl
    return (
        dn - jnp.mean(dn, axis=-1, keepdims=True) - n * jnp.mean(dn * n, axis=-1, keepdims=True)
    ) * rstd


def turn(v, cosine, sine):
    lane = lax.broadcasted_iota(i32, v.shape, 1)
    partner = jnp.where(lane % 64 < 32, pltpu.roll(v, 96, 1), pltpu.roll(v, 32, 1))
    return v * cosine + partner * sine


def live_column(rows, c, length, first=0):
    r = lax.broadcasted_iota(i32, (rows, 1), 0) + first
    position = r + BLK * c + jnp.where(r >= BLK, BLK, 0)
    return position < length


def counts(length, c):
    nk = lax.shift_right_logical(length + (BLK - 1), 8)
    return nk, lax.shift_right_logical(nk - c + 1, 1)


class Copies:
    def __init__(self, sems):
        self.sems, self.started = sems, []

    def add(self, src, dst):
        copy = pltpu.make_async_copy(src, dst, self.sems.at[len(self.started)])
        copy.start()
        self.started.append(copy)

    def wait(self):
        for copy in self.started:
            copy.wait()


def load_shared(c, borrowed, w, wx_own, wx_oth, cols, wv, sem, into=None):
    into = cols if into is None else into
    whole = pltpu.make_async_copy(w.at[:, cols], wv.at[:, into], sem)
    pl.when(jnp.logical_not(borrowed))(lambda: whole.start())
    half = D // 2

    @pl.when(borrowed)
    def _():
        for source, at in ((wx_own, c), (wx_oth, 1 - c)):
            rows = pl.ds(pl.multiple_of(at * half, half), half)
            pltpu.make_async_copy(source.at[:, cols], wv.at[rows, into], sem).start()

    return whole


def gelu_parts(u):
    u2 = u * u
    t = jnp.tanh(0.7978845608028654 * (u * (1.0 + 0.044715 * u2)))
    return t, u2


def weight_grad_kernel(kind, sc, tt, st, y, out, xv, xt, yv, acc, ov, xsem, ysem, osem):
    chosen, c = tt[sc[0]], sc[1]

    def tile(j):
        return y.at[:, :, pl.ds(pl.multiple_of(j * D, D), D)]

    def into(j):
        at = pl.ds(pl.multiple_of(j * D, D), D)
        return out.at[at] if kind == "down" else out.at[:, at]

    def load_x(which):
        return pltpu.make_async_copy(st.at[which], xv, xsem.at[0])

    def load_y(j):
        slot = lax.rem(j, 2)
        return pltpu.make_async_copy(tile(j), yv.at[slot], ysem.at[slot])

    def store(j):
        slot = lax.rem(j, 2)
        return pltpu.make_async_copy(ov.at[slot], into(j), osem.at[slot])

    def live(mb):
        _, ns = counts(sc[2 + mb], c)
        picked = lax.rem(lax.shift_right_logical(chosen, mb), 2) == 1
        return jnp.where(picked, ns, 0)

    def transpose_rows(x):
        def step(mb, carry):
            def block(j, carry):
                xt[:, block_rows(2 * mb + j)] = x[mb, block_rows(j), :].T
                return carry

            return lax.fori_loop(0, live(mb), block, carry)

        lax.fori_loop(0, MB, step, 0)

    @pl.when(chosen > 0)
    def _():
        first = GB if kind == "down" else NM if kind == "attention" else NF
        load_x(first).start()
        load_y(0).start()
        load_x(first).wait()
        if kind != "down":
            transpose_rows(xv)
        if kind == "attention":
            load_x(AT).start()

        def step(j, carry):
            slot = lax.rem(j, 2)
            pl.when(j < 3)(lambda: load_y(j + 1).start())
            load_y(j).wait()
            if kind == "down":
                transpose_rows(yv.at[slot])
            if kind == "attention":

                @pl.when(j == 3)
                def _():
                    load_x(AT).wait()
                    transpose_rows(xv)

            acc[...] = jnp.zeros((D, D), f32)

            def add(mb, carry):
                for slots in (1, 2):

                    @pl.when(live(mb) == slots)
                    def _():
                        at = pl.ds(pl.multiple_of(mb * HALF, HALF), slots * BLK)
                        if kind == "down":
                            right = xv[mb, 0 : slots * BLK, :]
                        else:
                            right = yv[slot, mb, 0 : slots * BLK, :]
                        acc[...] += dot(xt[:, at], right)

                return carry

            lax.fori_loop(0, MB, add, 0)
            pl.when(j >= 2)(lambda: store(j - 2).wait())
            ov[slot] = acc[...].astype(bf16)
            store(j).start()
            return carry

        lax.fori_loop(0, 4, step, 0)
        store(2).wait()
        store(3).wait()


def reduce_kernel(roles, chips, mine, theirs, *refs):
    count, kept = len(mine[0]) + len(theirs[0]), len(mine[0])
    arrays, outs = refs[:count], refs[count : count + kept]
    near, total = refs[count + kept : 2 * count + kept], refs[2 * count + kept : 3 * count + kept]
    refs = refs[3 * count + kept :]
    paired = len(theirs[0]) > 0
    cross, refs = (refs[:kept], refs[kept:]) if paired else ((), refs)
    gathered, result, refs = refs[:kept], refs[kept : 2 * kept], refs[2 * kept :]
    load_sem, near_send, near_recv, cross_send, cross_recv, far_send, far_recv, out_sem = refs
    seg, dp = lax.axis_index("segment"), lax.axis_index("dp")
    core, place = lax.rem(dp, 2), lax.div(dp, 2)

    def device(segment, chip, at):
        return {"segment": segment, "dp": 2 * chip + at}

    def remote(src, dst, send, recv, target):
        return pltpu.make_async_remote_copy(
            src_ref=src, dst_ref=dst, send_sem=send, recv_sem=recv,
            device_id=target, device_id_type=pl.DeviceIdType.MESH,
        )

    def work(role, other, keep, give):
        barrier = pltpu.get_barrier_semaphore()
        peers = [device(role, place, 1 - core)]
        peers += [device(role, lax.rem(place + k, chips), core) for k in range(1, chips)]
        if paired:
            peers.append(device(other, place, core))
        for peer in peers:
            pl.semaphore_signal(
                barrier, inc=1, device_id=peer, device_id_type=pl.DeviceIdType.MESH
            )
        pl.semaphore_wait(barrier, len(peers))

        order = [lax.rem(place + k, chips) for k in range(1, chips)] + [place]
        nears, loads = [], []
        for z in range(chips):
            for k, at in enumerate(keep + give):
                to = remote(
                    arrays[at].at[2 * z + 1 - core], near[k].at[z],
                    near_send.at[k, z], near_recv.at[k, z], device(role, place, 1 - core),
                )
                to.start()
                nears.append(to)
                load = pltpu.make_async_copy(
                    arrays[at].at[2 * z + core], total[k].at[z], load_sem.at[k, z]
                )
                load.start()
                loads.append(load)
        crossing = []
        for z in range(chips):
            for k in list(range(kept, count)) + list(range(kept)):
                loads[z * count + k].wait()
                nears[z * count + k].wait()
                total[k][z] = total[k][z] + near[k][z]
                if k >= kept:
                    to = remote(
                        total[k].at[z], cross[k - kept].at[z],
                        cross_send.at[k - kept, z], cross_recv.at[k - kept, z],
                        device(other, place, core),
                    )
                    to.start()
                    crossing.append(to)
        far = []
        for z in range(chips):
            for k in range(kept):
                if paired:
                    crossing[z * kept + k].wait()
                    total[k][z] = total[k][z] + cross[k][z]
                far.append(
                    remote(
                        total[k].at[z], gathered[k].at[place],
                        far_send.at[k, z], far_recv.at[k, place], device(role, z, core),
                    )
                )
                pl.when(place != z)(far[-1].start)
        for k in range(kept):
            result[k][...] = total[k][place].astype(f32)
        for z in order[:-1]:
            for k in range(kept):
                remote(
                    total[k].at[z], gathered[k].at[z],
                    far_send.at[k, z], far_recv.at[k, z], device(role, z, core),
                ).wait_recv()
                result[k][...] += gathered[k][z].astype(f32)
        copies = []
        for k in range(kept):
            copies.append(pltpu.make_async_copy(result[k], outs[k], out_sem.at[k]))
            copies[-1].start()
        for z in range(chips):
            for k in range(kept):
                pl.when(place != z)(far[z * kept + k].wait_send)
        for copy in copies:
            copy.wait()

    for index, role in enumerate(roles):
        other = roles[1 - index] if paired else role
        pl.when(seg == role)(functools.partial(work, role, other, mine[index], theirs[index]))


def gather_kernel(size, rows, out, own_sem, send, recv):
    seg, dp = lax.axis_index("segment"), lax.axis_index("dp")

    def peer(k):
        return {"segment": seg, "dp": lax.rem(dp + k, size)}

    barrier = pltpu.get_barrier_semaphore()
    for k in range(1, size):
        pl.semaphore_signal(
            barrier, inc=1, device_id=peer(k), device_id_type=pl.DeviceIdType.MESH
        )
    pl.semaphore_wait(barrier, size - 1)
    own = pltpu.make_async_copy(rows, out.at[dp], own_sem)
    own.start()

    def copy(k, slot):
        return pltpu.make_async_remote_copy(
            src_ref=rows, dst_ref=out.at[slot], send_sem=send.at[k], recv_sem=recv.at[slot],
            device_id=peer(k), device_id_type=pl.DeviceIdType.MESH,
        )

    for k in range(1, size):
        copy(k, dp).start()
    own.wait()
    for k in range(1, size):
        copy(k, dp).wait_send()
        copy(k, lax.rem(dp + k, size)).wait_recv()


def gathered_rows(rows, size, number):
    return pl.pallas_call(
        functools.partial(gather_kernel, size),
        out_shape=jax.ShapeDtypeStruct((size, *rows.shape), rows.dtype),
        in_specs=[VMEM],
        out_specs=VMEM,
        scratch_shapes=[
            pltpu.SemaphoreType.DMA,
            pltpu.SemaphoreType.DMA((size,)),
            pltpu.SemaphoreType.DMA((size,)),
        ],
        compiler_params=pltpu.CompilerParams(
            vmem_limit_bytes=VLIM, collective_id=number, has_side_effects=True
        ),
        name="gather_sums",
    )(rows)


def reduced(arrays, roles, mine, theirs, chips, number, name):
    dims = [a.shape[1:] for a in arrays]
    kept, count = len(mine[0]), len(mine[0]) + len(theirs[0])
    order = mine[0] + theirs[0]
    every = [vm((chips, *dims[k])) for k in order]
    keeps = [vm((chips, *dims[k])) for k in mine[0]]
    pairs = pltpu.SemaphoreType.DMA((count, chips))
    return pl.pallas_call(
        functools.partial(reduce_kernel, roles, chips, mine, theirs),
        out_shape=[jax.ShapeDtypeStruct(dims[k], f32) for k in mine[0]],
        in_specs=[ANY] * len(arrays),
        out_specs=[ANY] * kept,
        scratch_shapes=every + every + (keeps if theirs[0] else []) + keeps
        + [vm(dims[k], f32) for k in mine[0]]
        + [pairs] * 7 + [pltpu.SemaphoreType.DMA((kept,))],
        compiler_params=pltpu.CompilerParams(
            vmem_limit_bytes=VLIM, collective_id=number, has_side_effects=True
        ),
        cost_estimate=cost(60),
        name=name,
    )(*arrays)


ANY = pl.BlockSpec(memory_space=pl.ANY)
VMEM = pl.BlockSpec(memory_space=pltpu.VMEM)


def shape(dims, dtype=bf16):
    return jax.ShapeDtypeStruct(dims, dtype)


ROWS = shape((HALF, D))
ST = shape((10, MB, HALF, D))
KV = shape((2, MB, SEQ_LEN, D))
LSE = shape((MB, HALF, 128), f32)
YS = shape((MB, HALF, FF))
DM = shape((MB, 8, D), f32)
DKV = shape((2, D, HALF))


def vm(dims, dtype=bf16):
    return pltpu.VMEM(dims, dtype)


HV, FV = vm((HALF, D)), vm((SEQ_LEN, D))


def cost(micros):
    return pl.CostEstimate(flops=int(micros * 1e9), bytes_accessed=1 << 20, transcendentals=0)


MESH = pl.DeviceIdType.MESH
ATT_F, FF_F, FF_B, ATT_B = range(4)


def chain_kernel(
    lens, xs, cs, w, rows2, cos, sin, mod,
    xa, xf, gf, ga, st, kv, lse, y, yf, act, dma, dmf, fin,
    wa, w1, w2, xv, nv, kvv, vv, h0, h1, h2, h3, h4, h5, h6, h7, h8, ov, lv, cv, sv,
    dkt, dvt, rcvv, dpv, duv, actv, accv, dmv, moda, modf,
    w_send, w_recv, wf_send, wf_recv, x_send, xa_own, xa_oth, fwd_send, c_send, gf_sem, xf_sem,
    ga_sem, push_sem, dkv_send, dkv_recv, ld, osem,
):
    role, dp = lax.axis_index("segment"), lax.axis_index("dp")
    c, place = lax.rem(dp, 2), lax.div(dp, 2)
    quarter, half_d = FF // 4, D // 2

    def device(segment, core):
        return {"segment": segment, "dp": 2 * place + core}

    def remote(src, dst, send, recv, target):
        return pltpu.make_async_remote_copy(
            src_ref=src, dst_ref=dst, send_sem=send, recv_sem=recv, device_id=target,
            device_id_type=MESH,
        )

    def local_copy(src, dst, sem):
        return pltpu.make_async_copy(src, dst, sem)

    partner = device(role, 1 - c)

    def rows_at(start, size):
        return pl.ds(pl.multiple_of(start, size), size)

    barrier = pltpu.get_barrier_semaphore()
    pl.semaphore_signal(barrier, inc=1, device_id=partner, device_id_type=MESH)
    for who, others in ((0, (1,)), (1, (0, 2, 3)), (2, (1, 3)), (3, (1, 2))):

        @pl.when(role == who)
        def _():
            for other in others:
                pl.semaphore_signal(
                    barrier, inc=1, device_id=device(other, c), device_id_type=MESH
                )
            pl.semaphore_wait(barrier, 1 + len(others))

    tables = [local_copy(cos, cv, ld.at[0]), local_copy(sin, sv, ld.at[1])]
    for copy in tables:
        copy.start()

    def give_x(k):
        return remote(xs.at[k], xa.at[2 * k + c], x_send.at[k], xa_oth.at[2 * k + c, 0], partner)

    def keep_x(k):
        return local_copy(xs.at[k], xa.at[2 * k + c], ld.at[4 + k])

    w_half = rows_at(c * half_d, half_d)
    rows_half = rows_at(c * quarter, quarter)
    high_half = rows_at(2 * quarter + c * quarter, quarter)

    def give_rows(dst, target):
        return remote(rows2.at[rows_half], w2.at[dst], w_send.at[1], w_recv.at[1], device(target, c))

    def give_w(dst, target):
        return remote(w.at[w_half], dst.at[w_half], w_send.at[0], w_recv.at[0], device(target, c))

    def give_mod(dst, target):
        return remote(mod, dst, w_send.at[2], w_recv.at[2], device(target, c))

    def give_c(k, j):
        return remote(
            cs.at[k, block_rows(1 - c + 2 * j)], gf.at[2 * k + c, pl.ds(j * BLK, BLK)],
            c_send.at[k, j], gf_sem.at[2 * k + c, j], partner,
        )

    def keep_c(k, j):
        return local_copy(
            cs.at[k, block_rows(c + 2 * j)], gf.at[2 * k + c, pl.ds(j * BLK, BLK)],
            ld.at[4 + 2 * k + j],
        )

    def forward_w(dst):
        return remote(dst.at[w_half], dst.at[w_half], wf_send.at[0], wf_recv.at[0], partner)

    def forward_rows(dst):
        return remote(w2.at[dst], w2.at[dst], wf_send.at[1], wf_recv.at[1], partner)

    def settle(copies):
        for given, passed in copies:
            given.wait_recv()
            passed.start()
        for given, passed in copies:
            passed.wait()

    @pl.when(role == 0)
    def _():
        for k in range(2):
            give_x(k).start()
            keep_x(k).start()
        give_rows(rows_half, 1).start()
        load = local_copy(w, wa, ld.at[2])
        load.start()
        local_copy(mod, moda, ld.at[3]).start()
        for k in range(2):
            keep_x(k).wait()
        local_copy(mod, moda, ld.at[3]).wait()
        load.wait()

    @pl.when(role == 1)
    def _():
        loads = [
            local_copy(w, w1, ld.at[2]), local_copy(mod, modf, ld.at[3]),
            local_copy(rows2, w2.at[pl.ds(2 * quarter, 2 * quarter)], ld.at[4]),
        ]
        for copy in loads:
            copy.start()
        settle([(give_rows(rows_half, 1), forward_rows(rows_half))])
        for copy in loads:
            copy.wait()

    for who in (2, 3):

        @pl.when(role == who)
        def _():
            other = 5 - who
            mine, theirs = (wa, w1) if who == 2 else (w1, wa)
            mod_mine, mod_theirs = (moda, modf) if who == 2 else (modf, moda)
            there, here = (rows_half, high_half) if who == 2 else (high_half, rows_half)
            give_mod(mod_mine, other).start()
            give_w(mine, other).start()
            give_rows(there, other).start()
            loads = [
                local_copy(w, mine, ld.at[2]), local_copy(mod, mod_mine, ld.at[3]),
                local_copy(
                    rows2, w2.at[pl.ds(0 if who == 2 else 2 * quarter, 2 * quarter)], ld.at[8]
                ),
            ]
            for copy in loads:
                copy.start()

            @pl.when(c == who - 2)
            def _():
                for k in range(2):
                    for j in range(2):
                        give_c(k, j).start()
                        keep_c(k, j).start()
                for k in range(2):
                    for j in range(2):
                        keep_c(k, j).wait()

            settle(
                [(give_w(theirs, other), forward_w(theirs)),
                 (give_rows(here, other), forward_rows(here))]
            )
            give_mod(mod_theirs, other).wait_recv()
            for copy in loads:
                copy.wait()

    for copy in tables:
        copy.wait()

    def pushed(step):
        return (
            ((role == 0) & (step < 4)) | (role == 1) | ((role >= 2) & (lax.rem(step, 4) == 3))
        ) & (step >= 0)

    def wait_pushed(step):
        @pl.when(pushed(step))
        def _():
            for j in range(2):
                at = pl.ds(j * BLK, BLK)
                remote(
                    ov.at[at], xf.at[0, at], push_sem.at[j], xf_sem.at[0, j], partner
                ).wait_send()

    def push(j, dst, recv, segment):
        remote(ov.at[block_rows(j)], dst, push_sem.at[j], recv, device(segment, c)).start()

    def att_f(step, mb):
        length = lens[mb]

        @pl.when(role == 0)
        def _():
            @pl.when(lax.rem(mb, 2) != c)
            def _():
                remote(
                    xs.at[0], xa.at[mb], x_send.at[0], xa_oth.at[mb, 0], partner
                ).wait_recv()

            load = local_copy(xa.at[mb], xv, ld.at[0])
            load.start()
            load.wait()

        def forward(j):
            at = block_rows(c + 2 * j)
            return remote(xa.at[mb, at], xa.at[mb, at], fwd_send.at[j], xa_oth.at[mb, j], partner)

        @pl.when(role != 0)
        def _():
            for j in range(2):
                at = block_rows(c + 2 * j)
                remote(
                    ov.at[pl.ds(j * BLK, BLK)], xa.at[mb, at], push_sem.at[j], xa_own.at[mb, j],
                    partner,
                ).wait_recv()
                forward(j).start()
                local_copy(xa.at[mb, at], xv.at[at], ld.at[j]).start()
            for j in range(2):
                at = block_rows(1 - c + 2 * j)
                remote(
                    xa.at[mb, at], xa.at[mb, at], fwd_send.at[j], xa_oth.at[mb, j], partner
                ).wait_recv()
                local_copy(xa.at[mb, at], xv.at[at], ld.at[2 + j]).start()
            for j in range(2):
                at, to = block_rows(c + 2 * j), block_rows(1 - c + 2 * j)
                local_copy(xa.at[mb, at], xv.at[at], ld.at[j]).wait()
                local_copy(xa.at[mb, to], xv.at[to], ld.at[2 + j]).wait()
                forward(j).wait_send()

        off, scl, gat = moda[mb, 0:1, :], 1.0 + moda[mb, 1:2, :], moda[mb, 2:3, :]

        def kv_block(b, carry):
            rows = block_rows(b)
            norm, _ = norm_parts(xv[rows, :].astype(f32))
            n = (norm * scl + off).astype(bf16)
            nv[rows, :] = n
            cosine, sine = cv[rows, :], sv[rows, :]
            kk = dot(n, wa[:, D : 2 * D])
            for p in range(6):
                ls = slice(p * 128, (p + 1) * 128)
                kvv[rows, ls] = turn(kk[:, ls], cosine, sine).astype(bf16)
            vv[rows, :] = dot(n, wa[:, 2 * D : 3 * D]).astype(bf16)
            return carry

        lax.fori_loop(0, 4, kv_block, 0)

        def q_block(j, carry):
            nat = block_rows(c + 2 * j)
            rows = block_rows(j)
            cosine, sine = cv[nat, :] * 0.125, sv[nat, :] * 0.125
            qq = dot(nv[nat, :], wa[:, 0:D])
            for p in range(6):
                ls = slice(p * 128, (p + 1) * 128)
                h0[rows, ls] = turn(qq[:, ls], cosine, sine).astype(bf16)
            return carry

        lax.fori_loop(0, 2, q_block, 0)
        sends = Copies(osem)
        sends.add(h0, st.at[QS, mb])
        sends.add(kvv, kv.at[0, mb])
        sends.add(vv, kv.at[1, mb])
        lane = lax.broadcasted_iota(i32, (BLK, 128), 1)
        position = lax.broadcasted_iota(i32, (1, SEQ_LEN), 1)
        bias = jnp.where(position < length, 0.0, -1e30).astype(f32)
        lv[...] = jnp.zeros((HALF, 128), f32)
        wait_pushed(step - 1)

        def block(j, carry):
            rows = block_rows(j)

            def pair(hp, carry):
                ls = lanes(hp)
                k2, v2, q2 = kvv[:, ls], vv[:, ls], h0[rows, ls]
                outs, stats = [], lv[rows, :]
                for a in range(2):
                    s = dot_nt(jnp.where((lane < 64) == (a == 0), q2, jnp.zeros_like(q2)), k2)
                    s = s + bias
                    m = jnp.max(s, axis=1, keepdims=True)
                    e = jnp.exp(s - m)
                    total = jnp.sum(e, axis=1, keepdims=True)
                    outs.append(dot(e.astype(bf16), v2) / total)
                    stats = jnp.where(lane == 2 * hp + a, m + jnp.log(total), stats)
                h1[rows, ls] = jnp.where(lane < 64, outs[0], outs[1]).astype(bf16)
                lv[rows, :] = stats
                return carry

            lax.fori_loop(0, HEADS // 2, pair, 0)
            branch = dot(h1[rows, :], wa[:, 3 * D : 4 * D])
            live = live_column(BLK, c, length, j * BLK)
            x = xv[block_rows(c + 2 * j), :].astype(f32)
            ov[rows, :] = (x + jnp.where(live, gat * branch, 0.0)).astype(bf16)
            h2[rows, :] = branch.astype(bf16)
            pl.when(role == 0)(lambda: push(j, xf.at[mb, rows], xf_sem.at[mb, j], 1))
            return carry

        lax.fori_loop(0, 2, block, 0)
        sends.add(h1, st.at[AT, mb])
        sends.add(h2, st.at[BR, mb])
        sends.add(lv, lse.at[mb])

        @pl.when(role != 0)
        def _():
            to_ff = local_copy(ov, xf.at[mb], ld.at[0])
            to_ff.start()
            to_ff.wait()

        sends.wait()

    def ff_f(step, mb):
        length = lens[mb]
        off, scl, gat = modf[mb, 0:1, :], 1.0 + modf[mb, 1:2, :], modf[mb, 2:3, :]
        wait_pushed(step - 1)

        def block(j, carry):
            rows = block_rows(j)

            @pl.when(role == 1)
            def _():
                remote(
                    ov.at[rows], xf.at[mb, rows], push_sem.at[j], xf_sem.at[mb, j], partner
                ).wait_recv()

            load = local_copy(xf.at[mb, rows], h0.at[rows], ld.at[0])
            load.start()
            load.wait()
            x = h0[rows, :].astype(f32)
            norm, _ = norm_parts(x)
            h1[rows, :] = (norm * scl + off).astype(bf16)
            accv[rows, :] = jnp.zeros((BLK, D), f32)

            def part(p, carry):
                at = pl.ds(pl.multiple_of(p * D, D), D)
                u = dot(h1[rows, :], w1[:, at])
                t, _ = gelu_parts(u)
                accv[rows, :] += dot((0.5 * u * (1.0 + t)).astype(bf16), w2[at, :])
                return carry

            lax.fori_loop(0, 4, part, 0)
            acc = accv[rows, :]
            live = live_column(BLK, c, length, j * BLK)
            ov[rows, :] = (h0[rows, :].astype(f32) + jnp.where(live, gat * acc, 0.0)).astype(bf16)
            h2[rows, :] = acc.astype(bf16)

            @pl.when(role == 1)
            def _():
                push(j, xa.at[mb, block_rows(c + 2 * j)], xa_own.at[mb, j], 2 + lax.rem(mb, 2))

            return carry

        lax.fori_loop(0, 2, block, 0)
        sends = Copies(osem)
        sends.add(h2, st.at[BF, mb])

        @pl.when(role != 1)
        def _():
            final = local_copy(ov, fin.at[mb], ld.at[0])
            final.start()
            final.wait()

        sends.wait()

    def ff_b(step, mb):
        length = lens[mb]
        off, scl, gat = modf[mb, 0:1, :], 1.0 + modf[mb, 1:2, :], modf[mb, 2:3, :]
        loads = [
            local_copy(xf.at[mb], h0, ld.at[0]),
            local_copy(st.at[BF, mb], h2, ld.at[1]),
        ]
        for copy in loads:
            copy.start()
        dmv[...] = jnp.zeros((8, D), f32)
        for copy in loads:
            copy.wait()
        wait_pushed(step - 1)

        def block(j, carry):
            rows = block_rows(j)

            @pl.when((role == 1) | (lax.rem(mb, 2) != c))
            def _():
                remote(
                    ov.at[rows], gf.at[mb, rows], push_sem.at[j], gf_sem.at[mb, j], partner
                ).wait_recv()

            load = local_copy(gf.at[mb, rows], h1.at[rows], ld.at[2])
            load.start()
            load.wait()
            norm, _ = norm_parts(h0[rows, :].astype(f32))
            h3[rows, :] = (norm * scl + off).astype(bf16)
            live = live_column(BLK, c, length, j * BLK)
            gl = jnp.where(live, h1[rows, :].astype(f32), 0.0)
            h4[rows, :] = (gl * gat).astype(bf16)
            dmv[2:3, :] += jnp.sum(gl * h2[rows, :].astype(f32), axis=0, keepdims=True)
            accv[rows, :] = jnp.zeros((BLK, D), f32)

            def part(p, carry):
                cols = pl.ds(pl.multiple_of(p * D, D), D)
                u = dot(h3[rows, :], w1[:, cols])
                t, u2 = gelu_parts(u)
                half = 0.5 * (1.0 + t)
                actv[rows, cols] = (u * half).astype(bf16)
                slope = half + 0.5 * u * (1.0 - t * t) * (
                    0.7978845608028654 * (1.0 + 3 * 0.044715 * u2)
                )
                du = (dot_nt(h4[rows, :], w2[cols, :]) * slope).astype(bf16)
                duv[rows, cols] = du
                accv[rows, :] += dot_nt(du, w1[:, cols])
                return carry

            lax.fori_loop(0, 4, part, 0)
            acc = accv[rows, :]
            n, rstd = norm_parts(h0[rows, :].astype(f32))
            dmv[0:1, :] += jnp.sum(acc, axis=0, keepdims=True)
            dmv[1:2, :] += jnp.sum(acc * n, axis=0, keepdims=True)
            ov[rows, :] = (h1[rows, :].astype(f32) + norm_back(acc, n, rstd, scl)).astype(bf16)
            pl.when(role == 1)(lambda: push(j, ga.at[mb, rows], ga_sem.at[mb, j], 0))
            return carry

        lax.fori_loop(0, 2, block, 0)
        sends = Copies(osem)
        sends.add(h3, st.at[NF, mb])
        sends.add(h4, st.at[GB, mb])
        sends.add(duv, yf.at[mb])
        sends.add(actv, act.at[mb])
        sends.add(dmv, dmf.at[mb])

        @pl.when(role != 1)
        def _():
            to_att = local_copy(ov, ga.at[mb], ld.at[0])
            to_att.start()
            to_att.wait()

        sends.wait()

    def att_b(step, mb):
        length = lens[mb]
        off, scl, gat = moda[mb, 0:1, :], 1.0 + moda[mb, 1:2, :], moda[mb, 2:3, :]
        gv, atv, qv, gbv, dov, dqv, xo, brv, no = h0, h1, h2, h3, h4, h5, h6, h7, h8
        loads = [
            local_copy(st.at[QS, mb], qv, ld.at[0]),
            local_copy(kv.at[0, mb], kvv, ld.at[1]),
            local_copy(kv.at[1, mb], vv, ld.at[2]),
            local_copy(st.at[AT, mb], atv, ld.at[3]),
            local_copy(lse.at[mb], lv, ld.at[4]),
            local_copy(st.at[BR, mb], brv, ld.at[5]),
        ]
        for j in range(2):
            loads.append(
                local_copy(
                    xa.at[mb, block_rows(c + 2 * j)], xo.at[pl.ds(j * BLK, BLK)], ld.at[6 + j]
                )
            )
        for copy in loads:
            copy.start()
        dmv[...] = jnp.zeros((8, D), f32)

        def grad_block(j, carry):
            rows = block_rows(j)

            @pl.when(role == 0)
            def _():
                remote(
                    ov.at[rows], ga.at[mb, rows], push_sem.at[j], ga_sem.at[mb, j], partner
                ).wait_recv()

            load = local_copy(ga.at[mb, rows], gv.at[rows], ld.at[8])
            load.start()
            load.wait()
            live = live_column(BLK, c, length, j * BLK)
            gb = jnp.where(live, gv[rows, :].astype(f32) * gat, 0.0).astype(bf16)
            gbv[rows, :] = gb
            dov[rows, :] = dot_nt(gb, wa[:, 3 * D : 4 * D]).astype(bf16)
            return carry

        lax.fori_loop(0, 2, grad_block, 0)
        sends = Copies(osem)
        sends.add(gbv, y.at[mb, :, pl.ds(3 * D, D)])
        for copy in loads:
            copy.wait()
        lane = lax.broadcasted_iota(i32, (HALF, 128), 1)
        position = lax.broadcasted_iota(i32, (1, SEQ_LEN), 1)
        bias = jnp.where(position < length, 0.0, -1e30).astype(f32)

        def pair(hp, carry):
            ls = lanes(hp)
            k2, v2 = kvv[:, ls], vv[:, ls]
            q2, do2 = qv[:, ls], dov[:, ls]
            q2t, do2t = q2.T, do2.T
            both = do2.astype(f32) * atv[:, ls].astype(f32)
            stats = lv[...]
            dqs = []
            for a in range(2):
                head = (lane < 64) == (a == 0)
                zero = jnp.zeros_like(q2)
                s = dot_nt(jnp.where(head, q2, zero), k2) + bias
                base = jnp.sum(jnp.where(lane == 2 * hp + a, stats, 0.0), axis=1, keepdims=True)
                p = jnp.exp(s - base)
                dp_ = dot_nt(jnp.where(head, do2, zero), v2)
                delta = jnp.sum(jnp.where(head, both, 0.0), axis=1, keepdims=True)
                ds = (p * (dp_ - delta)).astype(bf16)
                dqs.append(dot(ds, k2))
                at = pl.ds(pl.multiple_of(hp * 128 + a * 64, 64), 64)
                dkt[at, :] = dot(q2t[a * 64 : (a + 1) * 64, :], ds).astype(bf16)
                dvt[at, :] = dot(do2t[a * 64 : (a + 1) * 64, :], p.astype(bf16)).astype(bf16)
            dqv[:, ls] = jnp.where(lane < 64, dqs[0], dqs[1]).astype(bf16)
            return carry

        lax.fori_loop(0, HEADS // 2, pair, 0)
        gives = []
        for part, grad in enumerate((dkt, dvt)):
            for j in range(2):
                give = remote(
                    grad.at[:, block_rows(1 - c + 2 * j)],
                    rcvv.at[mb, part, :, pl.ds(j * BLK, BLK)],
                    dkv_send.at[part, j], dkv_recv.at[mb, part, j], partner,
                )
                give.start()
                gives.append(give)
        wait_pushed(step - 1)
        for give in gives:
            give.wait()

        def last(j, carry):
            rows, nat = block_rows(j), block_rows(c + 2 * j)
            cosine, sine = cv[nat, :], -sv[nat, :]
            for p in range(6):
                ls = slice(p * 128, (p + 1) * 128)
                dpv[rows, ls] = (turn(dqv[rows, ls].astype(f32), cosine, sine) * 0.125).astype(bf16)
                for part, own in enumerate((dkt, dvt)):
                    total = own[ls, nat].astype(f32) + rcvv[mb, part, ls, rows].astype(f32)
                    grad = total.T
                    if part == 0:
                        grad = turn(grad.astype(bf16).astype(f32), cosine, sine)
                    dpv[rows, (part + 1) * D + p * 128 : (part + 1) * D + (p + 1) * 128] = (
                        grad.astype(bf16)
                    )
            acc = dot_nt(dpv[rows, :], wa[:, 0 : 3 * D])
            n, rstd = norm_parts(xo[rows, :].astype(f32))
            no[rows, :] = (n * scl + off).astype(bf16)
            g = gv[rows, :].astype(f32)
            live = live_column(BLK, c, length, j * BLK)
            gl = jnp.where(live, g, 0.0)
            dmv[0:1, :] += jnp.sum(acc, axis=0, keepdims=True)
            dmv[1:2, :] += jnp.sum(acc * n, axis=0, keepdims=True)
            dmv[2:3, :] += jnp.sum(gl * brv[rows, :].astype(f32), axis=0, keepdims=True)
            ov[rows, :] = (g + norm_back(acc, n, rstd, scl)).astype(bf16)
            pl.when(role != 0)(lambda: push(j, gf.at[mb, rows], gf_sem.at[mb, j], 1))
            return carry

        lax.fori_loop(0, 2, last, 0)
        sends.add(dpv, y.at[mb, :, pl.ds(0, 3 * D)])
        sends.add(no, st.at[NM, mb])
        sends.add(dmv, dma.at[mb])

        @pl.when(role == 0)
        def _():
            final = local_copy(ov, fin.at[mb], ld.at[0])
            final.start()
            final.wait()

        sends.wait()

    def run(step, carry):
        first = step < 4
        kind = jnp.where(
            role == 0, jnp.where(first, ATT_F, ATT_B),
            jnp.where(role == 1, jnp.where(first, FF_F, FF_B), lax.rem(step, 4)),
        )
        mb = jnp.where(role < 2, lax.rem(step, 4), lax.div(step, 4) * 2 + role - 2)
        for which, work in ((ATT_F, att_f), (FF_F, ff_f), (FF_B, ff_b), (ATT_B, att_b)):
            pl.when(kind == which)(functools.partial(work, step, mb))
        return carry

    lax.fori_loop(0, 8, run, 0)
    wait_pushed(7)

    @pl.when(role == 0)
    def _():
        for k in range(2):
            give_x(k).wait_send()
        give_rows(rows_half, 1).wait_send()

    for who in (2, 3):

        @pl.when(role == who)
        def _():
            other = 5 - who
            mine, mod_mine = (wa, moda) if who == 2 else (w1, modf)
            there = rows_half if who == 2 else high_half
            give_mod(mod_mine, other).wait_send()
            give_w(mine, other).wait_send()
            give_rows(there, other).wait_send()

            @pl.when(c == who - 2)
            def _():
                for k in range(2):
                    for j in range(2):
                        give_c(k, j).wait_send()


def chain(lens, xs, cs, w, rows2, cos, sin, mod):
    def sems(*dims):
        return pltpu.SemaphoreType.DMA(dims)

    outs = [shape((MB, SEQ_LEN, D)), shape((MB, HALF, D)), shape((MB, HALF, D)), shape((MB, HALF, D)),
            ST, KV, LSE, YS, YS, YS, DM, DM, shape((MB, HALF, D))]
    table = vm((SEQ_LEN, 128), f32)
    return pl.pallas_call(
        chain_kernel,
        out_shape=outs,
        in_specs=[pl.BlockSpec(memory_space=pltpu.SMEM)] + [ANY] * 7,
        out_specs=[ANY] * len(outs),
        scratch_shapes=[
            vm((D, FF)), vm((D, FF)), vm((FF, D)), FV, FV, FV, FV,
            HV, HV, HV, HV, HV, HV, HV, HV, HV, HV, vm((HALF, 128), f32), table, table,
            vm((D, SEQ_LEN)), vm((D, SEQ_LEN)), vm((MB, 2, D, HALF)), vm((HALF, 3 * D)),
            vm((HALF, FF)), vm((HALF, FF)), vm((HALF, D), f32), vm((8, D), f32),
            vm((MB, 8, D), f32), vm((MB, 8, D), f32),
            sems(3), sems(3), sems(2), sems(2), sems(2), sems(MB, 2), sems(MB, 2), sems(2),
            sems(2, 2), sems(MB, 2), sems(MB, 2), sems(MB, 2), sems(2), sems(2, 2),
            sems(MB, 2, 2), sems(12), sems(10),
        ],
        compiler_params=pltpu.CompilerParams(
            vmem_limit_bytes=62 << 20, collective_id=0, has_side_effects=True
        ),
        cost_estimate=cost(300),
        name="layers",
    )(lens, xs, cs, w, rows2, cos, sin, mod)


def time_cond(steps):
    half_width = D // 2
    frequency = jnp.exp(
        jnp.arange(half_width, dtype=f32) * (-math.log(10000.0) / half_width)
    )
    angles = steps.astype(f32)[:, None] * frequency[None, :]
    return jax.nn.silu(jnp.concatenate([jnp.cos(angles), jnp.sin(angles)], axis=1))


def rope_tables():
    inverse = np.exp(np.arange(32, dtype=np.float32) * np.float32(-math.log(10000.0) / 32))
    angles = np.arange(SEQ_LEN, dtype=np.float32)[:, None] * inverse[None, :]
    cosine, sine = np.cos(angles), np.sin(angles)
    return (
        np.concatenate([cosine] * 4, axis=1).astype(np.float32),
        np.concatenate([-sine, sine, -sine, sine], axis=1).astype(np.float32),
    )


def local(block_input, cotangent, lengths, steps, mod_weight, mod_bias, first_weight, down_rows):
    ndp = lax.axis_size("dp")
    seg, dp = lax.axis_index("segment"), lax.axis_index("dp")
    core, chips, place = dp % 2, ndp // 2, dp // 2
    w, rows2 = first_weight[0], down_rows[0]

    def across(value, moves):
        pairs = [
            (r * ndp + 2 * i + c, q * ndp + 2 * i + e) for (r, c), (q, e) in moves for i in range(chips)
        ]
        return lax.ppermute(value, ("segment", "dp"), pairs)

    def swap(value, roles=(0, 1, 2, 3)):
        return across(value, [((r, c), (r, 1 - c)) for r in roles for c in range(2)])

    def hop(value, pairs):
        return lax.ppermute(value, "segment", pairs)

    def after(value, other):
        return lax.optimization_barrier((value, other))[0]

    info = jnp.stack([lengths, steps])
    other_info = swap(info)
    full = (lengths[1] > lengths[0]).astype(i32)
    xs = jnp.where(full == 0, block_input, block_input[::-1])
    cs = jnp.where(full == 0, cotangent, cotangent[::-1])
    info0 = jnp.where(core == 0, info, other_info)
    info1 = jnp.where(core == 0, other_info, info)
    full0 = (info0[0, 1] > info0[0, 0]).astype(i32)
    full1 = (info1[0, 1] > info1[0, 0]).astype(i32)
    chip = jnp.stack([info0[:, full0], info1[:, full1], info0[:, 1 - full0], info1[:, 1 - full1]])
    lens = chip[:, 0]
    sc = jnp.concatenate([jnp.stack([seg, core]), lens]).astype(i32)
    conditions = time_cond(chip[:, 1]).astype(bf16)
    modulation = jnp.dot(conditions, mod_weight[0], preferred_element_type=f32)
    modulation = modulation + mod_bias[0].astype(f32)
    mod = jnp.pad(modulation.reshape(MB, 3, D), ((0, 0), (0, 5), (0, 0)))
    cos, sin = (jnp.asarray(t) for t in rope_tables())
    _, _, _, _, st, _, _, y, yf, act, dma, dmf, fin = chain(lens, xs, cs, w, rows2, cos, sin, mod)

    depth, wide_rows = D // ndp, FF // 2 // ndp

    def weight_grad(kind, chosen, right):
        turns = np.array([chosen.get(r, 0) for r in range(4)], np.int32)
        pairs = pltpu.SemaphoreType.DMA((2,))
        return pl.pallas_call(
            functools.partial(weight_grad_kernel, kind),
            grid_spec=pltpu.PrefetchScalarGridSpec(
                num_scalar_prefetch=2,
                grid=(1,),
                in_specs=[ANY, ANY],
                out_specs=ANY,
                scratch_shapes=[
                    vm((MB, HALF, D)), vm((D, MB * HALF)), vm((2, MB, HALF, D)), vm((D, D), f32),
                    vm((2, D, D)), pairs, pairs, pairs,
                ],
            ),
            out_shape=shape((FF, D) if kind == "down" else (D, FF)),
            compiler_params=pltpu.CompilerParams(vmem_limit_bytes=VLIM),
            cost_estimate=cost(12),
            name=kind + "_gradient",
        )(sc, turns, st, right)

    def ff_grads(chosen):
        up = weight_grad("up", chosen, yf)
        down = weight_grad("down", chosen, act).reshape(2 * ndp, wide_rows, D)
        return up.reshape(ndp, depth, FF), down[:ndp], down[ndp:]

    def owned(ac, bd):
        keep = jnp.where(core == 0, ac, bd)
        give = jnp.where(core == 0, bd, ac)
        return jnp.where(core == seg % 2, keep, swap(give))

    masks = {2: 5, 3: 10}
    att_23 = weight_grad("attention", {0: 15, **masks}, y).reshape(ndp, depth, FF)
    up_x, low_x, high_x = ff_grads({1: 15, **masks})
    first_23, rows_23 = reduced(
        (att_23, up_x, low_x, high_x), (2, 3), ([0, 2], [1, 3]), ([1, 3], [0, 2]), chips, 1,
        "second_layer_sums",
    )
    up_1, low_1, high_1 = reduced(
        (up_x, low_x, high_x), (1,), ([0, 1, 2],), ([],), chips, 2, "feedforward_sums"
    )
    (first_0,) = reduced((att_23,), (0,), ([0],), ([],), chips, 3, "attention_sums")
    low_0 = hop(after(low_1, first_0), [(1, 0)])
    even = seg % 2 == 0
    first_sum = jnp.where(seg == 0, first_0, jnp.where(seg == 1, up_1, first_23))
    rows_sum = jnp.where(seg == 0, low_0, jnp.where(seg == 1, high_1, rows_23))

    pairs = fin.reshape(2, 2, HALF, D)
    one, two = pairs[:, 0], pairs[:, 1]
    first_one = across(one[:, :BLK], [((2, c), (c, c)) for c in range(2)])
    first_two = across(two[:, :BLK], [((3, c), (c, c)) for c in range(2)])
    mid = jnp.where(seg == 2, one[:, BLK:], two[:, BLK:])
    crossed = across(mid, [((2, 1), (3, 1)), ((3, 0), (2, 0))])
    outs = owned(
        jnp.where(seg < 2, first_one, jnp.where(seg == 2, mid, crossed)),
        jnp.where(seg < 2, first_two, jnp.where(seg == 2, crossed, mid)),
    )
    to_one = across(pairs[:, :, :BLK], [((0, 1), (1, 1))])
    to_others = across(pairs[:, :, BLK:], [((0, 0), (2, 0)), ((0, 1), (3, 1))])
    got = jnp.where(seg == 0, pairs[:, :, :BLK], jnp.where(seg == 1, to_one, to_others))
    grads = owned(got[:, 0], got[:, 1])

    mine = np.array([[True] * 4, [True] * 4, [True, False] * 2, [False, True] * 2])
    mine = jnp.asarray(mine)[seg][:, None, None]
    dma, dmf = (jnp.where(mine, m[:, :3], 0.0) for m in (dma, dmf))
    sums = jnp.where(even, dma, dmf) + hop(jnp.where(even, dmf, dma), [(2, 3), (3, 2)])
    mod_rows = jnp.concatenate([sums.reshape(MB, 3 * D), conditions.astype(f32)], axis=1)
    all_rows = gathered_rows(mod_rows.reshape(-1, 128), ndp, 4).reshape(ndp * MB, 4 * D)
    mine = lax.dynamic_slice_in_dim(all_rows, 3 * D + dp * depth, depth, axis=1)
    all_rows = all_rows[:, : 3 * D]
    mod_w_sum = jnp.dot(mine.T, all_rows, precision=lax.Precision.HIGHEST, preferred_element_type=f32)
    width = 3 * D // ndp
    mod_b_sum = jnp.sum(lax.dynamic_slice_in_dim(all_rows, dp * width, width, axis=1), axis=0)

    def placed(both, part):
        both = jnp.where(full == 0, both, both[::-1])
        live = (seg * BLK + jnp.arange(BLK))[None, :, None] < lengths[:, None, None]
        return jnp.where(live, both, lax.dynamic_slice_in_dim(part, seg * BLK, BLK, axis=1))

    return (
        placed(outs, block_input),
        placed(grads, cotangent).astype(f32),
        mod_w_sum[None],
        mod_b_sum[None],
        first_sum.astype(f32)[None],
        rows_sum.astype(f32)[None],
    )


def solution(mesh):
    in_specs = (
        P("dp", None, None),
        P("dp", None, None),
        P("dp"),
        P("dp"),
        P("segment", None, None),
        P("segment", None),
        P("segment", None, None),
        P("segment", None, None),
    )
    out_specs = (
        P("dp", "segment", None),
        P("dp", "segment", None),
        P("segment", "dp", None),
        P("segment", "dp"),
        P("segment", "dp", None),
        P("segment", "dp", None),
    )
    return jax.shard_map(local, mesh=mesh, in_specs=in_specs, out_specs=out_specs, check_vma=False)
```

time: 750 us -> 642 us (0.86)
  Pallas kernels: 355 us -> 530 us
  waiting for transfers between devices: 194 us -> 19.8 us
  starting transfers between devices: 117 us -> 40.2 us
  local copies, waits for them, and re-layouts: 45.3 us -> 16.1 us
    pallas_call x27 -> x1, Pallas kernels: 216 us -> 422 us  [chain(): pl.pallas_call(chain_kernel, out_shape=outs, in_specs=[pl.BlockSpec(memor...]
    ppermute x22 -> x2, waiting for transfers between devices: 188 us -> 0.01 us  [hop(): return lax.ppermute(value, 'segment', pairs)]
    ppermute x22 -> x2, starting transfers between devices: 68.7 us -> 1.94 us  [hop(): return lax.ppermute(value, 'segment', pairs)]
    unnamed x153 -> x37, local copies, waits for them, and re-layouts: 24.5 us -> 3.06 us
    pallas_call x3, Pallas kernels: 68.6 us -> 52.6 us  [reduced(): pl.pallas_call(functools.partial(reduce_kernel, roles, chips, mine, their...]
    ppermute x30 -> x8, waiting for transfers between devices: 5.63 us -> 19.8 us  [across(): return lax.ppermute(value, ('segment', 'dp'), pairs)]
    pallas_call x1, Pallas kernels: 49.9 us -> 36.5 us  [gathered_rows(): pl.pallas_call(functools.partial(gather_kernel, size), out_shape=jax.Shap...]
    ppermute x30 -> x8, starting transfers between devices: 47.9 us -> 38.3 us  [across(): return lax.ppermute(value, ('segment', 'dp'), pairs)]
  transfers between devices with their start and end apart: 52 -> 10, of which waited for: 12 -> 2; matrix products, arithmetic and copies ran while one was open for 4% -> 4% of each run, Pallas kernels for 23% -> 6%
where the time goes in v3:
time: 642 us; the launch traced here: 638 us
  Pallas kernels  530 us (83%)
  starting transfers between devices  40.2 us (6%)
  other arithmetic  24.1 us (4%)
  waiting for transfers between devices  19.8 us (3%)
  local copies, waits for them, and re-layouts  16.1 us (3%)
    pallas_call x1, Pallas kernels, chain(): pl.pallas_call(chain_kernel, out_shape=outs, in_specs=[pl.BlockSpec(memor...  422 us
    pallas_call x3, Pallas kernels, reduced(): pl.pallas_call(functools.partial(reduce_kernel, roles, chips, mine, their...  52.6 us
    ppermute x8, starting transfers between devices, across(): return lax.ppermute(value, ('segment', 'dp'), pairs)  38.3 us
    pallas_call x1, Pallas kernels, gathered_rows(): pl.pallas_call(functools.partial(gather_kernel, size), out_shape=jax.Shap...  36.5 us
    ppermute x8, waiting for transfers between devices, across(): return lax.ppermute(value, ('segment', 'dp'), pairs)  19.8 us
    pallas_call x3, Pallas kernels, weight_grad(): pl.pallas_call(functools.partial(weight_grad_kernel, kind), grid_spec=plt...  18.8 us
  transfers between devices with their start and end apart: 10, of which 2 were waited for; matrix products, arithmetic and copies ran while one was open for 4% of the time, Pallas kernels for 6%

profile of v3, /device:TPU:0, one launch (start us, length us, event | category | flops | bytes accessed | tf_op | source)
XLA Modules:
  0.0 637.6 jit_solution(17431998317143762199)
XLA Ops:
  2.4 1.3 fusion.25
  3.7 0.7 convert_reduce_fusion
  5.7 1.3 broadcast_compare_fusion
  7.0 1.2 fusion.12
  8.3 9.0 %reverse_select_fusion = (bf16[2,1024,768]{2,1,0:T(8,128)(2,1)}, bf16[2,1024,768]{2,1,0:T(8,128)(2,1)}) fusion(bf16[2,1024,768]{2,1,0:T(8,128)(2,1)} %param.15, pred[]{:T(512)} %bitcast, bf16[2,1024,768]{2,1,0:T(8,128)(2,1)} %param.14), kind=kLoop, calls=%fused_computation | loop fusion | flops 3145728 | bytes 12582913 | tf_op jit(solution)/shard_map/jit(_where)/select_n | solution.py:1057
  22.2 1.0 fusion.13
  23.5 0.8 multiply_cosine_fusion
  26.2 422.0 %layers.1 = (bf16[4,1024,768]{2,1,0:T(8,128)(2,1)}, bf16[4,512,768]{2,1,0:T(8,128)(2,1)}, bf16[4,512,768]{2,1,0:T(8,128)(2,1)}, bf16[4,512,768]{2,1,0:T(8,128)(2...) custom-call(s32[4]{0:T(128)} %copy-done.16, ...), custom_call_target="tpu_custom_call" | custom-call | flops 299999985664 | bytes 1048576 | tf_op jit(solution)/shard_map/layers/pallas_call | solution.py:990
  448.2 0.7 down_gradient.1
  449.0 4.8 fusion.20
  453.8 0.7 up_gradient.1
  454.6 17.3 %attention_gradient.1 = bf16[768,3072]{1,0:T(8,128)(2,1)} custom-call(s32[6]{0:T(128)} %pad_add_fusion.2.sc, s32[4]{0:T(128)} %constant.71.clone.tt, bf16[10,4,512,768]{3,2,1,0:T(8,128)(2,1)} %get-tuple-element.22.st, bf16[4,512,3072]{2,1,0:T(8,128)(2,1)} %get-tuple-element.23.y), custom_call_target="tpu_custom_call" | custom-call | flops 12000000000 | bytes 1048576 | tf_op jit(solution)/shard_map/attention_gradient/pallas_call | solution.py:1077
  471.9 50.4 %attention_sums.1 = f32[96,3072]{1,0:T(8,128)} custom-call(bf16[8,96,3072]{2,1,0:T(8,128)(2,1)} %bitcast.51), custom_call_target="tpu_custom_call" | custom-call | flops 60000002048 | bytes 1048576 | tf_op jit(solution)/shard_map/attention_sums/pallas_call | solution.py:350
  522.4 0.8 feedforward_sums.1
  523.2 1.3 second_layer_sums.1
  527.1 0.8 collective-permute-start.5
  528.0 16.2 %collective-permute-start.6 = (bf16[2,2,256,768]{3,2,0,1:T(8,128)(2,1)S(1)}, bf16[2,2,256,768]{3,2,0,1:T(8,128)(2,1)S(1)}, u32[]{:S(2)}, u32[]{:S(2)}) collective-permute-start(bf16[2,2,256,768]{3,2,0,1:T(8,128)(2,1)S(1)} %copy.32), channel_id=1, source_target_pairs={{0,16},{2,18},{4,20},{6,22},{1,25},{3,27},{5,29},{7,31}} | collective-permute-start | bytes 4718600 | tf_op jit(solution)/shard_map/ppermute | solution.py:1042
  544.9 1.4 collective-permute-start.1
  546.3 0.7 collective-permute-start.2
  547.0 1.3 collective-permute-start.3
  548.4 1.2 select_bitcast_fusion
  549.7 9.2 %collective-permute-done.1 = bf16[2,256,768]{2,1,0:T(8,128)(2,1)S(1)} collective-permute-done((bf16[2,256,768]{2,1,0:T(8,128)(2,1)S(1)}, bf16[2,256,768]{2,1,0:T(8,128)(2,1)S(1)}, u32[]{:S(2)}, u32[]{:S(2)}) %collective-permute-start.1) | collective-permute-done | bytes 786464 | tf_op jit(solution)/shard_map/ppermute | solution.py:1042
  558.9 1.3 collective-permute-start.9
  560.2 10.6 %collective-permute-done.3 = bf16[2,256,768]{2,1,0:T(8,128)(2,1)S(1)} collective-permute-done((bf16[2,256,768]{2,1,0:T(8,128)(2,1)S(1)}, bf16[2,256,768]{2,1,0:T(8,128)(2,1)S(1)}, u32[]{:S(2)}, u32[]{:S(2)}) %collective-permute-start.3) | collective-permute-done | bytes 786464 | tf_op jit(solution)/shard_map/ppermute | solution.py:1042
  570.7 1.1 broadcast_select_fusion
  572.1 1.0 select_bitcast_fusion.1
  573.0 17.5 %collective-permute-start.7 = (bf16[2,256,768]{2,1,0:T(8,128)(2,1)}, bf16[2,256,768]{2,1,0:T(8,128)(2,1)}, u32[]{:S(2)}, u32[]{:S(2)}) collective-permute-start(bf16[2,256,768]{2,1,0:T(8,128)(2,1)} %select_bitcast_fusion.1), channel_id=1, source_target_pairs={{0,1},{2,3},{4,5},{6,7},{1,0},{3,2},{5,4},{7,6},{8,9},{10,11},{12,... | collective-permute-start | bytes 2359304 | tf_op jit(solution)/shard_map/ppermute | solution.py:1042
  591.1 36.5 %gather_sums.1 = f32[8,96,128]{2,1,0:T(8,128)} custom-call(f32[96,128]{1,0:T(8,128)} %reshape.96.rows), custom_call_target="tpu_custom_call" | custom-call | tf_op jit(solution)/shard_map/gather_sums/pallas_call | solution.py:326
  627.7 1.1 reshape.97
  629.4 1.9 convolution_bitcast_fusion
  631.3 2.2 select_bitcast_fusion.2
  634.3 3.3 fusion.7
  (75 shorter events, 12.0 us)
Async XLA Ops:
  1.3 15.9 %collective-permute-start = (s32[2,2]{1,0:T(2,128)S(1)}, s32[2,2]{1,0:T(2,128)}, u32[]{:S(2)}, u32[]{:S(2)}) collective-permute-start(s32[2,2]{1,0:T(2,128)S(1)} %pad_add_fusion.1), channel_id=1, source_target_pairs={{0,1},{2,3},{4,5},{6,7},{1,0},{3,2},{5,4},{7,6},{8,9},{10,11},{12,... | collective-permute-start | bytes 56 | tf_op jit(solution)/shard_map/ppermute | solution.py:1042
  8.3 9.0 %copy-start.12 = (s32[2]{0:T(128)S(1)}, s32[2]{0:T(128)}, u32[]{:S(2)}) copy-start(s32[2]{0:T(128)} %param.16) | copy-start | bytes 28
  8.3 9.0 %copy-start.15 = (s32[2]{0:T(128)S(1)}, s32[2]{0:T(128)}, u32[]{:S(2)}) copy-start(s32[2]{0:T(128)} %param.17) | copy-start | bytes 28
  8.3 16.1 %copy-start.1 = (bf16[1,768,2304]{2,1,0:T(8,128)(2,1)S(1)}, bf16[1,768,2304]{2,1,0:T(8,128)(2,1)}, u32[]{:S(2)}) copy-start(bf16[1,768,2304]{2,1,0:T(8,128)(2,1)} %param.18) | copy-start | bytes 10616836
  17.9 0.6 copy-start.11
  23.5 2.7 copy-start.16
  24.3 1.3 copy-start.7
  24.3 1.3 copy-start.9
  523.2 1.9 copy-start
  525.3 0.9 copy-start.5
  525.3 0.9 copy-start.6
  525.3 0.9 copy-start.14
  526.3 20.7 %collective-permute-start.8 = (f32[4,3,768]{2,1,0:T(4,128)S(1)}, f32[4,3,768]{2,1,0:T(4,128)S(1)}, u32[]{:S(2)}, u32[]{:S(2)}) collective-permute-start(f32[4,3,768]{2,1,0:T(4,128)S(1)} %fusion.8), channel_id=1, source_target_pairs={{16,24},{24,16},{17,25},{25,17},{18,26},{26,18},{19,27},{27,19},{2... | collective-permute-start | bytes 110600 | tf_op jit(solution)/shard_map/ppermute | solution.py:1048
  527.1 44.7 %collective-permute-start.5 = (bf16[2,2,256,768]{3,2,0,1:T(8,128)(2,1)S(1)}, bf16[2,2,256,768]{3,2,0,1:T(8,128)(2,1)S(1)}, u32[]{:S(2)}, u32[]{:S(2)}) collective-permute-start(bf16[2,2,256,768]{3,2,0,1:T(8,128)(2,1)S(1)} %copy.31), channel_id=1, source_target_pairs={{1,9},{3,11},{5,13},{7,15}} | collective-permute-start | bytes 4718600 | tf_op jit(solution)/shard_map/ppermute | solution.py:1042
  528.0 43.8 %collective-permute-start.6 = (bf16[2,2,256,768]{3,2,0,1:T(8,128)(2,1)S(1)}, bf16[2,2,256,768]{3,2,0,1:T(8,128)(2,1)S(1)}, u32[]{:S(2)}, u32[]{:S(2)}) collective-permute-start(bf16[2,2,256,768]{3,2,0,1:T(8,128)(2,1)S(1)} %copy.32), channel_id=1, source_target_pairs={{0,16},{2,18},{4,20},{6,22},{1,25},{3,27},{5,29},{7,31}} | collective-permute-start | bytes 4718600 | tf_op jit(solution)/shard_map/ppermute | solution.py:1042
  544.1 0.7 copy-start.8
  544.2 0.7 copy-start.10
  544.2 4.2 copy-start.2
  544.2 4.2 copy-start.3
  544.2 4.2 copy-start.4
  544.9 14.0 %collective-permute-start.1 = (bf16[2,256,768]{2,1,0:T(8,128)(2,1)S(1)}, bf16[2,256,768]{2,1,0:T(8,128)(2,1)S(1)}, u32[]{:S(2)}, u32[]{:S(2)}) collective-permute-start(bf16[2,256,768]{2,1,0:T(8,128)(2,1)S(1)} %get-tuple-element.47), channel_id=1, source_target_pairs={{16,0},{18,2},{20,4},{22,6},{17,9},{19,11},{21,13},{23,15}} | collective-permute-start | bytes 2359304 | tf_op jit(solution)/shard_map/ppermute | solution.py:1042
  546.3 13.9 %collective-permute-start.2 = (bf16[2,256,768]{2,1,0:T(8,128)(2,1)S(1)}, bf16[2,256,768]{2,1,0:T(8,128)(2,1)S(1)}, u32[]{:S(2)}, u32[]{:S(2)}) collective-permute-start(bf16[2,256,768]{2,1,0:T(8,128)(2,1)S(1)} %get-tuple-element.46), channel_id=1, source_target_pairs={{17,25},{19,27},{21,29},{23,31},{24,16},{26,18},{28,20},{30,22}} | collective-permute-start | bytes 2359304 | tf_op jit(solution)/shard_map/ppermute | solution.py:1042
  547.0 23.7 %collective-permute-start.3 = (bf16[2,256,768]{2,1,0:T(8,128)(2,1)S(1)}, bf16[2,256,768]{2,1,0:T(8,128)(2,1)S(1)}, u32[]{:S(2)}, u32[]{:S(2)}) collective-permute-start(bf16[2,256,768]{2,1,0:T(8,128)(2,1)S(1)} %get-tuple-element.45), channel_id=1, source_target_pairs={{24,0},{26,2},{28,4},{30,6},{25,9},{27,11},{29,13},{31,15}} | collective-permute-start | bytes 2359304 | tf_op jit(solution)/shard_map/ppermute | solution.py:1042
  558.9 72.4 %collective-permute-start.9 = (f32[192,768]{1,0:T(8,128)}, f32[192,768]{1,0:T(8,128)}, u32[]{:S(2)}, u32[]{:S(2)}) collective-permute-start(f32[192,768]{1,0:T(8,128)} %get-tuple-element.29), channel_id=1, source_target_pairs={{8,0},{9,1},{10,2},{11,3},{12,4},{13,5},{14,6},{15,7}} | collective-permute-start | bytes 1769480 | tf_op jit(solution)/shard_map/ppermute | solution.py:1048
  571.8 61.7 %collective-permute-start.4 = (bf16[2,256,768]{2,1,0:T(8,128)(2,1)}, bf16[2,256,768]{2,1,0:T(8,128)(2,1)}, u32[]{:S(2)}, u32[]{:S(2)}) collective-permute-start(bf16[2,256,768]{2,1,0:T(8,128)(2,1)} %get-tuple-element.36), channel_id=1, source_target_pairs={{0,1},{2,3},{4,5},{6,7},{1,0},{3,2},{5,4},{7,6},{8,9},{10,11},{12,... | collective-permute-start | bytes 2359304 | tf_op jit(solution)/shard_map/ppermute | solution.py:1042
  573.0 60.6 %collective-permute-start.7 = (bf16[2,256,768]{2,1,0:T(8,128)(2,1)}, bf16[2,256,768]{2,1,0:T(8,128)(2,1)}, u32[]{:S(2)}, u32[]{:S(2)}) collective-permute-start(bf16[2,256,768]{2,1,0:T(8,128)(2,1)} %select_bitcast_fusion.1), channel_id=1, source_target_pairs={{0,1},{2,3},{4,5},{6,7},{1,0},{3,2},{5,4},{7,6},{8,9},{10,11},{12,... | collective-permute-start | bytes 2359304 | tf_op jit(solution)/shard_map/ppermute | solution.py:1042
  633.6 0.7 copy-start.13

commit v4 on v3

v4 whole, which is shorter than its diff:
```python
import functools
import math

import jax
import jax.numpy as jnp
import numpy as np
from jax import lax
from jax.experimental import pallas as pl
from jax.experimental.pallas import tpu as pltpu
from jax.sharding import PartitionSpec as P

D = 768
HEADS = 12
HEAD_DIM = 64
FF = 3072
SEQ_LEN = 1024
BLK = 256
HALF = SEQ_LEN // 2
MB = 4
QS, AT, BR, NM, BF, NF, GB = range(7)
VLIM = 56 << 20
bf16, f32, i32 = jnp.bfloat16, jnp.float32, jnp.int32


def dot(a, b):
    return lax.dot_general(a, b, (((1,), (0,)), ((), ())), preferred_element_type=f32)


def dot_nt(a, b):
    return lax.dot_general(a, b, (((1,), (1,)), ((), ())), preferred_element_type=f32)


def dot_tn(a, b):
    return lax.dot_general(a, b, (((0,), (0,)), ((), ())), preferred_element_type=f32)


def block_rows(b):
    return pl.ds(pl.multiple_of(b * BLK, BLK), BLK)


def lanes(p):
    return pl.ds(pl.multiple_of(p * 128, 128), 128)


def norm_parts(x):
    center = x - jnp.mean(x, axis=-1, keepdims=True)
    rstd = lax.rsqrt(jnp.mean(center * center, axis=-1, keepdims=True) + 1e-06)
    return center * rstd, rstd


def norm_back(d_normed, n, rstd, scl):
    dn = d_normed * scl
    return (
        dn - jnp.mean(dn, axis=-1, keepdims=True) - n * jnp.mean(dn * n, axis=-1, keepdims=True)
    ) * rstd


def turn(v, cosine, sine):
    lane = lax.broadcasted_iota(i32, v.shape, 1)
    partner = jnp.where(lane % 64 < 32, pltpu.roll(v, 96, 1), pltpu.roll(v, 32, 1))
    return v * cosine + partner * sine


def live_column(c, length, j):
    r = lax.broadcasted_iota(i32, (BLK, 1), 0) + BLK * (c + 2 * j)
    return r.astype(f32) < length


def gelu_parts(u):
    u2 = u * u
    t = jnp.tanh(0.7978845608028654 * (u * (1.0 + 0.044715 * u2)))
    return t, u2


def weight_grad_kernel(kind, roles, st, y, out, xv, yv, acc, ov, xsem, ysem, osem):
    role = lax.axis_index("segment")
    parts = jnp.where(role < 2, 2, 1)

    def tile(j):
        return y.at[:, :, pl.ds(pl.multiple_of(j * D, D), D)]

    def into(j):
        at = pl.ds(pl.multiple_of(j * D, D), D)
        return out.at[at] if kind == "down" else out.at[:, at]

    def load_x(which):
        return pltpu.make_async_copy(st.at[which], xv, xsem.at[0])

    def load_y(j):
        slot = lax.rem(j, 2)
        return pltpu.make_async_copy(tile(j), yv.at[slot], ysem.at[slot])

    def store(j):
        slot = lax.rem(j, 2)
        return pltpu.make_async_copy(ov.at[slot], into(j), osem.at[slot])

    chosen = functools.reduce(jnp.logical_or, [role == r for r in roles])

    @pl.when(chosen)
    def _():
        load_x(GB if kind == "down" else NM if kind == "attention" else NF).start()
        load_y(0).start()
        load_x(0).wait()

        def step(j, carry):
            slot = lax.rem(j, 2)
            pl.when(j < 3)(lambda: load_y(j + 1).start())
            load_y(j).wait()
            if kind == "attention":

                @pl.when(j == 3)
                def _():
                    load_x(AT).start()
                    load_x(AT).wait()

            def product(h):
                if kind == "down":
                    return dot_tn(yv[slot, h], xv[h])
                return dot_tn(xv[h], yv[slot, h])

            pl.when(j >= 2)(lambda: store(j - 2).wait())

            @pl.when(parts == 1)
            def _():
                ov[slot] = product(0).astype(bf16)

            @pl.when(parts == 2)
            def _():
                acc[...] = product(0)
                ov[slot] = (acc[...] + product(1)).astype(bf16)

            store(j).start()
            return carry

        lax.fori_loop(0, 4, step, 0)
        store(2).wait()
        store(3).wait()


ANY = pl.BlockSpec(memory_space=pl.ANY)
VMEM = pl.BlockSpec(memory_space=pltpu.VMEM)


def shape(dims, dtype=bf16):
    return jax.ShapeDtypeStruct(dims, dtype)


ST = shape((7, 2, SEQ_LEN, D))
KV = shape((2, MB, SEQ_LEN, D))
LSE = shape((MB, HALF, 128), f32)
YS = shape((2, SEQ_LEN, FF))
DM = shape((MB, 8, D), f32)
OWNED = shape((2, BLK, D))


def vm(dims, dtype=bf16):
    return pltpu.VMEM(dims, dtype)


HV, FV = vm((HALF, D)), vm((SEQ_LEN, D))


def cost(micros):
    return pl.CostEstimate(flops=int(micros * 1e9), bytes_accessed=1 << 20, transcendentals=0)


MESH = pl.DeviceIdType.MESH


def sums_kernel(
    chips, att, up, down, dma, dmf, mod, fin, first_out, rows_out, gathered, out_g,
    near_w, near_r, tot_w, tot_r, cross_w, cross_r, right_w, right_r, left_w, left_r, res_w, res_r,
    dm_own, dm_near, dm_tot, modv,
    load_sem, near_send, near_recv, cross_send, cross_recv, line_send, right_recv, left_recv,
    dm_load, dm_send, dm_recv, g_send, g_recv, fin_send, fin_recv,
):
    seg, dp = lax.axis_index("segment"), lax.axis_index("dp")
    core, place = lax.rem(dp, 2), lax.div(dp, 2)
    size = 2 * chips

    def device(segment, chip, at):
        return {"segment": segment, "dp": 2 * chip + at}

    def remote(src, dst, send, recv, target):
        return pltpu.make_async_remote_copy(
            src_ref=src, dst_ref=dst, send_sem=send, recv_sem=recv,
            device_id=target, device_id_type=MESH,
        )

    def work(role):
        other = 5 - role if role >= 2 else 1 - role
        second = role >= 2
        low, high = 0, size
        parts = {
            0: {0: (att, 0)},
            1: {0: (up, 0), 1: (down, high), 3: (down, low)},
            2: {0: (att, 0), 1: (down, low), 2: (up, 0), 3: (down, high)},
            3: {0: (up, 0), 1: (down, high), 2: (att, 0), 3: (down, low)},
        }[role]
        kept = 2
        give = [k for k in (0, 1) if k + 2 in parts]
        taken = {0: [1], 1: [], 2: [0, 1], 3: [0, 1]}[role]

        def pick(wide, rows, k):
            return (rows if k % 2 else wide).at[k // 2]

        def near(k):
            return pick(near_w, near_r, k)

        def total(k):
            return pick(tot_w, tot_r, k)

        def right(k):
            return pick(right_w, right_r, k)

        def left(k):
            return pick(left_w, left_r, k)

        def cross(k):
            return pick(cross_w, cross_r, k)

        barrier = pltpu.get_barrier_semaphore()

        def greet(target):
            pl.semaphore_signal(barrier, inc=1, device_id=target, device_id_type=MESH)

        for k in range(1, size):
            greet({"segment": role, "dp": lax.rem(dp + k, size)})
        waits = size - 1
        if role < 2:
            greet(device(1 - role, place, core))
            waits += 1
        else:
            for k in range(size):
                greet({"segment": other, "dp": lax.rem(dp + k, size)})
            waits += size
        if role > 0:
            greet(device(0, place, role % 2))
        else:
            waits += 2 + 2 * core
        pl.semaphore_wait(barrier, waits)

        def each_part(act_local, act_remote):
            for j in range(2):
                segment = core + 2 * j
                for mb in range(MB):
                    src, dst = fin.at[mb, pl.ds(j * BLK, BLK)], out_g.at[mb // 2]
                    here = (segment == 0) & (core == mb % 2)
                    local = pltpu.make_async_copy(src, dst, fin_send.at[mb, j])
                    there = remote(
                        src, dst, fin_send.at[mb, j], fin_recv.at[mb // 2],
                        device(segment, place, mb % 2),
                    )
                    pl.when(here)(functools.partial(act_local, local))
                    pl.when(jnp.logical_not(here))(functools.partial(act_remote, there))

        if role == 0:
            each_part(lambda x: x.start(), lambda x: x.start())

        partner = device(role, place, 1 - core)
        mates = [dma, dmf] if role % 2 == 0 else [dmf, dma]
        mates = mates[: 2 if second else 1]
        def nears(k, z):
            array, base = parts[k]
            return remote(
                array.at[base + 2 * z + 1 - core], near(k).at[z], near_send.at[k, z],
                near_recv.at[k, z], partner,
            )

        for k in sorted(parts, reverse=True):
            array, base = parts[k]
            for z in range(chips):
                nears(k, z).start()
                pltpu.make_async_copy(
                    array.at[base + 2 * z + core], total(k).at[z], load_sem.at[k, z]
                ).start()
        small = []
        for n, rows in enumerate(mates):
            for k in range(2):
                move = remote(
                    rows.at[2 * k + 1 - core], dm_near.at[n, k], dm_send.at[n, k],
                    dm_recv.at[n, k], partner,
                )
                move.start()
                small.append(move)
                load = pltpu.make_async_copy(rows.at[2 * k + core], dm_own.at[n, k], dm_load.at[n, k])
                load.start()
                small.append(load)
        load = pltpu.make_async_copy(mod, modv, dm_load.at[2, 0])
        load.start()
        small.append(load)

        def nth(p):
            near_end = jnp.minimum(place, chips - 1 - place)
            lead = chips - 1 - 2 * near_end
            rest = p - lead
            z = jnp.where(
                rest < 0, chips - 1 - p,
                jnp.where(lax.rem(rest, 2) == 0, 2 * near_end - lax.div(rest, 2), lax.div(rest, 2)),
            )
            return jnp.where(place > chips - 1 - place, chips - 1 - z, z)

        def in_turn(body):
            def turn_at(p, carry):
                z = nth(p)
                pl.when(z > place)(lambda: body(p, z, 1))
                pl.when(z < place)(lambda: body(p, z, -1))
                return carry

            lax.fori_loop(0, chips - 1, turn_at, 0)

        at_end = (place == 0) | (place == chips - 1)

        def line_sent(z):
            for k in range(kept):
                remote(
                    total(k).at[z], right(k).at[z], line_send.at[k, z], right_recv.at[k, z], partner
                ).wait_send()

        def near_add(k, z):
            nears(k, z).wait()
            pltpu.make_async_copy(total(k).at[z], total(k).at[z], load_sem.at[k, z]).wait()
            total(k)[z] = total(k)[z] + near(k)[z]

        def crossing(k, z):
            return remote(
                total(kept + k).at[z], cross(k).at[z], cross_send.at[k, z], cross_recv.at[k, z],
                device(other, place, core),
            )

        def cross_start(z):
            for k in give:
                near_add(kept + k, z)
                crossing(k, z).start()

        def cross_sent(z):
            for k in give:
                crossing(k, z).wait_send()

        cross_start(nth(0))
        for k in (0, 1):
            for z in range(chips):
                if k in parts:
                    near_add(k, z)

        for move in small:
            move.wait()
        for n in range(len(mates)):
            for k in range(2):
                dm_tot[n, k] = dm_own[n, k] + dm_near[n, k]
                dm_tot[n, k, 4:5, :] = modv[k, 4:5, :]

        def column_move(n, k, slot):
            return remote(
                dm_tot.at[n], gathered.at[n, slot], g_send.at[n, k], g_recv.at[n, slot],
                {"segment": role if n == 0 else other, "dp": lax.rem(dp + k, size)},
            )

        for n in range(len(mates)):
            for k in range(1 - n, size):
                column_move(n, k, dp).start()
        mine = pltpu.make_async_copy(dm_tot.at[0], gathered.at[0, dp], dm_load.at[2, 1])
        mine.start()

        def settle(k, z):
            if k in taken:
                crossing(k, z).wait_recv()
                total(k)[z] = total(k)[z] + cross(k)[z] if k in parts else cross(k)[z]

        def forward(p, z, by):
            line, recv = (right, right_recv) if by > 0 else (left, left_recv)
            first = place == (0 if by > 0 else chips - 1)
            target = device(role, place + by, core)
            cross_sent(z)
            cross_start(nth(p + 1))
            pl.when(at_end & (p > 0))(lambda: line_sent(nth(p - 1)))
            for k in range(kept):
                settle(k, z)
                here = remote(line(k).at[z], line(k).at[z], line_send.at[k, z], recv.at[k, z], target)
                start = remote(total(k).at[z], line(k).at[z], line_send.at[k, z], recv.at[k, z], target)
                pl.when(first)(start.start)

                @pl.when(jnp.logical_not(first))
                def _():
                    here.wait_recv()
                    line(k)[z] = line(k)[z] + total(k)[z]
                    here.start()

        in_turn(forward)
        cross_sent(place)
        for k in range(kept):
            settle(k, place)

        def result(k):
            return res_r if k else res_w

        for k in range(kept):
            result(k)[...] = total(k)[place].astype(f32)
            for line, recv, edge in ((right, right_recv, 0), (left, left_recv, chips - 1)):

                @pl.when(place != edge)
                def _():
                    remote(
                        line(k).at[place], line(k).at[place], line_send.at[k, 0],
                        recv.at[k, place], partner,
                    ).wait_recv()
                    result(k)[...] += line(k)[place].astype(f32)

        outs = [
            pltpu.make_async_copy(res_w, first_out, load_sem.at[0, 0]),
            pltpu.make_async_copy(res_r, rows_out, load_sem.at[1, 0]),
        ]
        for copy in outs:
            copy.start()
        pl.when(at_end)(lambda: line_sent(nth(chips - 2)))
        pl.when(jnp.logical_not(at_end))(lambda: in_turn(lambda p, z, by: line_sent(z)))
        mine.wait()
        for n in range(len(mates)):
            for k in range(1 - n, size):
                column_move(n, k, dp).wait_send()
                column_move(n, k, lax.rem(dp + k, size)).wait_recv()
        for copy in outs:
            copy.wait()
        if role == 0:
            each_part(lambda x: x.wait(), lambda x: x.wait_send())
        for k in range(2):
            remote(
                fin.at[0, pl.ds(0, BLK)], out_g.at[k], fin_send.at[0, 0], fin_recv.at[k], partner
            ).wait_recv() if role > 0 else pl.when(core != 0)(
                remote(
                    fin.at[0, pl.ds(0, BLK)], out_g.at[k], fin_send.at[0, 0], fin_recv.at[k], partner
                ).wait_recv
            )

    for role in range(4):
        pl.when(seg == role)(functools.partial(work, role))


def sums(att, up, down, dma, dmf, mod, fin, chips):
    wide, rows = att.shape[1:], down.shape[1:]

    def sems(*dims):
        return pltpu.SemaphoreType.DMA(dims)

    each = sems(4, chips)
    return pl.pallas_call(
        functools.partial(sums_kernel, chips),
        out_shape=[
            jax.ShapeDtypeStruct(wide, f32), jax.ShapeDtypeStruct(rows, f32),
            jax.ShapeDtypeStruct((2, 2 * chips, 2, 8, D), f32), OWNED,
        ],
        in_specs=[ANY] * 7,
        out_specs=[ANY] * 4,
        scratch_shapes=[
            vm((2, chips, *wide)), vm((2, chips, *rows)), vm((2, chips, *wide)), vm((2, chips, *rows)),
            vm((1, chips, *wide)), vm((1, chips, *rows)),
            vm((1, chips, *wide)), vm((1, chips, *rows)), vm((1, chips, *wide)), vm((1, chips, *rows)),
            vm(wide, f32), vm(rows, f32),
            vm((2, 2, 8, D), f32), vm((2, 2, 8, D), f32), vm((2, 2, 8, D), f32), vm((2, 8, D), f32),
            each, each, each, each, each, each, each, each, sems(3, 2),
            sems(2, 2), sems(2, 2), sems(2, 2 * chips), sems(2, 2 * chips), sems(MB, 2), sems(2),
        ],
        compiler_params=pltpu.CompilerParams(
            vmem_limit_bytes=VLIM, collective_id=1, has_side_effects=True
        ),
        name="gradient_sums",
    )(att, up, down, dma, dmf, mod, fin)


ATT_F, FF_F, FF_B, ATT_B = range(4)


def chain_kernel(
    xs, cs, w, rows2, cos, sin, mod,
    xa, st, kv, lse, y, yf, act, dma, dmf, out_x, fin,
    wa, w1, w2, xv, nv, kvv, vv, inbox, qv, atv, bra, n1, brf, gbv, dov, dqv, xo, ov, fv, lv, cv, sv,
    dkt, dvt, rcvv, dpv, duv, actv, accv, dmv, zerov, moda, modf,
    w_send, w_recv, wf_send, wf_recv, x_send, x_recv, row_recv, fwd_send, fwd_recv, c_send, c_recv,
    push_sem, dkv_send, dkv_recv, mod_send, mod_recv, far_send, far_recv, fin_send, out_recv, ld, osem,
):
    role, dp = lax.axis_index("segment"), lax.axis_index("dp")
    c, place = lax.rem(dp, 2), lax.div(dp, 2)
    quarter, half_d = FF // 4, D // 2

    def device(segment, core):
        return {"segment": segment, "dp": 2 * place + core}

    def remote(src, dst, send, recv, target):
        return pltpu.make_async_remote_copy(
            src_ref=src, dst_ref=dst, send_sem=send, recv_sem=recv, device_id=target,
            device_id_type=MESH,
        )

    def local_copy(src, dst, sem):
        return pltpu.make_async_copy(src, dst, sem)

    partner = device(role, 1 - c)

    def rows_at(start, size):
        return pl.ds(pl.multiple_of(start, size), size)

    barrier = pltpu.get_barrier_semaphore()
    for k in range(1, 8):
        to = lax.rem(role * 2 + c + k, 8)
        pl.semaphore_signal(
            barrier, inc=1, device_id=device(lax.div(to, 2), lax.rem(to, 2)), device_id_type=MESH
        )
    pl.semaphore_wait(barrier, 7)

    tables = [local_copy(cos, cv, ld.at[0]), local_copy(sin, sv, ld.at[1])]
    for copy in tables:
        copy.start()

    def give_x(k):
        return remote(xs.at[k], xa.at[2 * k + c], x_send.at[k], x_recv.at[k], partner)

    def keep_x(k):
        return local_copy(xs.at[k], xa.at[2 * k + c], ld.at[4 + k])

    w_half = rows_at(c * half_d, half_d)
    rows_half = rows_at(c * quarter, quarter)
    high_half = rows_at(2 * quarter + c * quarter, quarter)

    def give_rows(dst, target):
        return remote(rows2.at[rows_half], w2.at[dst], w_send.at[1], w_recv.at[1], device(target, c))

    def give_w(dst, target):
        return remote(w.at[w_half], dst.at[w_half], w_send.at[0], w_recv.at[0], device(target, c))

    def keep_mod(k, dst):
        return local_copy(mod.at[k], dst.at[2 * k + c], ld.at[9 + k])

    def give_mod(k, dst):
        return remote(mod.at[k], dst.at[2 * k + c], mod_send.at[k], mod_recv.at[k], partner)

    def far_mod(k, dst, segment, core):
        return remote(
            mod.at[k], dst.at[2 * k + c], far_send.at[k, core], far_recv.at[k, c],
            device(segment, core),
        )

    def share_mod(dst):
        for k in range(2):
            keep_mod(k, dst).start()
            give_mod(k, dst).start()

    def shared_mod(dst):
        for k in range(2):
            keep_mod(k, dst).wait()
            give_mod(k, dst).wait()

    def give_c(k, j):
        return remote(
            cs.at[k, block_rows(1 - c + 2 * j)], inbox.at[4 + k, pl.ds(j * BLK, BLK)],
            c_send.at[k, j], c_recv.at[k, j], partner,
        )

    def keep_c(k, j):
        return local_copy(
            cs.at[k, block_rows(c + 2 * j)], inbox.at[4 + k, pl.ds(j * BLK, BLK)],
            ld.at[4 + 2 * k + j],
        )

    def forward_w(dst):
        return remote(dst.at[w_half], dst.at[w_half], wf_send.at[0], wf_recv.at[0], partner)

    def forward_rows(dst):
        return remote(w2.at[dst], w2.at[dst], wf_send.at[1], wf_recv.at[1], partner)

    def settle(given, passed):
        given.wait_recv()
        passed.start()
        passed.wait()

    @pl.when(role == 0)
    def _():
        share_mod(moda)
        for k in range(2):
            give_x(k).start()
            keep_x(k).start()
        give_rows(rows_half, 1).start()
        load = local_copy(w, wa, ld.at[2])
        load.start()
        for k in range(2):
            keep_x(k).wait()
        shared_mod(moda)
        load.wait()

    @pl.when(role == 1)
    def _():
        share_mod(modf)
        loads = [
            local_copy(w, w1, ld.at[2]),
            local_copy(rows2, w2.at[pl.ds(2 * quarter, 2 * quarter)], ld.at[8]),
        ]
        for copy in loads:
            copy.start()
        settle(give_rows(rows_half, 1), forward_rows(rows_half))
        shared_mod(modf)
        for copy in loads:
            copy.wait()

    for who in (2, 3):

        @pl.when(role == who)
        def _():
            other = 5 - who
            mine, mod_mine = (wa, moda) if who == 2 else (w1, modf)
            there = rows_half if who == 2 else high_half
            share_mod(mod_mine)
            for k in range(2):
                for core in range(2):
                    far_mod(k, mod_mine, other, core).start()
            give_w(mine, other).start()
            give_rows(there, other).start()
            loads = [
                local_copy(w, mine, ld.at[2]),
                local_copy(
                    rows2, w2.at[pl.ds(0 if who == 2 else 2 * quarter, 2 * quarter)], ld.at[8]
                ),
            ]
            for copy in loads:
                copy.start()

            @pl.when(c == who - 2)
            def _():
                for k in range(2):
                    for j in range(2):
                        give_c(k, j).start()
                        keep_c(k, j).start()
                for k in range(2):
                    for j in range(2):
                        keep_c(k, j).wait()

            shared_mod(mod_mine)
            for copy in loads:
                copy.wait()

    def prepare(step):
        for who in (2, 3):
            other = 5 - who
            theirs, mod_theirs = (w1, modf) if who == 2 else (wa, moda)
            here = high_half if who == 2 else rows_half

            @pl.when((role == who) & (step == 3 - who))
            def _():
                settle(give_w(theirs, other), forward_w(theirs))
                for k in range(2):
                    for core in range(2):
                        remote(
                            mod.at[k], mod_theirs.at[2 * k + core], far_send.at[k, core],
                            far_recv.at[k, core], partner,
                        ).wait_recv()

            @pl.when((role == who) & (step == 1))
            def _():
                settle(give_rows(here, other), forward_rows(here))

    for copy in tables:
        copy.wait()

    def kind_of(step):
        first = step < 4
        return jnp.where(
            role == 0, jnp.where(first, ATT_F, ATT_B),
            jnp.where(role == 1, jnp.where(first, FF_F, FF_B), lax.rem(step, 4)),
        )

    def place_of(step):
        return jnp.where(role < 2, lax.rem(step, 4), lax.div(step, 4) * 2 + role - 2)

    def slot_rows(mb):
        n = jnp.where(role < 2, mb, lax.div(mb, 2))
        return lax.div(n, 2), pl.ds(pl.multiple_of(lax.rem(n, 2) * HALF, HALF), HALF)

    def x_rows(mb, b):
        slot = 2 * lax.div(mb, 2) + lax.div(b, 2)
        return inbox.at[slot, block_rows(lax.rem(b, 2))]

    def stores(kind, mb):
        half, spot = slot_rows(mb)
        if kind == ATT_F:
            kept = [
                (qv, st.at[QS, half, spot]), (kvv, kv.at[0, mb]), (vv, kv.at[1, mb]),
                (bra, st.at[BR, half, spot]), (lv, lse.at[mb]),
            ]
            return [(atv, st.at[AT, half, spot])], kept, role == 0
        if kind == FF_F:
            return [], [(brf, st.at[BF, half, spot])], role == 1
        if kind == FF_B:
            rows = [
                (n1, st.at[NF, half, spot]), (gbv, st.at[GB, half, spot]),
                (duv, yf.at[half, spot]), (actv, act.at[half, spot]), (dmv, dmf.at[mb]),
            ]
            return rows, [(zerov, dmf.at[mb + 1 - 2 * lax.rem(mb, 2)])], role >= 2
        rows = [
            (gbv, y.at[half, spot, pl.ds(3 * D, D)]), (dpv, y.at[half, spot, pl.ds(0, 3 * D)]),
            (n1, st.at[NM, half, spot]), (dmv, dma.at[mb]),
        ]
        return rows, [(zerov, dma.at[mb + 1 - 2 * lax.rem(mb, 2)])], role >= 2

    def copies(kind, mb):
        always, sometimes, when = stores(kind, mb)
        first = [local_copy(a, b, osem.at[k]) for k, (a, b) in enumerate(always)]
        rest = [local_copy(a, b, osem.at[len(always) + k]) for k, (a, b) in enumerate(sometimes)]
        return first, rest, when

    def store(kind, mb):
        first, rest, when = copies(kind, mb)
        for copy in first:
            copy.start()

        @pl.when(when)
        def _():
            for copy in rest:
                copy.start()

        if kind == ATT_B:
            pl.when(role == 0)(lambda: local_copy(ov, fin.at[mb], osem.at[5]).start())

    def wait_stored(step):
        kind_then, mb = kind_of(step), place_of(step)
        for kind in (ATT_F, FF_F, FF_B, ATT_B):

            @pl.when((step >= 0) & (kind_then == kind))
            def _():
                first, rest, when = copies(kind, mb)
                for copy in first:
                    copy.wait()

                @pl.when(when)
                def _():
                    for copy in rest:
                        copy.wait()

                if kind == ATT_B:
                    pl.when(role == 0)(lambda: local_copy(ov, fin.at[mb], osem.at[5]).wait())

    def wait_pushed(step):
        went = (
            ((role == 0) & (step < 4)) | (role == 1) | ((role >= 2) & (lax.rem(step, 4) == 3))
        ) & (step >= 0)

        @pl.when(went)
        def _():
            for j in range(2):
                at = pl.ds(j * BLK, BLK)
                remote(
                    ov.at[at], inbox.at[0, at], push_sem.at[j], row_recv.at[0, j], partner
                ).wait_send()

    def free(step):
        wait_pushed(step - 1)
        wait_stored(step - 1)

    def push(j, slot, rows, segment):
        remote(
            ov.at[block_rows(j)], inbox.at[slot, rows], push_sem.at[j], row_recv.at[slot, j],
            device(segment, c),
        ).start()

    def arrived(slot, j):
        at = block_rows(j)
        remote(
            ov.at[at], inbox.at[slot, at], push_sem.at[j], row_recv.at[slot, j], partner
        ).wait_recv()

    def spread(j, mb):
        segment, owner = c + 2 * j, lax.rem(mb, 2)
        here = (role == segment) & (c == owner)
        rows, k = block_rows(j), lax.div(mb, 2)

        @pl.when(here)
        def _():
            local_copy(fv.at[rows], out_x.at[k], fin_send.at[j]).start()

        @pl.when(jnp.logical_not(here))
        def _():
            remote(
                fv.at[rows], out_x.at[k], fin_send.at[j], out_recv.at[k], device(segment, owner)
            ).start()

    def wait_spread(mb):
        for j in range(2):
            here = (role == c + 2 * j) & (c == lax.rem(mb, 2))
            rows = pl.ds(j * BLK, BLK)

            @pl.when(here)
            def _():
                local_copy(fv.at[rows], out_x.at[0], fin_send.at[j]).wait()

            @pl.when(jnp.logical_not(here))
            def _():
                remote(
                    fv.at[rows], out_x.at[0], fin_send.at[j], out_recv.at[0], partner
                ).wait_send()

    def att_f(step, mb):
        length = moda[mb, 3:4, 0:1]
        off, scl, gat = moda[mb, 0:1, :], 1.0 + moda[mb, 1:2, :], moda[mb, 2:3, :]

        @pl.when(role == 0)
        def _():
            @pl.when(lax.rem(mb, 2) != c)
            def _():
                k = lax.div(mb, 2)
                remote(xs.at[0], xa.at[mb], x_send.at[0], x_recv.at[k], partner).wait_recv()

            load = local_copy(xa.at[mb], xv, ld.at[0])
            load.start()
            free(step)
            load.wait()

        def forward(j):
            rows = x_rows(mb, c + 2 * j)
            k = 2 * lax.div(mb, 2) + j
            return remote(rows, rows, fwd_send.at[j], fwd_recv.at[k], partner)

        @pl.when(role != 0)
        def _():
            for j in range(2):
                rows = x_rows(mb, c + 2 * j)
                remote(
                    ov.at[pl.ds(j * BLK, BLK)], rows, push_sem.at[j],
                    row_recv.at[2 * lax.div(mb, 2) + j, c], partner,
                ).wait_recv()
                forward(j).start()
            free(step)

        def kv_block(b, carry):
            rows = block_rows(b)

            @pl.when(role != 0)
            def _():
                j, there = lax.div(b, 2), lax.rem(b, 2) != c

                @pl.when(there)
                def _():
                    at = x_rows(mb, b)
                    remote(
                        at, at, fwd_send.at[0], fwd_recv.at[2 * lax.div(mb, 2) + j], partner
                    ).wait_recv()

                slot = 2 * lax.div(mb, 2) + j
                xv[rows, :] = inbox[slot, block_rows(lax.rem(b, 2)), :]

            norm, _ = norm_parts(xv[rows, :].astype(f32))
            n = (norm * scl + off).astype(bf16)
            nv[rows, :] = n
            cosine, sine = cv[rows, :], sv[rows, :]
            kk = dot(n, wa[:, D : 2 * D])
            for p in range(6):
                ls = slice(p * 128, (p + 1) * 128)
                kvv[rows, ls] = turn(kk[:, ls], cosine, sine).astype(bf16)
            vv[rows, :] = dot(n, wa[:, 2 * D : 3 * D]).astype(bf16)
            return carry

        lax.fori_loop(0, 4, kv_block, 0)

        @pl.when(role != 0)
        def _():
            for j in range(2):
                forward(j).wait_send()

        def q_block(j, carry):
            nat = block_rows(c + 2 * j)
            rows = block_rows(j)
            cosine, sine = cv[nat, :] * 0.125, sv[nat, :] * 0.125
            qq = dot(nv[nat, :], wa[:, 0:D])
            for p in range(6):
                ls = slice(p * 128, (p + 1) * 128)
                qv[rows, ls] = turn(qq[:, ls], cosine, sine).astype(bf16)
            return carry

        lax.fori_loop(0, 2, q_block, 0)
        lane = lax.broadcasted_iota(i32, (BLK, 128), 1)
        position = lax.broadcasted_iota(i32, (1, SEQ_LEN), 1).astype(f32)
        bias = jnp.where(position < length, 0.0, -1e30).astype(f32)
        lv[...] = jnp.zeros((HALF, 128), f32)

        def block(j, carry):
            rows = block_rows(j)

            def pair(hp, carry):
                ls = lanes(hp)
                k2, v2, q2 = kvv[:, ls], vv[:, ls], qv[rows, ls]
                outs, stats = [], lv[rows, :]
                for a in range(2):
                    s = dot_nt(jnp.where((lane < 64) == (a == 0), q2, jnp.zeros_like(q2)), k2)
                    s = s + bias
                    m = jnp.max(s, axis=1, keepdims=True)
                    e = jnp.exp(s - m)
                    total = jnp.sum(e, axis=1, keepdims=True)
                    outs.append(dot(e.astype(bf16), v2) / total)
                    stats = jnp.where(lane == 2 * hp + a, m + jnp.log(total), stats)
                atv[rows, ls] = jnp.where(lane < 64, outs[0], outs[1]).astype(bf16)
                lv[rows, :] = stats
                return carry

            lax.fori_loop(0, HEADS // 2, pair, 0)
            branch = dot(atv[rows, :], wa[:, 3 * D : 4 * D])
            live = live_column(c, length, j)
            x = xv[block_rows(c + 2 * j), :].astype(f32)
            out = (x + jnp.where(live, gat * branch, 0.0)).astype(bf16)
            bra[rows, :] = branch.astype(bf16)

            @pl.when(role == 0)
            def _():
                ov[rows, :] = out
                push(j, mb, rows, 1)

            @pl.when(role != 0)
            def _():
                inbox[6, rows, :] = out

            return carry

        lax.fori_loop(0, 2, block, 0)
        store(ATT_F, mb)

    def ff_f(step, mb):
        length = modf[mb, 3:4, 0:1]
        off, scl, gat = modf[mb, 0:1, :], 1.0 + modf[mb, 1:2, :], modf[mb, 2:3, :]
        slot = jnp.where(role == 1, mb, 6)
        pl.when((role >= 2) & (step >= 4))(lambda: wait_spread(mb))
        pl.when(role == 1)(lambda: arrived(mb, 0))
        free(step)

        def block(j, carry):
            rows = block_rows(j)
            pl.when((role == 1) & (j > 0))(lambda: arrived(mb, j))
            norm, _ = norm_parts(inbox[slot, rows, :].astype(f32))
            n1[rows, :] = (norm * scl + off).astype(bf16)
            accv[rows, :] = jnp.zeros((BLK, D), f32)

            def part(p, carry):
                at = pl.ds(pl.multiple_of(p * D, D), D)
                u = dot(n1[rows, :], w1[:, at])
                t, _ = gelu_parts(u)
                accv[rows, :] += dot((0.5 * u * (1.0 + t)).astype(bf16), w2[at, :])
                return carry

            lax.fori_loop(0, 4, part, 0)
            acc = accv[rows, :]
            live = live_column(c, length, j)
            x = inbox[slot, rows, :].astype(f32)
            out = (x + jnp.where(live, gat * acc, 0.0)).astype(bf16)
            brf[rows, :] = acc.astype(bf16)

            @pl.when(role != 1)
            def _():
                fv[rows, :] = out
                spread(j, mb)

            @pl.when(role == 1)
            def _():
                ov[rows, :] = out
                slot_there = 2 * lax.div(mb, 2) + j
                remote(
                    ov.at[rows], inbox.at[slot_there, block_rows(c)], push_sem.at[j],
                    row_recv.at[slot_there, c], device(2 + lax.rem(mb, 2), c),
                ).start()

            return carry

        lax.fori_loop(0, 2, block, 0)
        store(FF_F, mb)

    def ff_b(step, mb):
        length = modf[mb, 3:4, 0:1]
        off, scl, gat = modf[mb, 0:1, :], 1.0 + modf[mb, 1:2, :], modf[mb, 2:3, :]
        slot = jnp.where(role == 1, mb, 6)
        from_slot = jnp.where(role == 1, 4 + mb, 4 + lax.div(mb, 2))

        def wait_rows(j):
            pl.when(role == 1)(lambda: arrived(4 + mb, j))

            @pl.when((role != 1) & (lax.rem(mb, 2) != c))
            def _():
                at = block_rows(j)
                remote(
                    ov.at[at], inbox.at[from_slot, at], push_sem.at[j],
                    c_recv.at[lax.div(mb, 2), j], partner,
                ).wait_recv()

        wait_rows(0)
        free(step)

        @pl.when(role == 1)
        def _():
            half, spot = slot_rows(mb)
            load = local_copy(st.at[BF, half, spot], brf, ld.at[1])
            load.start()
            load.wait()

        dmv[...] = jnp.zeros((8, D), f32)

        def block(j, carry):
            rows = block_rows(j)
            pl.when(j > 0)(lambda: wait_rows(j))
            norm, _ = norm_parts(inbox[slot, rows, :].astype(f32))
            n1[rows, :] = (norm * scl + off).astype(bf16)
            live = live_column(c, length, j)
            gl = jnp.where(live, inbox[from_slot, rows, :].astype(f32), 0.0)
            gbv[rows, :] = (gl * gat).astype(bf16)
            dmv[2:3, :] += jnp.sum(gl * brf[rows, :].astype(f32), axis=0, keepdims=True)
            accv[rows, :] = jnp.zeros((BLK, D), f32)

            def part(p, carry):
                cols = pl.ds(pl.multiple_of(p * D, D), D)
                u = dot(n1[rows, :], w1[:, cols])
                t, u2 = gelu_parts(u)
                half = 0.5 * (1.0 + t)
                actv[rows, cols] = (u * half).astype(bf16)
                slope = half + 0.5 * u * (1.0 - t * t) * (
                    0.7978845608028654 * (1.0 + 3 * 0.044715 * u2)
                )
                du = (dot_nt(gbv[rows, :], w2[cols, :]) * slope).astype(bf16)
                duv[rows, cols] = du
                accv[rows, :] += dot_nt(du, w1[:, cols])
                return carry

            lax.fori_loop(0, 4, part, 0)
            acc = accv[rows, :]
            n, rstd = norm_parts(inbox[slot, rows, :].astype(f32))
            dmv[0:1, :] += jnp.sum(acc, axis=0, keepdims=True)
            dmv[1:2, :] += jnp.sum(acc * n, axis=0, keepdims=True)
            out = (
                inbox[from_slot, rows, :].astype(f32) + norm_back(acc, n, rstd, scl)
            ).astype(bf16)

            @pl.when(role == 1)
            def _():
                ov[rows, :] = out
                push(j, mb, rows, 0)

            @pl.when(role != 1)
            def _():
                inbox[7, rows, :] = out

            return carry

        lax.fori_loop(0, 2, block, 0)
        store(FF_B, mb)

    def att_b(step, mb):
        length = moda[mb, 3:4, 0:1]
        off, scl, gat = moda[mb, 0:1, :], 1.0 + moda[mb, 1:2, :], moda[mb, 2:3, :]
        slot = jnp.where(role == 0, mb, 7)
        half, spot = slot_rows(mb)
        turn_of = jnp.where(role == 0, lax.rem(mb, 2), lax.div(mb, 2))
        loads = [
            local_copy(st.at[QS, half, spot], qv, ld.at[0]),
            local_copy(kv.at[0, mb], kvv, ld.at[1]),
            local_copy(kv.at[1, mb], vv, ld.at[2]),
            local_copy(st.at[AT, half, spot], atv, ld.at[3]),
            local_copy(lse.at[mb], lv, ld.at[4]),
            local_copy(st.at[BR, half, spot], bra, ld.at[5]),
        ]
        for j in range(2):
            loads.append(
                local_copy(
                    xa.at[mb, block_rows(c + 2 * j)], xo.at[pl.ds(j * BLK, BLK)], ld.at[6 + j]
                )
            )
        free(step)

        @pl.when(role == 0)
        def _():
            for copy in loads:
                copy.start()

        dmv[...] = jnp.zeros((8, D), f32)

        def grad_block(j, carry):
            rows = block_rows(j)
            pl.when(role == 0)(lambda: arrived(mb, j))

            @pl.when(role != 0)
            def _():
                xo[rows, :] = inbox[2 * lax.div(mb, 2) + j, block_rows(c), :]

            live = live_column(c, length, j)
            gb = jnp.where(live, inbox[slot, rows, :].astype(f32) * gat, 0.0).astype(bf16)
            gbv[rows, :] = gb
            dov[rows, :] = dot_nt(gb, wa[:, 3 * D : 4 * D]).astype(bf16)
            return carry

        lax.fori_loop(0, 2, grad_block, 0)

        @pl.when(role == 0)
        def _():
            for copy in loads:
                copy.wait()

        lane = lax.broadcasted_iota(i32, (HALF, 128), 1)
        position = lax.broadcasted_iota(i32, (1, SEQ_LEN), 1).astype(f32)
        bias = jnp.where(position < length, 0.0, -1e30).astype(f32)

        def pair(hp, carry):
            ls = lanes(hp)
            k2, v2 = kvv[:, ls], vv[:, ls]
            q2, do2 = qv[:, ls], dov[:, ls]
            q2t, do2t = q2.T, do2.T
            both = do2.astype(f32) * atv[:, ls].astype(f32)
            stats = lv[...]
            dqs = []
            for a in range(2):
                head = (lane < 64) == (a == 0)
                zero = jnp.zeros_like(q2)
                s = dot_nt(jnp.where(head, q2, zero), k2) + bias
                base = jnp.sum(jnp.where(lane == 2 * hp + a, stats, 0.0), axis=1, keepdims=True)
                p = jnp.exp(s - base)
                dp_ = dot_nt(jnp.where(head, do2, zero), v2)
                delta = jnp.sum(jnp.where(head, both, 0.0), axis=1, keepdims=True)
                ds = (p * (dp_ - delta)).astype(bf16)
                dqs.append(dot(ds, k2))
                at = pl.ds(pl.multiple_of(hp * 128 + a * 64, 64), 64)
                dkt[at, :] = dot(q2t[a * 64 : (a + 1) * 64, :], ds).astype(bf16)
                dvt[at, :] = dot(do2t[a * 64 : (a + 1) * 64, :], p.astype(bf16)).astype(bf16)
            dqv[:, ls] = jnp.where(lane < 64, dqs[0], dqs[1]).astype(bf16)
            for part, grad in enumerate((dkt, dvt)):
                for j in range(2):
                    give_pair(hp, part, j).start()
            return carry

        def give_pair(hp, part, j):
            grad = (dkt, dvt)[part]
            return remote(
                grad.at[lanes(hp), block_rows(1 - c + 2 * j)],
                rcvv.at[turn_of, part, lanes(hp), pl.ds(j * BLK, BLK)],
                dkv_send.at[hp, part, j], dkv_recv.at[turn_of, hp, part, j], partner,
            )

        lax.fori_loop(0, HEADS // 2, pair, 0)

        def settled(hp, carry):
            for part in range(2):
                for j in range(2):
                    give_pair(hp, part, j).wait()
            return carry

        def first(j, carry):
            rows, nat = block_rows(j), block_rows(c + 2 * j)
            cosine, sine = cv[nat, :], -sv[nat, :]
            for p in range(6):
                ls = slice(p * 128, (p + 1) * 128)
                dpv[rows, ls] = (turn(dqv[rows, ls].astype(f32), cosine, sine) * 0.125).astype(bf16)
            return carry

        lax.fori_loop(0, 2, first, 0)
        lax.fori_loop(0, HEADS // 2, settled, 0)

        def last(j, carry):
            rows, nat = block_rows(j), block_rows(c + 2 * j)
            cosine, sine = cv[nat, :], -sv[nat, :]
            for p in range(6):
                ls = slice(p * 128, (p + 1) * 128)
                for part, own in enumerate((dkt, dvt)):
                    total = own[ls, nat].astype(f32) + rcvv[turn_of, part, ls, rows].astype(f32)
                    grad = total.T
                    if part == 0:
                        grad = turn(grad.astype(bf16).astype(f32), cosine, sine)
                    dpv[rows, (part + 1) * D + p * 128 : (part + 1) * D + (p + 1) * 128] = (
                        grad.astype(bf16)
                    )
            acc = dot_nt(dpv[rows, :], wa[:, 0 : 3 * D])
            n, rstd = norm_parts(xo[rows, :].astype(f32))
            n1[rows, :] = (n * scl + off).astype(bf16)
            g = inbox[slot, rows, :].astype(f32)
            live = live_column(c, length, j)
            gl = jnp.where(live, g, 0.0)
            dmv[0:1, :] += jnp.sum(acc, axis=0, keepdims=True)
            dmv[1:2, :] += jnp.sum(acc * n, axis=0, keepdims=True)
            dmv[2:3, :] += jnp.sum(gl * bra[rows, :].astype(f32), axis=0, keepdims=True)
            ov[rows, :] = (g + norm_back(acc, n, rstd, scl)).astype(bf16)
            pl.when(role != 0)(lambda: push(j, 4 + mb, rows, 1))
            return carry

        lax.fori_loop(0, 2, last, 0)
        store(ATT_B, mb)

    def run(step, carry):
        kind, mb = kind_of(step), place_of(step)
        prepare(step)
        for which, work in ((ATT_F, att_f), (FF_F, ff_f), (FF_B, ff_b), (ATT_B, att_b)):
            pl.when(kind == which)(functools.partial(work, step, mb))
        return carry

    zerov[...] = jnp.zeros((8, D), f32)
    lax.fori_loop(0, 8, run, 0)
    free(8)
    pl.when(role >= 2)(lambda: wait_spread(role))

    @pl.when(role != c + 2)
    def _():
        for k in range(2):
            remote(
                fv.at[pl.ds(0, BLK)], out_x.at[k], fin_send.at[0], out_recv.at[k], partner
            ).wait_recv()

    @pl.when(role == 0)
    def _():
        for k in range(2):
            give_x(k).wait_send()
        give_rows(rows_half, 1).wait_send()

    for who in (2, 3):

        @pl.when(role == who)
        def _():
            other = 5 - who
            mine, mod_mine = (wa, moda) if who == 2 else (w1, modf)
            there = rows_half if who == 2 else high_half
            for k in range(2):
                for core in range(2):
                    far_mod(k, mod_mine, other, core).wait_send()
            give_w(mine, other).wait_send()
            give_rows(there, other).wait_send()

            @pl.when(c == who - 2)
            def _():
                for k in range(2):
                    for j in range(2):
                        give_c(k, j).wait_send()


def chain(xs, cs, w, rows2, cos, sin, mod):
    def sems(*dims):
        return pltpu.SemaphoreType.DMA(dims)

    table = vm((SEQ_LEN, 128), f32)
    outs = [
        shape((MB, SEQ_LEN, D)), ST, KV, LSE, YS, YS, YS, DM, DM, OWNED, shape((MB, HALF, D)),
    ]
    return pl.pallas_call(
        chain_kernel,
        out_shape=outs,
        in_specs=[ANY] * 7,
        out_specs=[ANY] * len(outs),
        scratch_shapes=[
            vm((D, FF)), vm((D, FF)), vm((FF, D)), FV, FV, FV, FV, vm((8, HALF, D)),
            HV, HV, HV, HV, HV, HV, HV, HV, HV, HV, HV, vm((HALF, 128), f32), table, table,
            vm((D, SEQ_LEN)), vm((D, SEQ_LEN)), vm((2, 2, D, HALF)), vm((HALF, 3 * D)),
            vm((HALF, FF)), vm((HALF, FF)), vm((HALF, D), f32), vm((8, D), f32), vm((8, D), f32),
            vm((MB, 8, D), f32), vm((MB, 8, D), f32),
            sems(3), sems(3), sems(2), sems(2), sems(2), sems(2), sems(8, 2), sems(2), sems(4),
            sems(2, 2), sems(2, 2), sems(2), sems(HEADS // 2, 2, 2), sems(2, HEADS // 2, 2, 2),
            sems(2), sems(2), sems(2, 2), sems(2, 2), sems(2), sems(2), sems(12), sems(6),
        ],
        compiler_params=pltpu.CompilerParams(
            vmem_limit_bytes=62 << 20, collective_id=0, has_side_effects=True
        ),
        cost_estimate=cost(300),
        name="layers",
    )(xs, cs, w, rows2, cos, sin, mod)


def time_cond(steps):
    half_width = D // 2
    frequency = jnp.exp(
        jnp.arange(half_width, dtype=f32) * (-math.log(10000.0) / half_width)
    )
    angles = steps.astype(f32)[:, None] * frequency[None, :]
    return jax.nn.silu(jnp.concatenate([jnp.cos(angles), jnp.sin(angles)], axis=1))


def rope_tables():
    inverse = np.exp(np.arange(32, dtype=np.float32) * np.float32(-math.log(10000.0) / 32))
    angles = np.arange(SEQ_LEN, dtype=np.float32)[:, None] * inverse[None, :]
    cosine, sine = np.cos(angles), np.sin(angles)
    return (
        np.concatenate([cosine] * 4, axis=1).astype(np.float32),
        np.concatenate([-sine, sine, -sine, sine], axis=1).astype(np.float32),
    )


def local(block_input, cotangent, lengths, steps, mod_weight, mod_bias, first_weight, down_rows):
    ndp = lax.axis_size("dp")
    seg, dp = lax.axis_index("segment"), lax.axis_index("dp")
    chips = ndp // 2
    w, rows2 = first_weight[0], down_rows[0]
    conditions = time_cond(steps).astype(bf16)
    modulation = jnp.dot(conditions, mod_weight[0], preferred_element_type=f32)
    modulation = (modulation + mod_bias[0].astype(f32)).reshape(2, 3, D)
    length = jnp.broadcast_to(lengths.astype(f32)[:, None, None], (2, 1, D))
    mod = jnp.concatenate(
        [modulation, length, conditions.astype(f32)[:, None], jnp.zeros((2, 3, D), f32)], axis=1
    )
    cos, sin = (jnp.asarray(t) for t in rope_tables())
    _, st, _, _, y, yf, act, dma, dmf, out_x, fin = chain(
        block_input, cotangent, w, rows2, cos, sin, mod
    )
    depth, wide_rows = D // ndp, FF // 2 // ndp

    def weight_grad(kind, roles, right):
        pairs = pltpu.SemaphoreType.DMA((2,))
        return pl.pallas_call(
            functools.partial(weight_grad_kernel, kind, roles),
            in_specs=[ANY, ANY],
            out_specs=ANY,
            scratch_shapes=[
                vm((2, SEQ_LEN, D)), vm((2, 2, SEQ_LEN, D)), vm((D, D), f32), vm((2, D, D)),
                pairs, pairs, pairs,
            ],
            out_shape=shape((FF, D) if kind == "down" else (D, FF)),
            compiler_params=pltpu.CompilerParams(vmem_limit_bytes=VLIM),
            cost_estimate=cost(12),
            name=kind + "_gradient",
        )(st, right)

    down = weight_grad("down", (1, 2, 3), act).reshape(2 * ndp, wide_rows, D)
    up = weight_grad("up", (1, 2, 3), yf).reshape(ndp, depth, FF)
    att = weight_grad("attention", (0, 2, 3), y).reshape(ndp, depth, FF)
    first_sum, rows_sum, rows, out_g = sums(att, up, down, dma, dmf, mod, fin, chips)

    rows = jnp.where((jnp.arange(2) == 1)[:, None, None, None, None] & (seg < 2), 0.0, rows)
    columns = rows[:, :, :, :3].reshape(4 * ndp, 3 * D)
    kept = rows[:, :, :, 4].reshape(4 * ndp, D)
    mine = lax.dynamic_slice_in_dim(kept, dp * depth, depth, axis=1)
    mod_w_sum = jnp.dot(
        mine.T, columns, precision=lax.Precision.HIGHEST, preferred_element_type=f32
    )
    width = 3 * D // ndp
    mod_b_sum = jnp.sum(lax.dynamic_slice_in_dim(columns, dp * width, width, axis=1), axis=0)

    live = (seg * BLK + jnp.arange(BLK))[None, :, None] < lengths[:, None, None]

    def placed(given, part):
        return jnp.where(live, given, lax.dynamic_slice_in_dim(part, seg * BLK, BLK, axis=1))

    return (
        placed(out_x, block_input),
        placed(out_g, cotangent).astype(f32),
        mod_w_sum[None],
        mod_b_sum[None],
        first_sum[None],
        rows_sum[None],
    )


def solution(mesh):
    in_specs = (
        P("dp", None, None),
        P("dp", None, None),
        P("dp"),
        P("dp"),
        P("segment", None, None),
        P("segment", None),
        P("segment", None, None),
        P("segment", None, None),
    )
    out_specs = (
        P("dp", "segment", None),
        P("dp", "segment", None),
        P("segment", "dp", None),
        P("segment", "dp"),
        P("segment", "dp", None),
        P("segment", "dp", None),
    )
    return jax.shard_map(local, mesh=mesh, in_specs=in_specs, out_specs=out_specs, check_vma=False)
```

time: 642 us -> 510 us (0.79)
  starting transfers between devices: 40.2 us -> 0 us
  Pallas kernels: 530 us -> 493 us
  waiting for transfers between devices: 19.8 us -> 0 us
  other arithmetic: 24.1 us -> 6.99 us
  local copies, waits for them, and re-layouts: 16.1 us -> 4.21 us
    ppermute x10 -> x0, starting transfers between devices: 40.2 us -> none  [the longest x8 38.3 us: across(): return lax.ppermute(value, ('segment', 'dp'), pairs)]
    pallas_call x8 -> x5, Pallas kernels: 530 us -> 493 us  [the longest x1 397 us: chain(): pl.pallas_call(chain_kernel, out_shape=outs, in_specs=[ANY] * 7, out_spec...]
    ppermute x10 -> x0, waiting for transfers between devices: 19.8 us -> none  [the longest x8 19.8 us: across(): return lax.ppermute(value, ('segment', 'dp'), pairs)]
    select_n x8 -> x1, other arithmetic: 12.1 us -> 1.39 us  [local(): jnp.where((jnp.arange(2) == 1)[:, None, None, None, None] & (seg < 2), 0....]
    slice x7 -> x2, local copies, waits for them, and re-layouts: 7.67 us -> 0.36 us  [the longest x1 0.3 us: local(): kept = rows[:, :, :, 4].reshape(4 * ndp, D)]
  transfers between devices with their start and end apart: 10 -> 0, of which waited for: 2 -> 0; matrix products, arithmetic and copies ran while one was open for 4% -> 0% of each run, Pallas kernels for 6% -> 0%
where the time goes in v4:
time: 510 us
  Pallas kernels  493 us (97%)
  other arithmetic  6.99 us (1%)
    pallas_call x1, Pallas kernels, chain(): pl.pallas_call(chain_kernel, out_shape=outs, in_specs=[ANY] * 7, out_spec...  397 us
    pallas_call x1, Pallas kernels, sums(): pl.pallas_call(functools.partial(sums_kernel, chips), out_shape=[jax.Shap...  79.2 us
    pallas_call x3, Pallas kernels, weight_grad(): pl.pallas_call(functools.partial(weight_grad_kernel, kind, roles), in_spe...  17 us

profile of v4, /device:TPU:0, one launch (start us, length us, event | category | flops | bytes accessed | tf_op | source)
XLA Modules:
  0.0 509.8 jit_solution(9780767650606415460)
XLA Ops:
  0.6 0.0 copy-start.3
  0.7 0.7 convert_element_type.33
  1.3 0.1 multiply_cosine_fusion
  1.4 0.7 convert_reduce_fusion
  2.2 2.6 fusion.2
  4.9 0.0 copy-done.3
  4.9 0.1 broadcast_in_dim.52
  5.0 0.1 pad.3.clone
  5.0 0.7 maximum_maximum_fusion.mod
  5.7 397.1 %layers.1 = (bf16[4,1024,768]{2,1,0:T(8,128)(2,1)}, bf16[7,2,1024,768]{3,2,1,0:T(8,128)(2,1)}, bf16[2,4,1024,768]{3,2,1,0:T(8,128)(2,1)}, f32[4,512,128]{2,1,0:T...) custom-call(bf16[2,1024,768]{2,1,0:T(8,128)(2,1)} %xs.1, ...), custom_call_target="tpu_custom_call" | custom-call | flops 299999985664 | bytes 1048576 | tf_op jit(solution)/shard_map/layers/pallas_call | solution.py:1236
  402.9 0.1 down_gradient.1
  403.0 0.1 up_gradient.1
  403.0 16.9 %attention_gradient.1 = bf16[768,3072]{1,0:T(8,128)(2,1)} custom-call(bf16[7,2,1024,768]{3,2,1,0:T(8,128)(2,1)} %get-tuple-element.19.st, bf16[2,1024,3072]{2,1,0:T(8,128)(2,1)} %get-tuple-element.20.y), custom_call_target="tpu_custom_call" | custom-call | flops 12000000000 | bytes 1048576 | tf_op jit(solution)/shard_map/attention_gradient/pallas_call | solution.py:1298
  419.9 79.2 %gradient_sums.1 = (f32[96,3072]{1,0:T(8,128)}, f32[192,768]{1,0:T(8,128)}, f32[2,8,2,8,768]{4,3,2,1,0:T(8,128)}, bf16[2,256,768]{2,1,0:T(8,128)(2,1)}) custom-call(bf16[8,96,3072]{2,1,0:T(8,128)(2,1)} %bitcast.22, bf16[8,96,3072]{2,1,0:T(8,128)(2,1)} %bitcast.21, bf16[16,192,768]{2,1,0:T(8,128)(2,1)} %bitcast.20, f32[4,8,768]{2,1,0:T(8,128)} %get-tuple-element.23.dma, ...), custom_call_target="tpu_custom_call" | custom-call | tf_op jit(solution)/shard_map/gradient_sums/pallas_call | solution.py:446
  499.1 0.0 copy-start.4
  499.1 0.0 copy-start.1
  499.1 0.0 copy-start.2
  499.2 1.4 broadcast_select_fusion
  500.6 0.1 slice.9
  500.6 0.1 copy.22
  500.7 0.3 slice_reduce_fusion
  501.0 0.0 copy-start
  501.0 0.1 reshape_squeeze.3
  501.1 1.9 convolution_bitcast_fusion
  503.0 0.0 copy-done.4
  503.0 0.1 broadcast_compare_fusion
  503.1 3.2 select_convert_fusion
  506.2 0.1 dynamic-slice_reduce_fusion
  506.3 0.6 broadcast_in_dim.57
  506.9 0.0 copy-done
  506.9 1.0 copy.27
  507.9 1.9 copy.28
  (11 shorter events, 0.1 us)
Async XLA Ops:
  0.6 4.2 copy-start.3
  499.1 3.8 copy-start.4
  499.1 3.9 copy-start.1
  499.1 3.9 copy-start.2
  501.0 5.9 %copy-start = (f32[96,3072]{1,0:T(8,128)S(1)}, f32[96,3072]{1,0:T(8,128)}, u32[]{:S(2)}) copy-start(f32[96,3072]{1,0:T(8,128)} %get-tuple-element.28) | copy-start | bytes 3538948

commit v5 on v4

--- a/solution.py
+++ b/solution.py
@@ -472,7 +472,7 @@
 
 def chain_kernel(
     xs, cs, w, rows2, cos, sin, mod,
-    xa, st, kv, lse, y, yf, act, dma, dmf, out_x, fin,
+    st, kv, lse, y, yf, act, dma, dmf, out_x, fin,
     wa, w1, w2, xv, nv, kvv, vv, inbox, qv, atv, bra, n1, brf, gbv, dov, dqv, xo, ov, fv, lv, cv, sv,
     dkt, dvt, rcvv, dpv, duv, actv, accv, dmv, zerov, moda, modf,
     w_send, w_recv, wf_send, wf_recv, x_send, x_recv, row_recv, fwd_send, fwd_recv, c_send, c_recv,
@@ -511,11 +511,11 @@
     for copy in tables:
         copy.start()
 
-    def give_x(k):
-        return remote(xs.at[k], xa.at[2 * k + c], x_send.at[k], x_recv.at[k], partner)
-
-    def keep_x(k):
-        return local_copy(xs.at[k], xa.at[2 * k + c], ld.at[4 + k])
+    def give_x(k, h):
+        return remote(
+            xs.at[k, pl.ds(h * HALF, HALF)], inbox.at[4 + 2 * k + h], x_send.at[k, h], x_recv.at[k, h],
+            partner,
+        )
 
     w_half = rows_at(c * half_d, half_d)
     rows_half = rows_at(c * quarter, quarter)
@@ -576,13 +576,11 @@
     def _():
         share_mod(moda)
         for k in range(2):
-            give_x(k).start()
-            keep_x(k).start()
+            for h in range(2):
+                give_x(k, h).start()
         give_rows(rows_half, 1).start()
         load = local_copy(w, wa, ld.at[2])
         load.start()
-        for k in range(2):
-            keep_x(k).wait()
         shared_mod(moda)
         load.wait()
 
@@ -673,9 +671,14 @@
         n = jnp.where(role < 2, mb, lax.div(mb, 2))
         return lax.div(n, 2), pl.ds(pl.multiple_of(lax.rem(n, 2) * HALF, HALF), HALF)
 
+    def x_slot(mb):
+        return 2 * lax.div(mb, 2) + jnp.where(role == 0, 4, 0)
+
     def x_rows(mb, b):
-        slot = 2 * lax.div(mb, 2) + lax.div(b, 2)
-        return inbox.at[slot, block_rows(lax.rem(b, 2))]
+        return inbox.at[x_slot(mb) + lax.div(b, 2), block_rows(lax.rem(b, 2))]
+
+    def own_x(mb):
+        return (role == 0) & (lax.rem(mb, 2) == c)
 
     def stores(kind, mb):
         half, spot = slot_rows(mb)
@@ -801,15 +804,19 @@
 
         @pl.when(role == 0)
         def _():
-            @pl.when(lax.rem(mb, 2) != c)
-            def _():
-                k = lax.div(mb, 2)
-                remote(xs.at[0], xa.at[mb], x_send.at[0], x_recv.at[k], partner).wait_recv()
-
-            load = local_copy(xa.at[mb], xv, ld.at[0])
-            load.start()
+            k = lax.div(mb, 2)
+            load = local_copy(xs.at[k], xv, ld.at[0])
+            pl.when(own_x(mb))(load.start)
             free(step)
-            load.wait()
+            pl.when(own_x(mb))(load.wait)
+
+            @pl.when(jnp.logical_not(own_x(mb)))
+            def _():
+                for h in range(2):
+                    remote(
+                        xs.at[0, pl.ds(0, HALF)], inbox.at[4 + 2 * k + h], x_send.at[0, 0],
+                        x_recv.at[k, h], partner,
+                    ).wait_recv()
 
         def forward(j):
             rows = x_rows(mb, c + 2 * j)
@@ -830,19 +837,18 @@
         def kv_block(b, carry):
             rows = block_rows(b)
 
-            @pl.when(role != 0)
+            @pl.when(jnp.logical_not(own_x(mb)))
             def _():
                 j, there = lax.div(b, 2), lax.rem(b, 2) != c
 
-                @pl.when(there)
+                @pl.when(there & (role != 0))
                 def _():
                     at = x_rows(mb, b)
                     remote(
                         at, at, fwd_send.at[0], fwd_recv.at[2 * lax.div(mb, 2) + j], partner
                     ).wait_recv()
 
-                slot = 2 * lax.div(mb, 2) + j
-                xv[rows, :] = inbox[slot, block_rows(lax.rem(b, 2)), :]
+                xv[rows, :] = inbox[x_slot(mb) + j, block_rows(lax.rem(b, 2)), :]
 
             norm, _ = norm_parts(xv[rows, :].astype(f32))
             n = (norm * scl + off).astype(bf16)
@@ -1057,12 +1063,12 @@
             local_copy(lse.at[mb], lv, ld.at[4]),
             local_copy(st.at[BR, half, spot], bra, ld.at[5]),
         ]
-        for j in range(2):
-            loads.append(
-                local_copy(
-                    xa.at[mb, block_rows(c + 2 * j)], xo.at[pl.ds(j * BLK, BLK)], ld.at[6 + j]
-                )
+        own_loads = [
+            local_copy(
+                xs.at[lax.div(mb, 2), block_rows(c + 2 * j)], xo.at[pl.ds(j * BLK, BLK)], ld.at[6 + j]
             )
+            for j in range(2)
+        ]
         free(step)
 
         @pl.when(role == 0)
@@ -1070,15 +1076,20 @@
             for copy in loads:
                 copy.start()
 
+        @pl.when(own_x(mb))
+        def _():
+            for copy in own_loads:
+                copy.start()
+
         dmv[...] = jnp.zeros((8, D), f32)
 
         def grad_block(j, carry):
             rows = block_rows(j)
             pl.when(role == 0)(lambda: arrived(mb, j))
 
-            @pl.when(role != 0)
-            def _():
-                xo[rows, :] = inbox[2 * lax.div(mb, 2) + j, block_rows(c), :]
+            @pl.when(jnp.logical_not(own_x(mb)))
+            def _():
+                xo[rows, :] = inbox[x_slot(mb) + j, block_rows(c), :]
 
             live = live_column(c, length, j)
             gb = jnp.where(live, inbox[slot, rows, :].astype(f32) * gat, 0.0).astype(bf16)
@@ -1091,6 +1102,11 @@
         @pl.when(role == 0)
         def _():
             for copy in loads:
+                copy.wait()
+
+        @pl.when(own_x(mb))
+        def _():
+            for copy in own_loads:
                 copy.wait()
 
         lane = lax.broadcasted_iota(i32, (HALF, 128), 1)
@@ -1202,7 +1218,8 @@
     @pl.when(role == 0)
     def _():
         for k in range(2):
-            give_x(k).wait_send()
+            for h in range(2):
+                give_x(k, h).wait_send()
         give_rows(rows_half, 1).wait_send()
 
     for who in (2, 3):
@@ -1231,7 +1248,7 @@
 
     table = vm((SEQ_LEN, 128), f32)
     outs = [
-        shape((MB, SEQ_LEN, D)), ST, KV, LSE, YS, YS, YS, DM, DM, OWNED, shape((MB, HALF, D)),
+        ST, KV, LSE, YS, YS, YS, DM, DM, OWNED, shape((MB, HALF, D)),
     ]
     return pl.pallas_call(
         chain_kernel,
@@ -1244,7 +1261,7 @@
             vm((D, SEQ_LEN)), vm((D, SEQ_LEN)), vm((2, 2, D, HALF)), vm((HALF, 3 * D)),
             vm((HALF, FF)), vm((HALF, FF)), vm((HALF, D), f32), vm((8, D), f32), vm((8, D), f32),
             vm((MB, 8, D), f32), vm((MB, 8, D), f32),
-            sems(3), sems(3), sems(2), sems(2), sems(2), sems(2), sems(8, 2), sems(2), sems(4),
+            sems(3), sems(3), sems(2), sems(2), sems(2, 2), sems(2, 2), sems(8, 2), sems(2), sems(4),
             sems(2, 2), sems(2, 2), sems(2), sems(HEADS // 2, 2, 2), sems(2, HEADS // 2, 2, 2),
             sems(2), sems(2), sems(2, 2), sems(2, 2), sems(2), sems(2), sems(12), sems(6),
         ],
@@ -1288,7 +1305,7 @@
         [modulation, length, conditions.astype(f32)[:, None], jnp.zeros((2, 3, D), f32)], axis=1
     )
     cos, sin = (jnp.asarray(t) for t in rope_tables())
-    _, st, _, _, y, yf, act, dma, dmf, out_x, fin = chain(
+    st, _, _, y, yf, act, dma, dmf, out_x, fin = chain(
         block_input, cotangent, w, rows2, cos, sin, mod
     )
     depth, wide_rows = D // ndp, FF // 2 // ndp

time: 510 us -> 425 us (0.83)
  Pallas kernels: 493 us -> 408 us
    pallas_call x1, Pallas kernels: 397 us -> 312 us  [chain(): pl.pallas_call(chain_kernel, out_shape=outs, in_specs=[ANY] * 7, out_spec...]
where the time goes in v5:
time: 425 us; the launch traced here: 424 us
  Pallas kernels  408 us (96%)
  other arithmetic  6.99 us (2%)
  matrix products  4.45 us (1%)
    pallas_call x1, Pallas kernels, chain(): pl.pallas_call(chain_kernel, out_shape=outs, in_specs=[ANY] * 7, out_spec...  312 us
    pallas_call x1, Pallas kernels, sums(): pl.pallas_call(functools.partial(sums_kernel, chips), out_shape=[jax.Shap...  79.2 us
    pallas_call x3, Pallas kernels, weight_grad(): pl.pallas_call(functools.partial(weight_grad_kernel, kind, roles), in_spe...  17 us

profile of v5, /device:TPU:0, one launch (start us, length us, event | category | flops | bytes accessed | tf_op | source)
XLA Modules:
  0.0 424.5 jit_solution(7001813527884342260)
XLA Ops:
  0.6 0.0 copy-start.3
  0.7 0.7 convert_element_type.33
  1.3 0.1 multiply_cosine_fusion
  1.4 0.7 convert_reduce_fusion
  2.2 2.6 fusion.2
  4.9 0.0 copy-done.3
  4.9 0.1 broadcast_in_dim.52
  5.0 0.1 pad.3.clone
  5.0 0.7 maximum_maximum_fusion.mod
  5.7 311.8 %layers.1 = (bf16[7,2,1024,768]{3,2,1,0:T(8,128)(2,1)}, bf16[2,4,1024,768]{3,2,1,0:T(8,128)(2,1)}, f32[4,512,128]{2,1,0:T(8,128)}, bf16[2,1024,3072]{2,1,0:T(8,1...) custom-call(bf16[2,1024,768]{2,1,0:T(8,128)(2,1)} %xs.1, ...), custom_call_target="tpu_custom_call" | custom-call | flops 299999985664 | bytes 1048576 | tf_op jit(solution)/shard_map/layers/pallas_call | solution.py:1253
  317.5 0.1 down_gradient.1
  317.6 0.1 up_gradient.1
  317.7 16.9 %attention_gradient.1 = bf16[768,3072]{1,0:T(8,128)(2,1)} custom-call(bf16[7,2,1024,768]{3,2,1,0:T(8,128)(2,1)} %get-tuple-element.19.st, bf16[2,1024,3072]{2,1,0:T(8,128)(2,1)} %get-tuple-element.20.y), custom_call_target="tpu_custom_call" | custom-call | flops 12000000000 | bytes 1048576 | tf_op jit(solution)/shard_map/attention_gradient/pallas_call | solution.py:1315
  334.6 79.2 %gradient_sums.1 = (f32[96,3072]{1,0:T(8,128)}, f32[192,768]{1,0:T(8,128)}, f32[2,8,2,8,768]{4,3,2,1,0:T(8,128)}, bf16[2,256,768]{2,1,0:T(8,128)(2,1)}) custom-call(bf16[8,96,3072]{2,1,0:T(8,128)(2,1)} %bitcast.22, bf16[8,96,3072]{2,1,0:T(8,128)(2,1)} %bitcast.21, bf16[16,192,768]{2,1,0:T(8,128)(2,1)} %bitcast.20, f32[4,8,768]{2,1,0:T(8,128)} %get-tuple-element.23.dma, ...), custom_call_target="tpu_custom_call" | custom-call | tf_op jit(solution)/shard_map/gradient_sums/pallas_call | solution.py:446
  413.8 0.0 copy-start.4
  413.8 0.0 copy-start.1
  413.8 0.0 copy-start.2
  413.8 1.4 broadcast_select_fusion
  415.2 0.1 slice.9
  415.3 0.1 copy.22
  415.3 0.3 slice_reduce_fusion
  415.6 0.0 copy-start
  415.6 0.1 reshape_squeeze.3
  415.7 1.9 convolution_bitcast_fusion
  417.6 0.0 copy-done.4
  417.6 0.1 broadcast_compare_fusion
  417.7 0.0 copy-done.1
  417.7 3.2 select_convert_fusion
  420.9 0.1 dynamic-slice_reduce_fusion
  421.0 0.6 broadcast_in_dim.57
  421.5 1.0 copy.27
  422.5 1.9 copy.28
  (11 shorter events, 0.1 us)
Async XLA Ops:
  0.6 4.2 copy-start.3
  413.8 3.8 copy-start.4
  413.8 3.9 copy-start.1
  413.8 3.9 copy-start.2
  415.6 5.9 %copy-start = (f32[96,3072]{1,0:T(8,128)S(1)}, f32[96,3072]{1,0:T(8,128)}, u32[]{:S(2)}) copy-start(f32[96,3072]{1,0:T(8,128)} %get-tuple-element.28) | copy-start | bytes 3538948

commit v6 on v5

--- a/solution.py
+++ b/solution.py
@@ -72,23 +72,29 @@
     return t, u2
 
 
+def gelu_slope(u, t, u2, half):
+    return half + 0.5 * u * (1.0 - t * t) * (
+        0.7978845608028654 * (1.0 + 3 * 0.044715 * u2)
+    )
+
+
 def weight_grad_kernel(kind, roles, st, y, out, xv, yv, acc, ov, xsem, ysem, osem):
     role = lax.axis_index("segment")
     parts = jnp.where(role < 2, 2, 1)
 
-    def tile(j):
-        return y.at[:, :, pl.ds(pl.multiple_of(j * D, D), D)]
+    def tile(j, h):
+        return y.at[h, :, pl.ds(pl.multiple_of(j * D, D), D)]
 
     def into(j):
         at = pl.ds(pl.multiple_of(j * D, D), D)
         return out.at[at] if kind == "down" else out.at[:, at]
 
-    def load_x(which):
-        return pltpu.make_async_copy(st.at[which], xv, xsem.at[0])
-
-    def load_y(j):
+    def load_x(which, h, into):
+        return pltpu.make_async_copy(st.at[which, h], xv.at[into, h], xsem.at[into, h])
+
+    def load_y(j, h):
         slot = lax.rem(j, 2)
-        return pltpu.make_async_copy(tile(j), yv.at[slot], ysem.at[slot])
+        return pltpu.make_async_copy(tile(j, h), yv.at[slot, h], ysem.at[slot, h])
 
     def store(j):
         slot = lax.rem(j, 2)
@@ -98,25 +104,31 @@
 
     @pl.when(chosen)
     def _():
-        load_x(GB if kind == "down" else NM if kind == "attention" else NF).start()
-        load_y(0).start()
-        load_x(0).wait()
+        which = GB if kind == "down" else NM if kind == "attention" else NF
+
+        def halves(act):
+            act(0)
+            pl.when(parts == 2)(lambda: act(1))
+
+        halves(lambda h: load_x(which, h, 0).start())
+        halves(lambda h: load_y(0, h).start())
+        if kind == "attention":
+            halves(lambda h: load_x(AT, h, 1).start())
+        halves(lambda h: load_x(which, h, 0).wait())
 
         def step(j, carry):
             slot = lax.rem(j, 2)
-            pl.when(j < 3)(lambda: load_y(j + 1).start())
-            load_y(j).wait()
+            pl.when(j < 3)(lambda: halves(lambda h: load_y(j + 1, h).start()))
+            halves(lambda h: load_y(j, h).wait())
+            source = 0
             if kind == "attention":
-
-                @pl.when(j == 3)
-                def _():
-                    load_x(AT).start()
-                    load_x(AT).wait()
+                pl.when(j == 3)(lambda: halves(lambda h: load_x(AT, h, 1).wait()))
+                source = lax.div(j, 3)
 
             def product(h):
                 if kind == "down":
-                    return dot_tn(yv[slot, h], xv[h])
-                return dot_tn(xv[h], yv[slot, h])
+                    return dot_tn(yv[slot, h], xv[source, h])
+                return dot_tn(xv[source, h], yv[slot, h])
 
             pl.when(j >= 2)(lambda: store(j - 2).wait())
 
@@ -473,7 +485,7 @@
 def chain_kernel(
     xs, cs, w, rows2, cos, sin, mod,
     st, kv, lse, y, yf, act, dma, dmf, out_x, fin,
-    wa, w1, w2, xv, nv, kvv, vv, inbox, qv, atv, bra, n1, brf, gbv, dov, dqv, xo, ov, fv, lv, cv, sv,
+    wa, w1, w2, xv, nv, kvv, vv, inbox, qv, atv, bra, n1, brf, gbv, dov, dqv, xo, ov, fv, n2, gb2, lv, cv, sv,
     dkt, dvt, rcvv, dpv, duv, actv, accv, dmv, zerov, moda, modf,
     w_send, w_recv, wf_send, wf_recv, x_send, x_recv, row_recv, fwd_send, fwd_recv, c_send, c_recv,
     push_sem, dkv_send, dkv_recv, mod_send, mod_recv, far_send, far_recv, fin_send, out_recv, ld, osem,
@@ -697,8 +709,8 @@
             ]
             return rows, [(zerov, dmf.at[mb + 1 - 2 * lax.rem(mb, 2)])], role >= 2
         rows = [
-            (gbv, y.at[half, spot, pl.ds(3 * D, D)]), (dpv, y.at[half, spot, pl.ds(0, 3 * D)]),
-            (n1, st.at[NM, half, spot]), (dmv, dma.at[mb]),
+            (gb2, y.at[half, spot, pl.ds(3 * D, D)]), (dpv, y.at[half, spot, pl.ds(0, 3 * D)]),
+            (n2, st.at[NM, half, spot]), (dmv, dma.at[mb]),
         ]
         return rows, [(zerov, dma.at[mb + 1 - 2 * lax.rem(mb, 2)])], role >= 2
 
@@ -942,8 +954,15 @@
             def part(p, carry):
                 at = pl.ds(pl.multiple_of(p * D, D), D)
                 u = dot(n1[rows, :], w1[:, at])
-                t, _ = gelu_parts(u)
-                accv[rows, :] += dot((0.5 * u * (1.0 + t)).astype(bf16), w2[at, :])
+                t, u2 = gelu_parts(u)
+                half = 0.5 * (1.0 + t)
+                actv[rows, at] = (u * half).astype(bf16)
+
+                @pl.when(role != 1)
+                def _():
+                    duv[rows, at] = gelu_slope(u, t, u2, half).astype(bf16)
+
+                accv[rows, :] += dot(actv[rows, at], w2[at, :])
                 return carry
 
             lax.fori_loop(0, 4, part, 0)
@@ -1014,13 +1033,15 @@
 
             def part(p, carry):
                 cols = pl.ds(pl.multiple_of(p * D, D), D)
-                u = dot(n1[rows, :], w1[:, cols])
-                t, u2 = gelu_parts(u)
-                half = 0.5 * (1.0 + t)
-                actv[rows, cols] = (u * half).astype(bf16)
-                slope = half + 0.5 * u * (1.0 - t * t) * (
-                    0.7978845608028654 * (1.0 + 3 * 0.044715 * u2)
-                )
+                @pl.when(role == 1)
+                def _():
+                    u = dot(n1[rows, :], w1[:, cols])
+                    t, u2 = gelu_parts(u)
+                    half = 0.5 * (1.0 + t)
+                    actv[rows, cols] = (u * half).astype(bf16)
+                    duv[rows, cols] = gelu_slope(u, t, u2, half).astype(bf16)
+
+                slope = duv[rows, cols].astype(f32)
                 du = (dot_nt(gbv[rows, :], w2[cols, :]) * slope).astype(bf16)
                 duv[rows, cols] = du
                 accv[rows, :] += dot_nt(du, w1[:, cols])
@@ -1069,7 +1090,7 @@
             )
             for j in range(2)
         ]
-        free(step)
+        pl.when(role == 0)(lambda: free(step))
 
         @pl.when(role == 0)
         def _():
@@ -1081,7 +1102,6 @@
             for copy in own_loads:
                 copy.start()
 
-        dmv[...] = jnp.zeros((8, D), f32)
 
         def grad_block(j, carry):
             rows = block_rows(j)
@@ -1093,7 +1113,7 @@
 
             live = live_column(c, length, j)
             gb = jnp.where(live, inbox[slot, rows, :].astype(f32) * gat, 0.0).astype(bf16)
-            gbv[rows, :] = gb
+            gb2[rows, :] = gb
             dov[rows, :] = dot_nt(gb, wa[:, 3 * D : 4 * D]).astype(bf16)
             return carry
 
@@ -1149,6 +1169,8 @@
             )
 
         lax.fori_loop(0, HEADS // 2, pair, 0)
+        pl.when(role != 0)(lambda: free(step))
+        dmv[...] = jnp.zeros((8, D), f32)
 
         def settled(hp, carry):
             for part in range(2):
@@ -1182,7 +1204,7 @@
                     )
             acc = dot_nt(dpv[rows, :], wa[:, 0 : 3 * D])
             n, rstd = norm_parts(xo[rows, :].astype(f32))
-            n1[rows, :] = (n * scl + off).astype(bf16)
+            n2[rows, :] = (n * scl + off).astype(bf16)
             g = inbox[slot, rows, :].astype(f32)
             live = live_column(c, length, j)
             gl = jnp.where(live, g, 0.0)
@@ -1257,7 +1279,7 @@
         out_specs=[ANY] * len(outs),
         scratch_shapes=[
             vm((D, FF)), vm((D, FF)), vm((FF, D)), FV, FV, FV, FV, vm((8, HALF, D)),
-            HV, HV, HV, HV, HV, HV, HV, HV, HV, HV, HV, vm((HALF, 128), f32), table, table,
+            HV, HV, HV, HV, HV, HV, HV, HV, HV, HV, HV, HV, HV, vm((HALF, 128), f32), table, table,
             vm((D, SEQ_LEN)), vm((D, SEQ_LEN)), vm((2, 2, D, HALF)), vm((HALF, 3 * D)),
             vm((HALF, FF)), vm((HALF, FF)), vm((HALF, D), f32), vm((8, D), f32), vm((8, D), f32),
             vm((MB, 8, D), f32), vm((MB, 8, D), f32),
@@ -1317,8 +1339,8 @@
             in_specs=[ANY, ANY],
             out_specs=ANY,
             scratch_shapes=[
-                vm((2, SEQ_LEN, D)), vm((2, 2, SEQ_LEN, D)), vm((D, D), f32), vm((2, D, D)),
-                pairs, pairs, pairs,
+                vm((2, 2, SEQ_LEN, D)), vm((2, 2, SEQ_LEN, D)), vm((D, D), f32), vm((2, D, D)),
+                pltpu.SemaphoreType.DMA((2, 2)), pltpu.SemaphoreType.DMA((2, 2)), pairs,
             ],
             out_shape=shape((FF, D) if kind == "down" else (D, FF)),
             compiler_params=pltpu.CompilerParams(vmem_limit_bytes=VLIM),

time: 425 us -> 422 us (level)
  no operation moved by 1% of the time
where the time goes in v6:
time: 422 us
  Pallas kernels  405 us (96%)
  other arithmetic  6.99 us (2%)
  matrix products  4.45 us (1%)
    pallas_call x1, Pallas kernels, chain(): pl.pallas_call(chain_kernel, out_shape=outs, in_specs=[ANY] * 7, out_spec...  311 us
    pallas_call x1, Pallas kernels, sums(): pl.pallas_call(functools.partial(sums_kernel, chips), out_shape=[jax.Shap...  79.2 us
    pallas_call x3, Pallas kernels, weight_grad(): pl.pallas_call(functools.partial(weight_grad_kernel, kind, roles), in_spe...  15.3 us

profile of v6, /device:TPU:0, one launch (start us, length us, event | category | flops | bytes accessed | tf_op | source)
XLA Modules:
  0.0 421.9 jit_solution(14183197441252659943)
XLA Ops:
  0.6 0.0 copy-start.3
  0.7 0.7 convert_element_type.33
  1.3 0.1 multiply_cosine_fusion
  1.4 0.7 convert_reduce_fusion
  2.2 2.6 fusion.2
  4.9 0.0 copy-done.3
  4.9 0.1 broadcast_in_dim.52
  5.0 0.1 pad.3.clone
  5.0 0.7 maximum_maximum_fusion.mod
  5.7 311.0 %layers.1 = (bf16[7,2,1024,768]{3,2,1,0:T(8,128)(2,1)}, bf16[2,4,1024,768]{3,2,1,0:T(8,128)(2,1)}, f32[4,512,128]{2,1,0:T(8,128)}, bf16[2,1024,3072]{2,1,0:T(8,1...) custom-call(bf16[2,1024,768]{2,1,0:T(8,128)(2,1)} %xs.1, ...), custom_call_target="tpu_custom_call" | custom-call | flops 299999985664 | bytes 1048576 | tf_op jit(solution)/shard_map/layers/pallas_call | solution.py:1275
  316.7 0.1 down_gradient.1
  316.9 0.1 up_gradient.1
  317.0 15.0 %attention_gradient.1 = bf16[768,3072]{1,0:T(8,128)(2,1)} custom-call(bf16[7,2,1024,768]{3,2,1,0:T(8,128)(2,1)} %get-tuple-element.19.st, bf16[2,1024,3072]{2,1,0:T(8,128)(2,1)} %get-tuple-element.20.y), custom_call_target="tpu_custom_call" | custom-call | flops 12000000000 | bytes 1048576 | tf_op jit(solution)/shard_map/attention_gradient/pallas_call | solution.py:1337
  332.0 79.2 %gradient_sums.1 = (f32[96,3072]{1,0:T(8,128)}, f32[192,768]{1,0:T(8,128)}, f32[2,8,2,8,768]{4,3,2,1,0:T(8,128)}, bf16[2,256,768]{2,1,0:T(8,128)(2,1)}) custom-call(bf16[8,96,3072]{2,1,0:T(8,128)(2,1)} %bitcast.22, bf16[8,96,3072]{2,1,0:T(8,128)(2,1)} %bitcast.21, bf16[16,192,768]{2,1,0:T(8,128)(2,1)} %bitcast.20, f32[4,8,768]{2,1,0:T(8,128)} %get-tuple-element.23.dma, ...), custom_call_target="tpu_custom_call" | custom-call | tf_op jit(solution)/shard_map/gradient_sums/pallas_call | solution.py:458
  411.2 0.0 copy-start.4
  411.2 0.0 copy-start.1
  411.3 0.0 copy-start.2
  411.3 1.4 broadcast_select_fusion
  412.7 0.1 slice.9
  412.7 0.1 copy.22
  412.8 0.3 slice_reduce_fusion
  413.1 0.0 copy-start
  413.1 0.1 reshape_squeeze.3
  413.2 1.9 convolution_bitcast_fusion
  415.1 0.0 copy-done.4
  415.1 0.1 broadcast_compare_fusion
  415.2 0.0 copy-done.2
  415.2 3.2 select_convert_fusion
  418.3 0.1 dynamic-slice_reduce_fusion
  418.4 0.6 broadcast_in_dim.57
  419.0 1.0 copy.27
  420.0 1.9 copy.28
  (11 shorter events, 0.1 us)
Async XLA Ops:
  0.6 4.2 %copy-start.3 = (s32[2]{0:T(128)S(1)}, s32[2]{0:T(128)}, u32[]{:S(2)}) copy-start(s32[2]{0:T(128)} %param.12) | copy-start | bytes 28
  411.2 3.8 copy-start.4
  411.2 3.9 copy-start.1
  411.3 3.9 copy-start.2
  413.1 5.9 %copy-start = (f32[96,3072]{1,0:T(8,128)S(1)}, f32[96,3072]{1,0:T(8,128)}, u32[]{:S(2)}) copy-start(f32[96,3072]{1,0:T(8,128)} %get-tuple-element.28) | copy-start | bytes 3538948
